TPU v7x, 128 devices: a whole 4x4x4 slice. The times are simulated.
128 devices in a mesh: lon: 16 (over z_hi, x, core), lat: 8 (over y, z_lo).
Axes of the slice: x: 4, y: 4, z: 4 (z_hi: 2, z_lo: 2; z = z_hi * 2 + z_lo), core: 2. Of those that a mesh axis runs over, the one named last changes fastest.
Arguments:
- tokens: bfloat16 [3, 16, 512, 1024], P(None, 'lat', 'lon'), may hold values from -48 to 48
- targets: bfloat16 [3, 16, 512, 1024], P(None, 'lat', 'lon'), may hold values from -48 to 48
- w_query: bfloat16 [1024, 1024], replicated, may hold values from -0.1875 to 0.1875
- w_key: bfloat16 [1024, 1024], replicated, may hold values from -0.1875 to 0.1875
- w_value: bfloat16 [1024, 1024], replicated, may hold values from -0.1875 to 0.1875
- w_out: bfloat16 [1024, 1024], replicated, may hold values from -0.1875 to 0.1875
- window_reach: int32 [8], replicated, may hold values from 0 to 2, as said below
- loss_table: int32 [4], replicated, may hold values from 1 to 8
Outputs:
- mixed: bfloat16 [3, 16, 512, 1024], P(None, 'lat', 'lon')
- grad_tokens: float32 [3, 16, 512, 1024], P(None, 'lat', 'lon')
- loss: float32 [], replicated
Inputs may be any that keep to these rules, and one draw needn't show every extreme that they name: `window_reach`: every head's reach is at most 2, and one head reaches exactly 2.
All inputs are finite; a program needn't handle non-finite values.
Results may differ from a plain program's by a relative error of at most 0.013.
The roundings to bfloat16 on the way count: a program that leaves them out, or rounds other values in their place, can miss the bound.
Values may be sent and summed in bfloat16 or wider, within the bound.
No kernel may reach another device: no remote copies, remote signals or barrier semaphores. Data moves between devices by JAX's collectives and lax.ppermute only.
A program may use at most 128 MiB of HBM per device.

v0:
```python
import math

import jax
import jax.numpy as jnp
from jax import lax
from jax.sharding import PartitionSpec as P

HEADS = 16


NEG = -1e30


def padded(cells, sides, width):
    for axis, dim in sides:
        count = lax.axis_size(axis)
        ends = count - 1
        head = lax.slice_in_dim(cells, 0, width, axis=dim)
        tail = lax.slice_in_dim(cells, cells.shape[dim] - width, cells.shape[dim], axis=dim)
        cells = jnp.concatenate(
            [
                lax.ppermute(tail, axis, [(i, (i + 1) % count) for i in range(ends)]),
                cells,
                lax.ppermute(head, axis, [((i + 1) % count, i) for i in range(ends)]),
            ],
            axis=dim,
        )
    return cells


def passed_along(value, axis, steps):
    count = lax.axis_size(axis)
    first, last = (max(0, -steps), min(count, count - steps))
    return lax.ppermute(value, axis, [(source, source + steps) for source in range(first, last)])


def masked_softmax(scores, allowed, axes):
    scores = jnp.where(allowed, scores, NEG)
    top = jnp.max(scores, axis=axes, keepdims=True)
    expo = jnp.exp(scores - top)
    return expo / jnp.sum(expo, axis=axes, keepdims=True)


def band_probs(queries, keys, scale):
    scores = (
        jnp.einsum("lrqhd,lrkhd->lrhqk", queries, keys, preferred_element_type=jnp.float32) * scale
    )
    top = jnp.max(scores, axis=-1, keepdims=True)
    expo = jnp.exp(scores - top)
    total = jnp.sum(expo, axis=-1, keepdims=True)
    return (expo / total, top, total)


def window_allowed(window_reach, rows, reach, base, grid_rows):
    query_row = jnp.arange(rows)[:, None]
    key_row = jnp.arange(rows + 2 * reach)[None, :]
    offset = key_row - query_row - reach
    global_row = base + key_row - reach
    inside = (global_row >= 0) & (global_row < grid_rows)
    near = jnp.abs(offset)[None, :, :] <= window_reach[:, None, None]
    allowed = near & inside[None, :, :]
    return jnp.transpose(allowed, (1, 0, 2))[None, :, None, :, None, :]


def per_device(tokens, targets, w_query, w_key, w_value, w_out, window_reach, loss_table):
    levels, rows, cols, width = tokens.shape
    head_dim = width // HEADS
    half = HEADS // 2
    scale = 1.0 / math.sqrt(head_dim)
    count = levels * rows * cols
    flat = tokens.reshape(count, width)
    shape_heads = (levels, rows, cols, HEADS, head_dim)
    queries = (
        jnp.dot(flat, w_query, preferred_element_type=jnp.float32)
        .astype(jnp.bfloat16)
        .reshape(shape_heads)
    )
    keys = (
        jnp.dot(flat, w_key, preferred_element_type=jnp.float32)
        .astype(jnp.bfloat16)
        .reshape(shape_heads)
    )
    values = (
        jnp.dot(flat, w_value, preferred_element_type=jnp.float32)
        .astype(jnp.bfloat16)
        .reshape(shape_heads)
    )
    band_q = queries[..., :half, :]
    band_k = keys[..., :half, :]
    band_v = values[..., :half, :]
    window_q = queries[..., half:, :]
    band_keys, band_values = (
        lax.all_gather(band_k, "lon", axis=2, tiled=True),
        lax.all_gather(band_v, "lon", axis=2, tiled=True),
    )
    probs, row_top, row_total = band_probs(band_q, band_keys, scale)
    band_weights = probs.astype(jnp.bfloat16)
    band_out = jnp.einsum(
        "lrhqk,lrkhd->lrqhd", band_weights, band_values, preferred_element_type=jnp.float32
    ).astype(jnp.bfloat16)
    stacked = jnp.stack([keys[..., half:, :], values[..., half:, :]]).reshape(
        2, levels, rows, cols, half * head_dim
    )
    extended = padded(stacked, (("lat", 2),), rows)
    extended = extended.reshape(2, levels, rows + 2 * rows, cols, half, head_dim)
    ext_keys = extended[0]
    ext_values = extended[1]
    base = lax.axis_index("lat") * rows
    grid_rows = rows * lax.axis_size("lat")
    allowed = window_allowed(window_reach, rows, rows, base, grid_rows)
    window_scores = (
        jnp.einsum("lrchd,mschd->lrchms", window_q, ext_keys, preferred_element_type=jnp.float32)
        * scale
    )
    window_probs = masked_softmax(window_scores, allowed, (-2, -1))
    window_weights = window_probs.astype(jnp.bfloat16)
    window_out = jnp.einsum(
        "lrchms,mschd->lrchd", window_weights, ext_values, preferred_element_type=jnp.float32
    ).astype(jnp.bfloat16)
    attended = jnp.concatenate([band_out, window_out], axis=3).reshape(count, width)
    mixed = (
        flat.astype(jnp.float32) + jnp.dot(attended, w_out, preferred_element_type=jnp.float32)
    ).astype(jnp.bfloat16)
    chan_weight = jnp.repeat(loss_table.astype(jnp.float32) / 4.0, width // loss_table.shape[0])
    diff = mixed.astype(jnp.float32) - targets.reshape(count, width).astype(jnp.float32)
    weighted = chan_weight[None, :] * diff
    total = lax.psum(jnp.sum(weighted * diff), ("lon", "lat"))
    loss = total / (count * width * lax.axis_size("lon") * lax.axis_size("lat"))
    d_mixed = weighted.astype(jnp.bfloat16)
    d_attended = (
        jnp.dot(d_mixed, jnp.transpose(w_out), preferred_element_type=jnp.float32)
        .astype(jnp.bfloat16)
        .reshape(shape_heads)
    )
    d_band = d_attended[..., :half, :]
    d_window = d_attended[..., half:, :]
    band_keys, band_values = (
        lax.all_gather(band_k, "lon", axis=2, tiled=True),
        lax.all_gather(band_v, "lon", axis=2, tiled=True),
    )
    probs, row_top, row_total = band_probs(band_q, band_keys, scale)
    band_weights = probs.astype(jnp.bfloat16)
    d_probs = jnp.einsum(
        "lrqhd,lrkhd->lrhqk", d_band, band_values, preferred_element_type=jnp.float32
    )
    delta = jnp.sum(d_band.astype(jnp.float32) * band_out.astype(jnp.float32), axis=-1)
    delta = jnp.transpose(delta, (0, 1, 3, 2))[..., None]
    band_grad_scores = (probs * (d_probs - delta) * scale).astype(jnp.bfloat16)
    band_dq = jnp.einsum(
        "lrhqk,lrkhd->lrqhd", band_grad_scores, band_keys, preferred_element_type=jnp.float32
    ).astype(jnp.bfloat16)
    key_terms = jnp.einsum(
        "lrhqk,lrqhd->lrkhd", band_grad_scores, band_q, preferred_element_type=jnp.float32
    )
    value_terms = jnp.einsum(
        "lrhqk,lrqhd->lrkhd", band_weights, d_band, preferred_element_type=jnp.float32
    )
    key_terms = lax.optimization_barrier(key_terms.astype(jnp.bfloat16)).astype(jnp.float32)
    value_terms = lax.optimization_barrier(value_terms.astype(jnp.bfloat16)).astype(jnp.float32)
    band_dk, band_dv = (
        lax.psum_scatter(
            key_terms.astype(jnp.bfloat16), "lon", scatter_dimension=2, tiled=True
        ).astype(jnp.float32),
        lax.psum_scatter(
            value_terms.astype(jnp.bfloat16), "lon", scatter_dimension=2, tiled=True
        ).astype(jnp.float32),
    )
    band_dk = band_dk.astype(jnp.bfloat16)
    band_dv = band_dv.astype(jnp.bfloat16)
    window_d_probs = jnp.einsum(
        "lrchd,mschd->lrchms", d_window, ext_values, preferred_element_type=jnp.float32
    )
    window_delta = jnp.sum(d_window.astype(jnp.float32) * window_out.astype(jnp.float32), axis=-1)[
        ..., None, None
    ]
    window_grad_scores = (window_probs * (window_d_probs - window_delta) * scale).astype(
        jnp.bfloat16
    )
    window_dq = jnp.einsum(
        "lrchms,mschd->lrchd", window_grad_scores, ext_keys, preferred_element_type=jnp.float32
    ).astype(jnp.bfloat16)
    ext_dk = jnp.einsum(
        "lrchms,lrchd->mschd", window_grad_scores, window_q, preferred_element_type=jnp.float32
    )
    ext_dv = jnp.einsum(
        "lrchms,lrchd->mschd", window_weights, d_window, preferred_element_type=jnp.float32
    )
    ext_grads = jnp.stack([ext_dk, ext_dv]).reshape(
        2, levels, rows + 2 * rows, cols, half * head_dim
    )
    lower_rim = ext_grads[:, :, :rows]
    upper_rim = ext_grads[:, :, rows + rows :]
    from_next = passed_along(lower_rim.astype(jnp.bfloat16), "lat", -1).astype(lower_rim.dtype)
    from_prev = passed_along(upper_rim.astype(jnp.bfloat16), "lat", 1).astype(upper_rim.dtype)
    owned = ext_grads[:, :, rows : rows + rows]
    owned = owned.at[:, :, rows - rows :].add(from_next)
    owned = owned.at[:, :, :rows].add(from_prev)
    owned = owned.reshape(2, levels, rows, cols, half, head_dim)
    window_dk = owned[0].astype(jnp.bfloat16)
    window_dv = owned[1].astype(jnp.bfloat16)
    d_queries = jnp.concatenate([band_dq, window_dq], axis=3).reshape(count, width)
    d_keys = jnp.concatenate([band_dk, window_dk], axis=3).reshape(count, width)
    d_values = jnp.concatenate([band_dv, window_dv], axis=3).reshape(count, width)
    grad = d_mixed.astype(jnp.float32)
    grad = grad + jnp.dot(d_queries, jnp.transpose(w_query), preferred_element_type=jnp.float32)
    grad = grad + jnp.dot(d_keys, jnp.transpose(w_key), preferred_element_type=jnp.float32)
    grad = grad + jnp.dot(d_values, jnp.transpose(w_value), preferred_element_type=jnp.float32)
    full_shape = (levels, rows, cols, width)
    return (mixed.reshape(full_shape), grad.reshape(full_shape), loss)


def solution(mesh):
    return jax.shard_map(
        per_device,
        mesh=mesh,
        in_specs=(
            P(None, "lat", "lon", None),
            P(None, "lat", "lon", None),
            P(),
            P(),
            P(),
            P(),
            P(),
            P(),
        ),
        out_specs=(P(None, "lat", "lon", None), P(None, "lat", "lon", None), P()),
        check_vma=False,
    )
```

profile of v0, /device:TPU:0, one launch (start us, length us, event | category | flops | bytes accessed | tf_op | source)
XLA Modules:
  0.0 395.4 jit_solution(13263259803044205717)
XLA Ops:
  7.2 3.2 convolution_convert_fusion.3
  13.9 2.9 convolution_convert_fusion.5
  25.7 5.8 %collective-permute-start = (bf16[2,3,2,32,512]{4,3,2,1,0:T(8,128)(2,1)}, bf16[2,3,2,32,512]{4,3,2,1,0:T(8,128)(2,1)}, u32[]{:S(2)}, u32[]{:S(2)}) collective-permute-start(bf16[2,3,2,32,512]{4,3,2,1,0:T(8,128)(2,1)} %constant_dynamic-update-slice_fusion), channel_id=1, source_target_pairs={{0,1},{1,2},{2,3},{3,4},{4,5},{5,6},{6,7},{8,9},{9,10},{10,11},{11... | collective-permute-start | bytes 1179656 | tf_op jit(solution)/shard_map/ppermute | solution.py:22
  31.6 2.2 convolution_convert_fusion.4
  35.3 1.9 fusion.51
  37.2 4.8 %collective-permute-done.1 = bf16[2,3,2,32,512]{4,3,2,1,0:T(8,128)(2,1)} collective-permute-done((bf16[2,3,2,32,512]{4,3,2,1,0:T(8,128)(2,1)}, bf16[2,3,2,32,512]{4,3,2,1,0:T(8,128)(2,1)}, u32[]{:S(2)}, u32[]{:S(2)}) %collective-permute-start.1) | collective-permute-done | bytes 393248 | tf_op jit(solution)/shard_map/ppermute | solution.py:24
  42.0 6.4 %collective-permute-done = bf16[2,3,2,32,512]{4,3,2,1,0:T(8,128)(2,1)} collective-permute-done((bf16[2,3,2,32,512]{4,3,2,1,0:T(8,128)(2,1)}, bf16[2,3,2,32,512]{4,3,2,1,0:T(8,128)(2,1)}, u32[]{:S(2)}, u32[]{:S(2)}) %collective-permute-start) | collective-permute-done | bytes 393248 | tf_op jit(solution)/shard_map/ppermute | solution.py:22
  50.6 2.5 squeeze.8
  54.8 6.7 %fusion.55 = (f32[3,2,32,8]{0,1,3,2:T(2,128)S(1)}, f32[3,2,32,8,3,6]{5,0,1,4,3,2:T(4,128)S(1)}) fusion(bf16[3,2,32,8,64]{4,3,2,1,0:T(8,128)(2,1)} %get-tuple-element.52, bf16[3,6,32,8,64,1]{4,3,2,1,0,5:T(8,128)(2,1)} %bitcast.127, pred[2,8,6]{2,0,1:T(4,128)(4,1)S(1)} %compare_and_fusion), kind=kOutput, calls=%fused_computation.88 | convolution fusion | flops 3620352 | bytes 903264 | tf_op jit(solution)/shard_map/lrchd,mschd->lrchms/dot_general | solution.py:112
  61.5 2.2 fusion.8
  68.4 27.6 %all-gather.5.cloned.1.call-done = bf16[3,2,512,8,64]{4,2,3,1,0:T(8,128)(2,1)} async-done(((bf16[3,2,32,8,64]{4,2,3,1,0:T(8,128)(2,1)}), bf16[3,2,512,8,64]{4,2,3,1,0:T(8,128)(2,1)}) %all-gather.5.cloned.1.call-update) | async-done | bytes 3145744 | tf_op jit(solution)/shard_map/all_gather | solution.py:93
  96.0 5.0 %fusion.40 = f32[3,2,8,32,512]{4,3,2,1,0:T(8,128)S(1)} fusion(bf16[3,2,512,8,64]{4,2,3,1,0:T(8,128)(2,1)} %all-gather.5.cloned.1.call-done, bf16[3,2,32,8,64]{4,3,2,1,0:T(8,128)(2,1)S(1)} %get-tuple-element.51), kind=kOutput, calls=%fused_computation.66 | convolution fusion | flops 100663296 | bytes 6488064 | tf_op jit(solution)/shard_map/lrqhd,lrkhd->lrhqk/dot_general | solution.py:46
  101.0 2.3 fusion.56
  103.3 63.0 %all-gather.3.cloned.1.call-done = bf16[3,2,512,8,64]{4,2,3,1,0:T(8,128)(2,1)} async-done(((bf16[3,2,32,8,64]{4,2,3,1,0:T(8,128)(2,1)}), bf16[3,2,512,8,64]{4,2,3,1,0:T(8,128)(2,1)}) %all-gather.3.cloned.1.call-update) | async-done | bytes 3145744 | tf_op jit(solution)/shard_map/all_gather | solution.py:94
  166.3 4.8 %fusion.30 = bf16[3,2,32,8,64]{4,2,3,1,0:T(8,128)(2,1)S(1)} fusion(bf16[3,2,512,8,64]{4,2,3,1,0:T(8,128)(2,1)} %all-gather.3.cloned.1.call-done, f32[3,2,8,32,512]{4,3,2,1,0:T(8,128)} %get-tuple-element.62, f32[3,2,8,32]{3,2,1,0:T(8,128)S(1)} %get-tuple-element.61), kind=kOutput, calls=%fused_computation.41 | convolution fusion | flops 102334464 | bytes 6494208 | tf_op jit(solution)/shard_map/lrhqk,lrkhd->lrqhd/dot_general | solution.py:98
  173.1 2.4 reshape.190
  175.5 3.1 fusion.32
  181.7 5.9 %multiply_convert_fusion = bf16[3,2,8,32,512]{4,3,2,1,0:T(8,128)(2,1)S(1)} fusion(bf16[3,2,512,8,64]{4,2,3,1,0:T(8,128)(2,1)} %all-gather.3.cloned.1.call-done, f32[3,2,8,32]{3,2,1,0:T(8,128)S(1)} %bitcast.133, f32[3,2,8,32,512]{4,3,2,1,0:T(8,128)} %get-tuple-element.62, f32[3,2,8,32]{3,2,1,0:T(8,128)S(1)} %get-tuple-element.61, ...), kind=kOutput, calls=%fused_computation.8 | convolution fusion | flops 104595456 | bytes 8073216 | tf_op jit(solution)/shard_map/lrqhd,lrkhd->lrhqk/dot_general | solution.py:143
  189.7 7.0 %copy.63 = bf16[3,2,512,8,64]{4,3,1,0,2:T(8,128)(2,1)} copy(bf16[3,2,512,8,64]{2,4,3,1,0:T(8,128)(2,1)S(1)} %convert_bitcast_fusion.1) | data formatting | bytes 6291456 | tf_op jit(solution)/shard_map/optimization_barrier | solution.py:158
  196.8 70.7 %psum.7 = f32[]{:T(128)} all-reduce(f32[]{:T(128)} %get-tuple-element.47), channel_id=1, replica_groups=mesh['lon'=16,'lat'=8] {'lon','lat'}, use_global_device_ids=true, to_apply=%region_9.10 | all-reduce | flops 1 | bytes 8 | tf_op jit(solution)/shard_map/psum | solution.py:127
  268.3 3.8 convert_bitcast_fusion
  272.1 8.6 %copy.69 = bf16[3,2,512,8,64]{4,3,1,0,2:T(8,128)(2,1)} copy(bf16[3,2,512,8,64]{2,4,3,1,0:T(8,128)(2,1)} %convert_bitcast_fusion) | data formatting | bytes 6291456 | tf_op jit(solution)/shard_map/optimization_barrier | solution.py:159
  280.8 2.4 multiply_reduce_fusion.1
  284.2 6.9 %fusion.3 = bf16[3,2,32,8,3,6]{5,0,1,4,3,2:T(4,128)(2,1)S(1)} fusion(bf16[3,6,32,8,64,1]{4,3,2,1,0,5:T(8,128)(2,1)} %bitcast.129, f32[3,2,32,8]{0,1,3,2:T(2,128)S(1)} %copy.58, bf16[3,2,32,8,64,1]{4,2,3,1,0,5:T(8,128)(2,1)} %bitcast.123, f32[3,2,32,8]{0,1,3,2:T(2,128)} %copy-done.26, f32[3,2,32,8,3,6]{5,0,1,4,3,2:T(4,128)S(1)} %copy-done.3, ...), kind=kOutput, calls=%fused_computation.4 | convolution fusion | flops 3704832 | bytes 970752 | tf_op jit(solution)/shard_map/lrchd,mschd->lrchms/dot_general | solution.py:170
  296.6 3.5 convolution_bitcast_fusion
  300.2 1.8 copy.66
  302.0 2.9 stack.22
  309.7 5.7 %collective-permute-start.3 = (bf16[2,3,2,32,512]{4,3,2,1,0:T(8,128)(2,1)}, bf16[2,3,2,32,512]{4,3,2,1,0:T(8,128)(2,1)}, u32[]{:S(2)}, u32[]{:S(2)}) collective-permute-start(bf16[2,3,2,32,512]{4,3,2,1,0:T(8,128)(2,1)} %get-tuple-element.44), channel_id=1, source_target_pairs={{0,1},{1,2},{2,3},{3,4},{4,5},{5,6},{6,7},{8,9},{9,10},{10,11},{11... | collective-permute-start | bytes 1179656 | tf_op jit(solution)/shard_map/ppermute | solution.py:34
  318.9 1.8 convolution_add_fusion.2
  321.2 12.6 %collective-permute-done.3 = bf16[2,3,2,32,512]{4,3,2,1,0:T(8,128)(2,1)} collective-permute-done((bf16[2,3,2,32,512]{4,3,2,1,0:T(8,128)(2,1)}, bf16[2,3,2,32,512]{4,3,2,1,0:T(8,128)(2,1)}, u32[]{:S(2)}, u32[]{:S(2)}) %collective-permute-start.3) | collective-permute-done | bytes 393248 | tf_op jit(solution)/shard_map/ppermute | solution.py:34
  337.7 42.8 %reduce-scatter.5.cloned.1.call-done = bf16[3,2,32,8,64]{4,3,1,0,2:T(8,128)(2,1)} async-done(((bf16[3,2,512,8,64]{4,3,1,0,2:T(8,128)(2,1)}), bf16[3,2,32,8,64]{4,3,1,0,2:T(8,128)(2,1)}) %reduce-scatter.5.cloned.1.call-update) | async-done | bytes 196624 | tf_op jit(solution)/shard_map/reduce_scatter | solution.py:164
  383.1 2.6 convolution_add_fusion.1
  (133 shorter events, 53.0 us)
Async XLA Ops:
  7.2 168.3 %copy-start = (bf16[1024,1024]{1,0:T(8,128)(2,1)S(1)}, bf16[1024,1024]{1,0:T(8,128)(2,1)}, u32[]{:S(2)}) copy-start(bf16[1024,1024]{1,0:T(8,128)(2,1)} %param.21) | copy-start | bytes 6291460
  7.2 88.8 %all-gather.5.cloned.1.call-start = ((), (), s32[]{:S(2)}) async-start(), calls=%async_computation.3 | async-start | bytes 6684672 | tf_op jit(solution)/shard_map/all_gather | solution.py:93
  10.4 3.5 copy-start.10
  13.9 152.4 %all-gather.3.cloned.1.call-start = ((), (), s32[]{:S(2)}) async-start(), calls=%async_computation.2 | async-start | bytes 6684672 | tf_op jit(solution)/shard_map/all_gather | solution.py:94
  18.5 13.0 %copy-start.29 = (s32[4]{0:T(128)S(1)}, s32[4]{0:T(128)}, u32[]{:S(2)}) copy-start(s32[4]{0:T(128)} %param.23) | copy-start | bytes 52
  20.3 315.5 %reduce-scatter.3.cloned.1.call-start = ((), (), s32[]{:S(2)}) async-start(), calls=%async_computation.4 | async-start | bytes 6684672 | tf_op jit(solution)/shard_map/reduce_scatter | solution.py:161
  24.3 10.9 %copy-start.28 = (s32[8]{0:T(128)S(1)}, s32[8]{0:T(128)}, u32[]{:S(2)}) copy-start(s32[8]{0:T(128)} %param.22) | copy-start | bytes 100
  24.3 17.7 %collective-permute-start.1 = (bf16[2,3,2,32,512]{4,3,2,1,0:T(8,128)(2,1)}, bf16[2,3,2,32,512]{4,3,2,1,0:T(8,128)(2,1)}, u32[]{:S(2)}, u32[]{:S(2)}) collective-permute-start(bf16[2,3,2,32,512]{4,3,2,1,0:T(8,128)(2,1)} %constant_dynamic-update-slice_fusion), channel_id=1, source_target_pairs={{1,0},{2,1},{3,2},{4,3},{5,4},{6,5},{7,6},{9,8},{10,9},{11,10},{12... | collective-permute-start | bytes 1179656 | tf_op jit(solution)/shard_map/ppermute | solution.py:24
  25.7 22.7 %collective-permute-start = (bf16[2,3,2,32,512]{4,3,2,1,0:T(8,128)(2,1)}, bf16[2,3,2,32,512]{4,3,2,1,0:T(8,128)(2,1)}, u32[]{:S(2)}, u32[]{:S(2)}) collective-permute-start(bf16[2,3,2,32,512]{4,3,2,1,0:T(8,128)(2,1)} %constant_dynamic-update-slice_fusion), channel_id=1, source_target_pairs={{0,1},{1,2},{2,3},{3,4},{4,5},{5,6},{6,7},{8,9},{9,10},{10,11},{11... | collective-permute-start | bytes 1179656 | tf_op jit(solution)/shard_map/ppermute | solution.py:22
  61.5 4.0 %copy-start.2 = (f32[3,2,32,8,3,6]{5,0,1,4,3,2:T(4,128)}, f32[3,2,32,8,3,6]{5,0,1,4,3,2:T(4,128)S(1)}, u32[]{:S(2)}) copy-start(f32[3,2,32,8,3,6]{5,0,1,4,3,2:T(4,128)S(1)} %get-tuple-element.60) | copy-start | bytes 331780
  61.5 4.0 %copy-start.25 = (f32[3,2,32,8]{0,1,3,2:T(2,128)}, f32[3,2,32,8]{0,1,3,2:T(2,128)S(1)}, u32[]{:S(2)}) copy-start(f32[3,2,32,8]{0,1,3,2:T(2,128)S(1)} %get-tuple-element.59) | copy-start | bytes 18436
  67.3 33.7 %copy-start.16 = (bf16[32,8,64,3,2]{2,3,4,1,0:T(4,128)(2,1)}, bf16[32,8,64,3,2]{2,3,4,1,0:T(4,128)(2,1)S(1)}, u32[]{:S(2)}) copy-start(bf16[32,8,64,3,2]{2,3,4,1,0:T(4,128)(2,1)S(1)} %fusion.18) | copy-start | bytes 589828
  103.3 78.0 %copy-start.27 = (f32[3,2,8,32]{3,2,1,0:T(8,128)}, f32[3,2,8,32]{3,2,1,0:T(8,128)S(1)}, u32[]{:S(2)}) copy-start(f32[3,2,8,32]{3,2,1,0:T(8,128)S(1)} %get-tuple-element.61) | copy-start | bytes 18436
  166.3 4.9 %copy-start.18 = (bf16[32,8,64,3,2]{2,0,1,4,3:T(8,128)(2,1)S(1)}, bf16[32,8,64,3,2]{2,0,1,4,3:T(8,128)(2,1)}, u32[]{:S(2)}) copy-start(bf16[32,8,64,3,2]{2,0,1,4,3:T(8,128)(2,1)} %copy.156) | copy-start | bytes 589828
  178.6 2.3 copy-start.11
  196.7 70.8 %copy-start.13 = (bf16[3,2,32,8,64]{4,3,2,1,0:T(8,128)(2,1)S(1)}, bf16[3,2,32,8,64]{4,3,2,1,0:T(8,128)(2,1)}, u32[]{:S(2)}) copy-start(bf16[3,2,32,8,64]{4,3,2,1,0:T(8,128)(2,1)} %get-tuple-element.50) | copy-start | bytes 589828
  196.7 71.6 %copy-start.14 = (f32[3,2,8,32,512]{4,3,2,1,0:T(8,128)S(1)}, f32[3,2,8,32,512]{4,3,2,1,0:T(8,128)}, u32[]{:S(2)}) copy-start(f32[3,2,8,32,512]{4,3,2,1,0:T(8,128)} %get-tuple-element.62) | copy-start | bytes 9437188
  196.8 183.7 %reduce-scatter.5.cloned.1.call-start = ((), (), s32[]{:S(2)}) async-start(), calls=%async_computation.5 | async-start | bytes 6684672 | tf_op jit(solution)/shard_map/reduce_scatter | solution.py:164
  280.8 3.4 copy-start.3
  284.2 6.9 %copy-start.23 = (bf16[3,6,32,8,64]{4,3,2,1,0:T(8,128)(2,1)S(1)}, bf16[3,6,32,8,64]{4,3,2,1,0:T(8,128)(2,1)}, u32[]{:S(2)}) copy-start(bf16[3,6,32,8,64]{4,3,2,1,0:T(8,128)(2,1)} %squeeze.9) | copy-start | bytes 1769476
  291.1 2.9 copy-start.15
  300.2 15.3 %slice-start = ((s8[6291456]{0:T(1024)(128)(4,1)}), s8[2097152]{0:T(1024)(128)(4,1)S(1)}, s32[]{:S(2)}) async-start(s8[6291456]{0:T(1024)(128)(4,1)} %bitcast.117), calls=%async_computation.6 | async-start | bytes 4194304
  304.9 10.6 %slice-start.1 = ((s8[6291456]{0:T(1024)(128)(4,1)}), s8[4194304]{0:T(1024)(128)(4,1)S(1)}, s32[]{:S(2)}) async-start(s8[6291456]{0:T(1024)(128)(4,1)} %bitcast.117), calls=%async_computation.7 | async-start | bytes 8388608
  306.6 8.8 %copy-start.9 = (bf16[3,2,8,32,512]{4,3,2,1,0:T(8,128)(2,1)S(1)}, bf16[3,2,8,32,512]{4,3,2,1,0:T(8,128)(2,1)}, u32[]{:S(2)}) copy-start(bf16[3,2,8,32,512]{4,3,2,1,0:T(8,128)(2,1)} %copy-done.8) | copy-start | bytes 4718596
  308.3 12.9 %collective-permute-start.2 = (bf16[2,3,2,32,512]{4,3,2,1,0:T(8,128)(2,1)}, bf16[2,3,2,32,512]{4,3,2,1,0:T(8,128)(2,1)}, u32[]{:S(2)}, u32[]{:S(2)}) collective-permute-start(bf16[2,3,2,32,512]{4,3,2,1,0:T(8,128)(2,1)} %get-tuple-element.43), channel_id=1, source_target_pairs={{1,0},{2,1},{3,2},{4,3},{5,4},{6,5},{7,6},{9,8},{10,9},{11,10},{12... | collective-permute-start | bytes 1179656 | tf_op jit(solution)/shard_map/ppermute | solution.py:34
  309.7 6.8 %copy-start.17 = (bf16[32,8,64,3,2]{2,0,1,4,3:T(8,128)(2,1)S(1)}, bf16[32,8,64,3,2]{2,0,1,4,3:T(8,128)(2,1)}, u32[]{:S(2)}) copy-start(bf16[32,8,64,3,2]{2,0,1,4,3:T(8,128)(2,1)} %copy.157) | copy-start | bytes 589828
  309.7 24.0 %collective-permute-start.3 = (bf16[2,3,2,32,512]{4,3,2,1,0:T(8,128)(2,1)}, bf16[2,3,2,32,512]{4,3,2,1,0:T(8,128)(2,1)}, u32[]{:S(2)}, u32[]{:S(2)}) collective-permute-start(bf16[2,3,2,32,512]{4,3,2,1,0:T(8,128)(2,1)} %get-tuple-element.44), channel_id=1, source_target_pairs={{0,1},{1,2},{2,3},{3,4},{4,5},{5,6},{6,7},{8,9},{9,10},{10,11},{11... | collective-permute-start | bytes 1179656 | tf_op jit(solution)/shard_map/ppermute | solution.py:34
  316.5 2.4 copy-start.4
  316.5 2.4 copy-start.12
  383.1 2.6 copy-start.5
  383.1 2.6 copy-start.22
  383.1 4.3 %copy-start.1 = (bf16[1024,1024]{1,0:T(8,128)(2,1)S(1)}, bf16[1024,1024]{1,0:T(8,128)(2,1)}, u32[]{:S(2)}) copy-start(bf16[1024,1024]{1,0:T(8,128)(2,1)} %param.21) | copy-start | bytes 6291460
  (8 other events, 11.0 us)
Sparse Core Ops, SparseCore 0:
  14.0 81.9 all-gather.4
  98.3 67.9 all-gather.2
  196.9 88.2 reduce-scatter.2
  289.2 91.2 reduce-scatter.4
where the time goes:
time: 400 us; the launch traced here: 395 us
  waiting for transfers between devices  158 us (40%)
  blocking collectives  70.7 us (18%)
  matrix products  62.2 us (16%)
  local copies, waits for them, and re-layouts  59.1 us (15%)
  between operations  16.5 us (4%)
  other arithmetic  14.7 us (4%)
  starting transfers between devices  14.5 us (4%)
    psum x1, blocking collectives, per_device(): total = lax.psum(jnp.sum(weighted * diff), ('lon', 'lat'))  70.7 us
    all_gather x1, waiting for transfers between devices, per_device(): lax.all_gather(band_v, 'lon', axis=2, tiled=True)  63 us
    reduce_scatter x1, waiting for transfers between devices, per_device(): lax.psum_scatter(value_terms.astype(jnp.bfloat16), 'lon', scatter_dimensi...  42.8 us
    all_gather x1, waiting for transfers between devices, per_device(): lax.all_gather(band_k, 'lon', axis=2, tiled=True)  27.6 us
    ppermute x2, waiting for transfers between devices, passed_along(): lax.ppermute(value, axis, [(source, source + steps) for source in range(f...  13 us
    optimization_barrier x1, local copies, waits for them, and re-layouts, per_device(): lax.optimization_barrier(value_terms.astype(jnp.bfloat16))  8.63 us
  transfers between devices with their start and end apart: 8, of which 7 were waited for; matrix products, arithmetic and copies ran while one was open for 23% of the time, Pallas kernels for 0%

commit v1 on v0

v1 whole, which is shorter than its diff:
```python
import functools
import math

import jax
import jax.numpy as jnp
from jax import lax
from jax.experimental import pallas as pl
from jax.experimental.pallas import tpu as pltpu
from jax.sharding import PartitionSpec as P

HEADS = 16
HALF = 8
HD = 64
LEVELS = 3
N_LON = 16
N_LAT = 8
TOK = 192
WIDTH = 1024
BAND = 512
SCALE = 0.125
LOG2E = math.log2(math.e)
NEG = -1e30
BF = jnp.bfloat16
F32 = jnp.float32
VMEM = 40 * 1024 * 1024


def call(kernel, out_shape, flops, nbytes, **kw):
    return pl.pallas_call(
        kernel,
        out_shape=out_shape,
        compiler_params=pltpu.CompilerParams(vmem_limit_bytes=VMEM),
        cost_estimate=pl.CostEstimate(flops=flops, bytes_accessed=nbytes, transcendentals=0),
        **kw,
    )


def dot(a, b):
    return jnp.dot(a, b, preferred_element_type=F32)


def dot_nt(a, b):
    return lax.dot_general(a, b, (((1,), (1,)), ((), ())), preferred_element_type=F32)


def tr(x):
    return jnp.transpose(x)


def band_proj_kernel(tok_ref, wq_ref, wk_ref, wv_ref, out_ref):
    tok = tok_ref[...]
    q = dot(tok, wq_ref[...]).astype(BF)
    k = dot(tok, wk_ref[...]).astype(BF)
    v = dot(tok, wv_ref[...]).astype(BF)
    for hh in range(4):
        lanes = slice(64 * hh, 64 * hh + 64)
        qk = jnp.concatenate([q[:, lanes], k[:, lanes]], axis=1)
        vh = v[:, lanes]
        for l in range(LEVELS):
            for r in range(2):
                base = l * 64 + r * 32
                out_ref[2 * hh + r, 48 * l : 48 * l + 32, :] = qk[base : base + 32]
                out_ref[2 * hh + r, 48 * l + 32 : 48 * l + 48, :] = jnp.concatenate(
                    [vh[base : base + 16], vh[base + 16 : base + 32]], axis=1
                )


def band_proj(tok, wq, wk, wv):
    wspec = pl.BlockSpec((WIDTH, 256), lambda g: (0, g))
    return call(
        band_proj_kernel,
        jax.ShapeDtypeStruct((N_LON, 144, 128), BF),
        6 * TOK * WIDTH * BAND,
        4 * 1024 * 1024,
        grid=(2,),
        in_specs=[pl.BlockSpec((TOK, WIDTH), lambda g: (0, 0)), wspec, wspec, wspec],
        out_specs=pl.BlockSpec((8, 144, 128), lambda g: (g, 0, 0)),
    )(tok, wq, wk, wv)


def unpack_qkv(x):
    qk = x[:, 0:32, :].reshape(512, 128)
    v = x[:, 32:48, :]
    v = jnp.concatenate([v[:, :, 0:64], v[:, :, 64:128]], axis=1).reshape(512, 64)
    return qk[:, 0:64], qk[:, 64:128], v


def unpack_one(x):
    return jnp.concatenate([x[:, :, 0:64], x[:, :, 64:128]], axis=1).reshape(512, 64)


def pack_one(x):
    x = x.reshape(N_LON, 32, 64)
    return jnp.concatenate([x[:, 0:16, :], x[:, 16:32, :]], axis=2)


def band_fwd_kernel(x_ref, o_ref, stat_ref):
    q, k, v = unpack_qkv(x_ref[...])
    s = dot_nt(k, q) * (SCALE * LOG2E)
    top = jnp.max(s, axis=0, keepdims=True)
    e = jnp.exp2(s - top)
    rtot = 1.0 / jnp.sum(e, axis=0, keepdims=True)
    w = (e * rtot).astype(BF)
    o = tr(dot(tr(v), w)).astype(BF)
    o_ref[...] = pack_one(o)
    stat_ref[0, 0:1, :] = top
    stat_ref[0, 1:2, :] = rtot


def band_fwd(x):
    return call(
        band_fwd_kernel,
        (
            jax.ShapeDtypeStruct((N_LON, 48, 128), BF),
            jax.ShapeDtypeStruct((LEVELS, 2, 512), F32),
        ),
        12 * 512 * 512 * 64,
        1024 * 1024,
        grid=(LEVELS,),
        in_specs=[pl.BlockSpec((N_LON, 48, 128), lambda l: (0, l, 0))],
        out_specs=(
            pl.BlockSpec((N_LON, 16, 128), lambda l: (0, l, 0)),
            pl.BlockSpec((1, 2, 512), lambda l: (l, 0, 0)),
        ),
    )(x)


def band_bwd_kernel(x_ref, o_ref, stat_ref, do_ref, loss_ref, out_ref, tot_ref):
    q, k, v = unpack_qkv(x_ref[...])
    o = unpack_one(o_ref[...])
    do = unpack_one(do_ref[...])
    s = dot_nt(k, q) * (SCALE * LOG2E)
    p = jnp.exp2(s - stat_ref[0, 0:1, :]) * stat_ref[0, 1:2, :]
    w = p.astype(BF)
    dp = dot_nt(v, do)
    delta = jnp.sum(tr(do.astype(F32) * o.astype(F32)), axis=0, keepdims=True)
    ds = (p * (dp - delta) * SCALE).astype(BF)
    dv = dot(w, do).astype(BF)
    dk = dot(ds, q).astype(BF)
    dq = tr(dot(tr(k), ds)).astype(BF)
    out_ref[:, 0:32, :] = jnp.concatenate([dq, dk], axis=1).reshape(N_LON, 32, 128)
    out_ref[:, 32:48, :] = pack_one(dv)
    tot_ref[...] = jnp.broadcast_to(jnp.sum(loss_ref[:, 0, 0:128].astype(F32)), (8, 128))


def band_bwd(x, o, stat, do):
    return call(
        band_bwd_kernel,
        (
            jax.ShapeDtypeStruct((N_LON, 144, 128), BF),
            jax.ShapeDtypeStruct((8, 128), F32),
        ),
        30 * 512 * 512 * 64,
        2 * 1024 * 1024,
        grid=(LEVELS,),
        in_specs=[
            pl.BlockSpec((N_LON, 48, 128), lambda l: (0, l, 0)),
            pl.BlockSpec((N_LON, 16, 128), lambda l: (0, l, 0)),
            pl.BlockSpec((1, 2, 512), lambda l: (l, 0, 0)),
            pl.BlockSpec((N_LON, 16, 128), lambda l: (0, l, 0)),
            pl.BlockSpec((N_LON, 16, 128), lambda l: (0, 3, 0)),
        ],
        out_specs=(
            pl.BlockSpec((N_LON, 48, 128), lambda l: (0, l, 0)),
            pl.BlockSpec((8, 128), lambda l: (0, 0)),
        ),
    )(x, o, stat, do, do)


def to_halves(x):
    return jnp.concatenate(
        [x[32 * i + 16 * s : 32 * i + 16 * s + 16] for s in range(2) for i in range(6)], axis=0
    )


def from_halves(x):
    return jnp.concatenate(
        [x[96 * s + 16 * i : 96 * s + 16 * i + 16] for i in range(6) for s in range(2)], axis=0
    )


def win_proj_kernel(tok_ref, wq_ref, wk_ref, wv_ref, q_ref, k_ref, v_ref):
    tok = to_halves(tok_ref[...])
    q_ref[...] = dot(tok, wq_ref[...]).astype(BF)
    k_ref[...] = dot(tok, wk_ref[...]).astype(BF)
    v_ref[...] = dot(tok, wv_ref[...]).astype(BF)


def win_proj(tok, wq, wk, wv):
    wspec = pl.BlockSpec((WIDTH, 256), lambda g: (0, 2 + g))
    ospec = pl.BlockSpec((TOK, 256), lambda g: (0, g))
    shape = jax.ShapeDtypeStruct((TOK, BAND), BF)
    return call(
        win_proj_kernel,
        (shape, shape, shape),
        6 * TOK * WIDTH * BAND,
        4 * 1024 * 1024,
        grid=(2,),
        in_specs=[pl.BlockSpec((TOK, WIDTH), lambda g: (0, 0)), wspec, wspec, wspec],
        out_specs=(ospec, ospec, ospec),
    )(tok, wq, wk, wv)


def halo_proj_kernel(prev_ref, next_ref, wk_ref, wv_ref, k_ref, v_ref):
    tok = jnp.concatenate([to_halves(prev_ref[...]), to_halves(next_ref[...])], axis=0)
    k_ref[...] = dot(tok, wk_ref[...]).astype(BF)
    v_ref[...] = dot(tok, wv_ref[...]).astype(BF)


def halo_proj(prev, nxt, wk, wv):
    tspec = pl.BlockSpec((TOK, WIDTH), lambda g: (0, 0))
    wspec = pl.BlockSpec((WIDTH, 256), lambda g: (0, 2 + g))
    ospec = pl.BlockSpec((2 * TOK, 256), lambda g: (0, g))
    shape = jax.ShapeDtypeStruct((2 * TOK, BAND), BF)
    return call(
        halo_proj_kernel,
        (shape, shape),
        8 * TOK * WIDTH * BAND,
        3 * 1024 * 1024,
        grid=(2,),
        in_specs=[tspec, tspec, wspec, wspec],
        out_specs=(ospec, ospec),
    )(prev, nxt, wk, wv)


def window_distance(pos):
    key = lax.broadcasted_iota(jnp.int32, (288, 96), 0)
    query = lax.broadcasted_iota(jnp.int32, (288, 96), 1)
    block = (key >= 96).astype(jnp.int32) + (key >= 192).astype(jnp.int32)
    inner = key - 96 * block
    shift = jnp.where(block == 1, -2, jnp.where(block == 2, 2, 0))
    offset = shift + ((inner >> 4) & 1) - ((query >> 4) & 1)
    allowed = (inner & 15) == (query & 15)
    allowed = allowed & ((block != 1) | (pos > 0)) & ((block != 2) | (pos < N_LAT - 1))
    return jnp.where(allowed, jnp.abs(offset), 99)


def extended(own, halo, half):
    rows = slice(96 * half, 96 * half + 96)
    nrows = slice(TOK + 96 * half, TOK + 96 * half + 96)
    return jnp.concatenate([own[rows], halo[rows], halo[nrows]], axis=0)


def win_fwd_kernel(pos_ref, reach_ref, q_ref, k_ref, v_ref, hk_ref, hv_ref, o_ref, ot_ref, stat_ref):
    dist = window_distance(pos_ref[0])
    for half in range(2):
        rows = slice(96 * half, 96 * half + 96)
        q = q_ref[rows]
        k = extended(k_ref[...], hk_ref[...], half)
        vt = tr(extended(v_ref[...], hv_ref[...], half))
        outs = []
        for h in range(HALF):
            lanes = slice(64 * h, 64 * h + 64)
            s = dot_nt(k[:, lanes], q[:, lanes]) * (SCALE * LOG2E)
            s = jnp.where(dist <= reach_ref[h], s, NEG)
            top = jnp.max(s, axis=0, keepdims=True)
            e = jnp.exp2(s - top)
            rtot = 1.0 / jnp.sum(e, axis=0, keepdims=True)
            w = (e * rtot).astype(BF)
            ot = dot(vt[lanes], w)
            outs.append(ot)
            stat_ref[half, 2 * h : 2 * h + 1, :] = top
            stat_ref[half, 2 * h + 1 : 2 * h + 2, :] = rtot
        ot = jnp.concatenate(outs, axis=0)
        ot_ref[half] = ot.astype(BF)
        o_ref[rows] = tr(ot).astype(BF)


SMEM = pl.BlockSpec(memory_space=pltpu.SMEM)


def win_fwd(pos, reach, q, k, v, hk, hv):
    return call(
        win_fwd_kernel,
        (
            jax.ShapeDtypeStruct((TOK, BAND), BF),
            jax.ShapeDtypeStruct((2, BAND, 96), BF),
            jax.ShapeDtypeStruct((2, 16, 96), F32),
        ),
        64 * 288 * 128 * 64,
        2 * 1024 * 1024,
        in_specs=[SMEM, SMEM] + [pl.BlockSpec(memory_space=pltpu.VMEM)] * 5,
        out_specs=(pl.BlockSpec(memory_space=pltpu.VMEM),) * 3,
    )(pos, reach, q, k, v, hk, hv)


def win_bwd_kernel(
    pos_ref, reach_ref, q_ref, k_ref, v_ref, hk_ref, hv_ref, ot_ref, stat_ref, do_ref,
    dq_ref, own_ref, prev_ref, next_ref,
):
    dist = window_distance(pos_ref[0])
    do_all = to_halves(do_ref[...])
    for half in range(2):
        rows = slice(96 * half, 96 * half + 96)
        q = q_ref[rows]
        k = extended(k_ref[...], hk_ref[...], half)
        v = extended(v_ref[...], hv_ref[...], half)
        kt = tr(k)
        do = do_all[rows]
        dot_t = tr(do)
        ot = ot_ref[half]
        dqs = []
        for pair in range(HALF // 2):
            dks = []
            dvs = []
            for h in (2 * pair, 2 * pair + 1):
                lanes = slice(64 * h, 64 * h + 64)
                s = dot_nt(k[:, lanes], q[:, lanes]) * (SCALE * LOG2E)
                e = jnp.exp2(s - stat_ref[half, 2 * h : 2 * h + 1, :])
                p = jnp.where(dist <= reach_ref[h], e, 0.0) * stat_ref[half, 2 * h + 1 : 2 * h + 2, :]
                w = p.astype(BF)
                dp = dot_nt(v[:, lanes], do[:, lanes])
                delta = jnp.sum(
                    dot_t[lanes].astype(F32) * ot[lanes].astype(F32), axis=0, keepdims=True
                )
                ds = (p * (dp - delta) * SCALE).astype(BF)
                dvs.append(dot(w, do[:, lanes]))
                dks.append(dot(ds, q[:, lanes]))
                dqs.append(dot(kt[lanes], ds))
            out = slice(128 * pair, 128 * pair + 128)
            for n, parts in enumerate((dks, dvs)):
                both = jnp.concatenate(parts, axis=1)
                own_ref[n, rows, out] = both[0:96]
                prev_ref[n, rows, out] = both[96:192].astype(BF)
                next_ref[n, rows, out] = both[192:288].astype(BF)
        dq_ref[rows] = tr(jnp.concatenate(dqs, axis=0)).astype(BF)


def win_bwd(pos, reach, q, k, v, hk, hv, ot, stat, do):
    rim = jax.ShapeDtypeStruct((2, TOK, BAND), BF)
    return call(
        win_bwd_kernel,
        (
            jax.ShapeDtypeStruct((TOK, BAND), BF),
            jax.ShapeDtypeStruct((2, TOK, BAND), F32),
            rim,
            rim,
        ),
        160 * 288 * 128 * 64,
        4 * 1024 * 1024,
        in_specs=[SMEM, SMEM] + [pl.BlockSpec(memory_space=pltpu.VMEM)] * 8,
        out_specs=(pl.BlockSpec(memory_space=pltpu.VMEM),) * 4,
    )(pos, reach, q, k, v, hk, hv, ot, stat, do)


def mid_kernel(table_ref, tok_ref, tgt_ref, o_ref, win_ref, wo_ref, mixed_ref, dm_ref, send_ref, dwin_ref):
    cols = []
    for pair in range(HALF // 2):
        parts = []
        for l in range(LEVELS):
            for r in range(2):
                a = o_ref[4 * pair + r, 16 * l : 16 * l + 16, :]
                b = o_ref[4 * pair + 2 + r, 16 * l : 16 * l + 16, :]
                parts.append(jnp.concatenate([a[:, 0:64], b[:, 0:64]], axis=1))
                parts.append(jnp.concatenate([a[:, 64:128], b[:, 64:128]], axis=1))
        cols.append(jnp.concatenate(parts, axis=0))
    att = jnp.concatenate(cols + [from_halves(win_ref[...])], axis=1)
    mixed = (tok_ref[...].astype(F32) + dot(att, wo_ref[...])).astype(BF)
    mixed_ref[...] = mixed
    lane = lax.broadcasted_iota(jnp.int32, (1, WIDTH), 1)
    weight = jnp.zeros((1, WIDTH), F32)
    for g in range(4):
        here = (lane >= 256 * g) & (lane < 256 * g + 256)
        weight = jnp.where(here, table_ref[g].astype(F32) * 0.25, weight)
    diff = mixed.astype(F32) - tgt_ref[...].astype(F32)
    weighted = weight * diff
    total = jnp.sum(weighted * diff)
    dm = weighted.astype(BF)
    dm_ref[...] = dm
    d_att = dot_nt(dm, wo_ref[...]).astype(BF)
    dwin_ref[...] = d_att[:, BAND:]
    for h in range(HALF):
        dh = d_att[:, 64 * h : 64 * h + 64]
        for l in range(LEVELS):
            for r in range(2):
                base = 64 * l + 32 * r
                send_ref[2 * h + r, 16 * l : 16 * l + 16, :] = jnp.concatenate(
                    [dh[base : base + 16], dh[base + 16 : base + 32]], axis=1
                )
    total = jnp.broadcast_to(total, (16, 128))
    high = total.astype(BF).astype(F32)
    mid = (total - high).astype(BF).astype(F32)
    low = total - high - mid
    at = lax.broadcasted_iota(jnp.int32, (16, 128), 1)
    parts = jnp.where(at == 0, high, jnp.where(at == 1, mid, jnp.where(at == 2, low, 0.0)))
    parts = parts.astype(BF)
    for j in range(N_LON):
        send_ref[j, 48:64, :] = parts


def mid(table, tok, tgt, o, win, wo):
    return call(
        mid_kernel,
        (
            jax.ShapeDtypeStruct((TOK, WIDTH), BF),
            jax.ShapeDtypeStruct((TOK, WIDTH), BF),
            jax.ShapeDtypeStruct((N_LON, 64, 128), BF),
            jax.ShapeDtypeStruct((TOK, BAND), BF),
        ),
        4 * TOK * WIDTH * WIDTH,
        4 * 1024 * 1024,
        in_specs=[SMEM] + [pl.BlockSpec(memory_space=pltpu.VMEM)] * 5,
        out_specs=(pl.BlockSpec(memory_space=pltpu.VMEM),) * 4,
    )(table, tok, tgt, o, win, wo)


def win_grad_kernel(dm_ref, dq_ref, own_ref, fp_ref, fn_ref, wq_ref, wk_ref, wv_ref, out_ref):
    dq = dq_ref[...]
    dk = (own_ref[0] + fp_ref[0].astype(F32) + fn_ref[0].astype(F32)).astype(BF)
    dv = (own_ref[1] + fp_ref[1].astype(F32) + fn_ref[1].astype(F32)).astype(BF)
    g = dot_nt(dq, wq_ref[...]) + dot_nt(dk, wk_ref[...]) + dot_nt(dv, wv_ref[...])
    out_ref[...] = dm_ref[...].astype(F32) + from_halves(g)


def win_grad(dm, dq, own, fp, fn, wq, wk, wv):
    wspec = pl.BlockSpec((256, BAND), lambda g: (g, 1))
    whole3 = pl.BlockSpec((2, TOK, BAND), lambda g: (0, 0, 0))
    nspec = pl.BlockSpec((TOK, 256), lambda g: (0, g))
    return call(
        win_grad_kernel,
        jax.ShapeDtypeStruct((TOK, WIDTH), F32),
        6 * TOK * WIDTH * BAND,
        5 * 1024 * 1024,
        grid=(4,),
        in_specs=[nspec, pl.BlockSpec((TOK, BAND), lambda g: (0, 0)), whole3, whole3, whole3]
        + [wspec] * 3,
        out_specs=nspec,
    )(dm, dq, own, fp, fn, wq, wk, wv)


def band_grad_kernel(x_ref, base_ref, wq_ref, wk_ref, wv_ref, out_ref, dq_s, dk_s, dv_s):
    @pl.when(pl.program_id(0) == 0)
    def _():
        for pair in range(HALF // 2):
            lanes = slice(128 * pair, 128 * pair + 128)
            for l in range(LEVELS):
                for r in range(2):
                    base = 64 * l + 32 * r
                    a = x_ref[4 * pair + r, 48 * l : 48 * l + 48, :]
                    b = x_ref[4 * pair + 2 + r, 48 * l : 48 * l + 48, :]
                    first = jnp.concatenate([a[:, 0:64], b[:, 0:64]], axis=1)
                    second = jnp.concatenate([a[:, 64:128], b[:, 64:128]], axis=1)
                    dq_s[base : base + 32, lanes] = first[0:32]
                    dk_s[base : base + 32, lanes] = second[0:32]
                    dv_s[base : base + 16, lanes] = first[32:48]
                    dv_s[base + 16 : base + 32, lanes] = second[32:48]

    g = dot_nt(dq_s[...], wq_ref[...]) + dot_nt(dk_s[...], wk_ref[...])
    out_ref[...] = base_ref[...] + g + dot_nt(dv_s[...], wv_ref[...])


def band_grad(x, base, wq, wk, wv):
    wspec = pl.BlockSpec((256, BAND), lambda g: (g, 0))
    nspec = pl.BlockSpec((TOK, 256), lambda g: (0, g))
    return call(
        band_grad_kernel,
        jax.ShapeDtypeStruct((TOK, WIDTH), F32),
        6 * TOK * WIDTH * BAND,
        5 * 1024 * 1024,
        grid=(4,),
        in_specs=[pl.BlockSpec((N_LON, 144, 128), lambda g: (0, 0, 0)), nspec] + [wspec] * 3,
        out_specs=nspec,
        scratch_shapes=[pltpu.VMEM((TOK, BAND), BF)] * 3,
    )(x, base, wq, wk, wv)


def swap(x):
    return lax.all_to_all(x, "lon", 0, 0, tiled=True)


UP = [(i, (i + 1) % N_LAT) for i in range(N_LAT)]
DOWN = [((i + 1) % N_LAT, i) for i in range(N_LAT)]


def per_device(tokens, targets, w_query, w_key, w_value, w_out, window_reach, loss_table):
    levels, rows, cols, width = tokens.shape
    count = levels * rows * cols
    tok = tokens.reshape(count, width)
    tgt = targets.reshape(count, width)
    pos = lax.axis_index("lat").astype(jnp.int32).reshape(1)

    with jax.named_scope("band_projection"):
        sent = band_proj(tok, w_query, w_key, w_value)
    with jax.named_scope("halo_tokens"):
        prev = lax.ppermute(tok, "lat", UP)
        nxt = lax.ppermute(tok, "lat", DOWN)
    with jax.named_scope("band_qkv_exchange"):
        x = swap(sent)
    with jax.named_scope("window_projection"):
        q, k, v = win_proj(tok, w_query, w_key, w_value)
        hk, hv = halo_proj(prev, nxt, w_key, w_value)
    with jax.named_scope("band_forward"):
        o, stat = band_fwd(x)
        o_back = swap(o)
    with jax.named_scope("window_forward"):
        win, ot, wstat = win_fwd(pos, window_reach, q, k, v, hk, hv)
    with jax.named_scope("middle"):
        mixed, dm, dsend, dwin = mid(loss_table, tok, tgt, o_back, win, w_out)
        do = swap(dsend)
    with jax.named_scope("window_backward"):
        dqw, own, rim_prev, rim_next = win_bwd(
            pos, window_reach, q, k, v, hk, hv, ot, wstat, dwin
        )
        from_prev = lax.ppermute(rim_next, "lat", UP)
        from_next = lax.ppermute(rim_prev, "lat", DOWN)
    with jax.named_scope("band_backward"):
        dsent, total = band_bwd(x, o, stat, do)
        dx = swap(dsent)
    with jax.named_scope("loss_sum"):
        for step in (1, 2, 4):
            total = total + lax.ppermute(total, "lat", [(i, i ^ step) for i in range(N_LAT)])
        loss = total[0, 0] / (count * width * N_LON * N_LAT)
    with jax.named_scope("token_gradient"):
        base = win_grad(dm, dqw, own, from_prev, from_next, w_query, w_key, w_value)
        grad = band_grad(dx, base, w_query, w_key, w_value)
    full = (levels, rows, cols, width)
    return (mixed.reshape(full), grad.reshape(full), loss)


def solution(mesh):
    spec = P(None, "lat", "lon", None)
    return jax.shard_map(
        per_device,
        mesh=mesh,
        in_specs=(spec, spec, P(), P(), P(), P(), P(), P()),
        out_specs=(spec, spec, P()),
        check_vma=False,
    )
```

time: 400 us -> 139 us (0.35)
  waiting for transfers between devices: 158 us -> 31.7 us
  matrix products: 62.2 us -> 0 us
  blocking collectives: 70.7 us -> 16.5 us
  local copies, waits for them, and re-layouts: 59.1 us -> 27 us
  Pallas kernels: 0 us -> 27 us
  starting transfers between devices: 14.5 us -> 33.1 us
  other arithmetic: 14.7 us -> 0.01 us
  between operations: 16.5 us -> 2.75 us
    all_gather x2 -> x0, waiting for transfers between devices: 90.6 us -> none  [the longest x1 63 us: per_device(): lax.all_gather(band_v, 'lon', axis=2, tiled=True)]
    psum x1 -> x0, blocking collectives: 70.7 us -> none  [per_device(): total = lax.psum(jnp.sum(weighted * diff), ('lon', 'lat'))]
    dot_general x20 -> x0, matrix products: 62.2 us -> none  [the longest x1 6.88 us: per_device(): jnp.einsum('lrchd,mschd->lrchms', d_window, ext_values, preferred_element...]
    reduce_scatter x2 -> x0, waiting for transfers between devices: 42.8 us -> none  [the longest x1 42.8 us: per_device(): lax.psum_scatter(value_terms.astype(jnp.bfloat16), 'lon', scatter_dimensi...]
    pallas_call x0 -> x10, Pallas kernels: none -> 27 us  [the longest x1 4.34 us: win_bwd(): call(win_bwd_kernel, (jax.ShapeDtypeStruct((TOK, BAND), BF), jax.ShapeDty...]
    all_to_all x0 -> x3, starting transfers between devices: none -> 21 us  [swap(): return lax.all_to_all(x, 'lon', 0, 0, tiled=True)]
    unnamed x71 -> x72, local copies, waits for them, and re-layouts: 6.18 us -> 26.5 us
    all_to_all x0 -> x1, blocking collectives: none -> 16.5 us  [swap(): return lax.all_to_all(x, 'lon', 0, 0, tiled=True)]
  transfers between devices with their start and end apart: 8 -> 10, of which waited for: 7 -> 4; matrix products, arithmetic and copies ran while one was open for 23% -> 0% of each run, Pallas kernels for 0% -> 12%
where the time goes in v1:
time: 139 us; the launch traced here: 138 us
  starting transfers between devices  33.1 us (24%)
  waiting for transfers between devices  31.7 us (23%)
  local copies, waits for them, and re-layouts  27 us (19%)
  Pallas kernels  27 us (19%)
  blocking collectives  16.5 us (12%)
  between operations  2.75 us (2%)
    unnamed x72, local copies, waits for them, and re-layouts  26.5 us
    all_to_all x3, starting transfers between devices, swap(): return lax.all_to_all(x, 'lon', 0, 0, tiled=True)  21 us
    ppermute x3, waiting for transfers between devices, per_device(): lax.ppermute(total, 'lat', [(i, i ^ step) for i in range(N_LAT)])  20.7 us
    all_to_all x1, blocking collectives, swap(): return lax.all_to_all(x, 'lon', 0, 0, tiled=True)  16.5 us
    all_to_all x3, waiting for transfers between devices, swap(): return lax.all_to_all(x, 'lon', 0, 0, tiled=True)  10.9 us
    ppermute x3, starting transfers between devices, per_device(): lax.ppermute(total, 'lat', [(i, i ^ step) for i in range(N_LAT)])  4.36 us
    pallas_call x1, Pallas kernels, win_bwd(): call(win_bwd_kernel, (jax.ShapeDtypeStruct((TOK, BAND), BF), jax.ShapeDty...  4.34 us
    ppermute x1, starting transfers between devices, per_device(): nxt = lax.ppermute(tok, 'lat', DOWN)  3.53 us
  transfers between devices with their start and end apart: 10, of which 4 were waited for; matrix products, arithmetic and copies ran while one was open for 0% of the time, Pallas kernels for 12%

profile of v1, /device:TPU:0, one launch (start us, length us, event | category | flops | bytes accessed | tf_op | source)
XLA Modules:
  0.0 138.0 jit_solution(3108111893761829859)
XLA Ops:
  0.6 1.6 %copy-done = bf16[1024,1024]{1,0:T(8,128)(2,1)S(1)} copy-done((bf16[1024,1024]{1,0:T(8,128)(2,1)S(1)}, bf16[1024,1024]{1,0:T(8,128)(2,1)}, u32[]{:S(2)}) %copy-start) | copy-done | bytes 2097176
  2.2 1.6 %copy-done.2 = bf16[1024,1024]{1,0:T(8,128)(2,1)S(1)} copy-done((bf16[1024,1024]{1,0:T(8,128)(2,1)S(1)}, bf16[1024,1024]{1,0:T(8,128)(2,1)}, u32[]{:S(2)}) %copy-start.2) | copy-done | bytes 2097176
  3.8 1.6 %copy-done.7 = bf16[1024,1024]{1,0:T(8,128)(2,1)S(1)} copy-done((bf16[1024,1024]{1,0:T(8,128)(2,1)S(1)}, bf16[1024,1024]{1,0:T(8,128)(2,1)}, u32[]{:S(2)}) %copy-start.7) | copy-done | bytes 2097176
  6.4 2.3 %band_projection.1 = bf16[16,144,128]{2,1,0:T(8,128)(2,1)} custom-call(bf16[192,1024]{1,0:T(8,128)(2,1)S(1)} %bitcast.6, bf16[1024,1024]{1,0:T(8,128)(2,1)S(1)} %copy-done.7, bf16[1024,1024]{1,0:T(8,128)(2,1)S(1)} %copy-done, bf16[1024,1024]{1,0:T(8,128)(2,1)S(1)} %copy-done.2), custom_call_target="tpu_custom_call" | custom-call | flops 603979776 | bytes 4194304 | tf_op jit(solution)/shard_map/band_projection/pallas_call | solution.py:70
  8.7 7.9 %all-to-all-start = ((bf16[16,144,128]{2,1,0:T(8,128)(2,1)}), bf16[16,144,128]{2,1,0:T(8,128)(2,1)S(1)}, u32[]{:S(2)}, u32[]{:S(2)}) async-start(bf16[16,144,128]{2,1,0:T(8,128)(2,1)} %band_projection.1), calls=%async_computation | async-start | bytes 1179648 | tf_op jit(solution)/shard_map/band_qkv_exchange/all_to_all | solution.py:468
  16.6 3.5 %collective-permute-start.1 = (bf16[192,1024]{1,0:T(8,128)(2,1)S(1)}, bf16[192,1024]{1,0:T(8,128)(2,1)S(1)}, u32[]{:S(2)}, u32[]{:S(2)}) collective-permute-start(bf16[192,1024]{1,0:T(8,128)(2,1)S(1)} %bitcast.7), channel_id=1, source_target_pairs={{1,0},{2,1},{3,2},{4,3},{5,4},{6,5},{7,6},{0,7},{9,8},{10,9},{11,1... | collective-permute-start | bytes 1179656 | tf_op jit(solution)/shard_map/halo_tokens/ppermute | solution.py:486
  20.2 10.9 %all-to-all-done.x_ref = bf16[16,144,128]{2,1,0:T(8,128)(2,1)S(1)} async-done(((bf16[16,144,128]{2,1,0:T(8,128)(2,1)}), bf16[16,144,128]{2,1,0:T(8,128)(2,1)S(1)}, u32[]{:S(2)}, u32[]{:S(2)}) %all-to-all-start) | async-done | bytes 589856 | tf_op jit(solution)/shard_map/band_qkv_exchange/all_to_all | solution.py:468
  31.1 2.9 %band_forward.1 = (bf16[16,48,128]{2,1,0:T(8,128)(2,1)S(1)}, f32[3,2,512]{2,1,0:T(2,128)S(1)}) custom-call(bf16[16,144,128]{2,1,0:T(8,128)(2,1)S(1)} %all-to-all-done.x_ref), custom_call_target="tpu_custom_call" | custom-call | flops 201326592 | bytes 1048576 | tf_op jit(solution)/shard_map/band_forward/pallas_call | solution.py:111
  34.7 9.5 %all-to-all-start.1 = ((bf16[16,48,128]{2,1,0:T(8,128)(2,1)}), bf16[16,48,128]{2,1,0:T(8,128)(2,1)S(1)}, u32[]{:S(2)}, u32[]{:S(2)}) async-start(bf16[16,48,128]{2,1,0:T(8,128)(2,1)} %copy-done.32), calls=%async_computation.1 | async-start | bytes 393216 | tf_op jit(solution)/shard_map/band_forward/all_to_all | solution.py:468
  44.2 1.6 %copy-done.3 = bf16[1024,1024]{1,0:T(8,128)(2,1)S(1)} copy-done((bf16[1024,1024]{1,0:T(8,128)(2,1)S(1)}, bf16[1024,1024]{1,0:T(8,128)(2,1)}, u32[]{:S(2)}) %copy-start.3) | copy-done | bytes 2097176
  45.8 1.6 %copy-done.8 = bf16[1024,1024]{1,0:T(8,128)(2,1)S(1)} copy-done((bf16[1024,1024]{1,0:T(8,128)(2,1)S(1)}, bf16[1024,1024]{1,0:T(8,128)(2,1)}, u32[]{:S(2)}) %copy-start.8) | copy-done | bytes 2097176
  47.3 1.5 %window_projection.2 = (bf16[192,512]{1,0:T(8,128)(2,1)S(1)}, bf16[192,512]{1,0:T(8,128)(2,1)S(1)}, bf16[192,512]{1,0:T(8,128)(2,1)S(1)}) custom-call(bf16[192,1024]{1,0:T(8,128)(2,1)S(1)} %bitcast.9, bf16[1024,1024]{1,0:T(8,128)(2,1)S(1)} %copy-done.8, bf16[1024,1024]{1,0:T(8,128)(2,1)S(1)} %copy-done.1, bf16[1024,1024]{1,0:T(8,128)(2,1)S(1)} %copy-done.3), custom_call_target="tpu_custom_call" | custom-call | flops 603979776 | bytes 4194304 | tf_op jit(solution)/shard_map/window_projection/pallas_call | solution.py:193
  48.9 2.4 %window_projection.3 = (bf16[384,512]{1,0:T(8,128)(2,1)S(1)}, bf16[384,512]{1,0:T(8,128)(2,1)S(1)}) custom-call(bf16[192,1024]{1,0:T(8,128)(2,1)} %collective-permute-done.prev_ref, bf16[192,1024]{1,0:T(8,128)(2,1)S(1)} %collective-permute-done.1.next_ref, bf16[1024,1024]{1,0:T(8,128)(2,1)S(1)} %copy-done.1, bf16[1024,1024]{1,0:T(8,128)(2,1)S(1)} %copy-done.4), custom_call_target="tpu_custom_call" | custom-call | flops 805306368 | bytes 3145728 | tf_op jit(solution)/shard_map/window_projection/pallas_call | solution.py:215
  51.4 3.0 %window_forward.1 = (bf16[192,512]{1,0:T(8,128)(2,1)S(1)}, bf16[2,512,96]{2,1,0:T(8,128)(2,1)S(1)}, f32[2,16,96]{2,1,0:T(8,128)S(1)}) custom-call(s32[1]{0:T(128)} %bitcast.2.pos_ref, s32[8]{0:T(128)S(1)} %copy-done.34, bf16[192,512]{1,0:T(8,128)(2,1)S(1)} %get-tuple-element.24.q_ref, bf16[192,512]{1,0:T(8,128)(2,1)S(1)} %get-tuple-element.25.k_ref, ...), custom_call_target="tpu_custom_call" | custom-call | flops 150994944 | bytes 2097152 | tf_op jit(solution)/shard_map/window_forward/pallas_call | solution.py:273
  55.8 1.6 %copy-done.13 = bf16[1024,1024]{1,0:T(8,128)(2,1)S(1)} copy-done((bf16[1024,1024]{1,0:T(8,128)(2,1)S(1)}, bf16[1024,1024]{1,0:T(8,128)(2,1)}, u32[]{:S(2)}) %copy-start.13) | copy-done | bytes 2097176
  58.4 2.6 %middle.1 = (bf16[192,1024]{1,0:T(8,128)(2,1)}, bf16[192,1024]{1,0:T(8,128)(2,1)S(1)}, bf16[16,64,128]{2,1,0:T(8,128)(2,1)S(1)}, bf16[192,512]{1,0:T(8,128)(2,1)S(1)}) custom-call(s32[4]{0:T(128)S(1)} %copy-done.35, bf16[192,1024]{1,0:T(8,128)(2,1)S(1)} %bitcast.10, bf16[192,1024]{1,0:T(8,128)(2,1)S(1)} %bitcast.11, ...), custom_call_target="tpu_custom_call" | custom-call | flops 805306368 | bytes 4194304 | tf_op jit(solution)/shard_map/middle/pallas_call | solution.py:392
  60.9 16.5 %all_to_all.20.do_ref.loss_ref = bf16[16,64,128]{2,1,0:T(8,128)(2,1)S(1)} all-to-all(bf16[16,64,128]{2,1,0:T(8,128)(2,1)S(1)} %get-tuple-element.32), channel_id=1, replica_groups=mesh['lon'=16,'lat'=8] {'lon'}, dimensions={0} | all-to-all | bytes 524288 | tf_op jit(solution)/shard_map/middle/all_to_all | solution.py:468
  78.4 3.0 %band_backward.1 = (bf16[16,144,128]{2,1,0:T(8,128)(2,1)S(1)}, f32[8,128]{1,0:T(8,128)S(1)}) custom-call(bf16[16,144,128]{2,1,0:T(8,128)(2,1)S(1)} %copy-done.24, bf16[16,48,128]{2,1,0:T(8,128)(2,1)S(1)} %copy-done.33, f32[3,2,512]{2,1,0:T(2,128)S(1)} %get-tuple-element.31.stat_ref, bf16[16,64,128]{2,1,0:T(8,128)(2,1)S(1)} %all_to_all.20.do_ref.loss_ref, ...), custom_call_target="tpu_custom_call" | custom-call | flops 503316480 | bytes 2097152 | tf_op jit(solution)/shard_map/band_backward/pallas_call | solution.py:147
  82.3 3.6 %all-to-all-start.3 = ((bf16[16,144,128]{2,1,0:T(8,128)(2,1)}), bf16[16,144,128]{2,1,0:T(8,128)(2,1)S(1)}, u32[]{:S(2)}, u32[]{:S(2)}) async-start(bf16[16,144,128]{2,1,0:T(8,128)(2,1)} %copy-done.22), calls=%async_computation.3 | async-start | bytes 1179648 | tf_op jit(solution)/shard_map/band_backward/all_to_all | solution.py:468
  90.5 4.3 %window_backward.1 = (bf16[192,512]{1,0:T(8,128)(2,1)S(1)}, f32[2,192,512]{2,1,0:T(8,128)S(1)}, bf16[2,192,512]{2,1,0:T(8,128)(2,1)S(1)}, bf16[2,192,512]{2,1,0:T(8,128)(2,1)S(1)}) custom-call(s32[1]{0:T(128)} %bitcast.2.pos_ref, s32[8]{0:T(128)S(1)} %copy-done.34, bf16[192,512]{1,0:T(8,128)(2,1)S(1)} %copy-done.17, bf16[192,512]{1,0:T(8,128)(2,1)S(1)} %copy-done.19, ...), custom_call_target="tpu_custom_call" | custom-call | flops 377487360 | bytes 4194304 | tf_op jit(solution)/shard_map/window_backward/pallas_call | solution.py:331
  95.6 3.5 %collective-permute-start.3 = (bf16[2,192,512]{2,1,0:T(8,128)(2,1)S(1)}, bf16[2,192,512]{2,1,0:T(8,128)(2,1)S(1)}, u32[]{:S(2)}, u32[]{:S(2)}) collective-permute-start(bf16[2,192,512]{2,1,0:T(8,128)(2,1)S(1)} %get-tuple-element.41), channel_id=1, source_target_pairs={{1,0},{2,1},{3,2},{4,3},{5,4},{6,5},{7,6},{0,7},{9,8},{10,9},{11,1... | collective-permute-start | bytes 1179656 | tf_op jit(solution)/shard_map/window_backward/ppermute | solution.py:505
  99.1 16.4 %collective-permute-done.4 = f32[8,128]{1,0:T(8,128)S(1)} collective-permute-done((f32[8,128]{1,0:T(8,128)S(1)}, f32[8,128]{1,0:T(8,128)S(1)}, u32[]{:S(2)}, u32[]{:S(2)}) %collective-permute-start.4) | collective-permute-done | bytes 4128 | tf_op jit(solution)/shard_map/loss_sum/ppermute | solution.py:511
  115.5 1.5 %collective-permute-start.5 = (f32[8,128]{1,0:T(8,128)S(1)}, f32[8,128]{1,0:T(8,128)S(1)}, u32[]{:S(2)}, u32[]{:S(2)}) collective-permute-start(f32[8,128]{1,0:T(8,128)S(1)} %add.9), channel_id=1, source_target_pairs={{0,2},{1,3},{2,0},{3,1},{4,6},{5,7},{6,4},{7,5},{8,10},{9,11},{10,... | collective-permute-start | bytes 12296 | tf_op jit(solution)/shard_map/loss_sum/ppermute | solution.py:511
  116.9 2.1 %collective-permute-done.5 = f32[8,128]{1,0:T(8,128)S(1)} collective-permute-done((f32[8,128]{1,0:T(8,128)S(1)}, f32[8,128]{1,0:T(8,128)S(1)}, u32[]{:S(2)}, u32[]{:S(2)}) %collective-permute-start.5) | collective-permute-done | bytes 4128 | tf_op jit(solution)/shard_map/loss_sum/ppermute | solution.py:511
  119.1 2.9 %collective-permute-start.6 = (f32[8,128]{1,0:T(8,128)S(1)}, f32[8,128]{1,0:T(8,128)S(1)}, u32[]{:S(2)}, u32[]{:S(2)}) collective-permute-start(f32[8,128]{1,0:T(8,128)S(1)} %add.10), channel_id=1, source_target_pairs={{0,4},{1,5},{2,6},{3,7},{4,0},{5,1},{6,2},{7,3},{8,12},{9,13},{10,... | collective-permute-start | bytes 12296 | tf_op jit(solution)/shard_map/loss_sum/ppermute | solution.py:511
  122.0 2.2 %collective-permute-done.6 = f32[8,128]{1,0:T(8,128)S(1)} collective-permute-done((f32[8,128]{1,0:T(8,128)S(1)}, f32[8,128]{1,0:T(8,128)S(1)}, u32[]{:S(2)}, u32[]{:S(2)}) %collective-permute-start.6) | collective-permute-done | bytes 4128 | tf_op jit(solution)/shard_map/loss_sum/ppermute | solution.py:511
  125.4 1.6 %copy-done.5 = bf16[1024,1024]{1,0:T(8,128)(2,1)S(1)} copy-done((bf16[1024,1024]{1,0:T(8,128)(2,1)S(1)}, bf16[1024,1024]{1,0:T(8,128)(2,1)}, u32[]{:S(2)}) %copy-start.5) | copy-done | bytes 2097176
  127.0 1.6 %copy-done.9 = bf16[1024,1024]{1,0:T(8,128)(2,1)S(1)} copy-done((bf16[1024,1024]{1,0:T(8,128)(2,1)S(1)}, bf16[1024,1024]{1,0:T(8,128)(2,1)}, u32[]{:S(2)}) %copy-start.9) | copy-done | bytes 2097176
  128.6 2.1 %token_gradient.2.base_ref = f32[192,1024]{1,0:T(8,128)S(1)} custom-call(bf16[192,1024]{1,0:T(8,128)(2,1)S(1)} %copy-done.26, bf16[192,512]{1,0:T(8,128)(2,1)S(1)} %get-tuple-element.38.dq_ref, f32[2,192,512]{2,1,0:T(8,128)S(1)} %get-tuple-element.39.own_ref, bf16[2,192,512]{2,1,0:T(8,128)(2,1)S(1)} %collective-permute-done.2.fp_ref, ...), custom_call_target="tpu_custom_call" | custom-call | flops 603979776 | bytes 5242880 | tf_op jit(solution)/shard_map/token_gradient/pallas_call | solution.py:419
  130.7 1.6 %copy-done.6 = bf16[1024,1024]{1,0:T(8,128)(2,1)S(1)} copy-done((bf16[1024,1024]{1,0:T(8,128)(2,1)S(1)}, bf16[1024,1024]{1,0:T(8,128)(2,1)}, u32[]{:S(2)}) %copy-start.6) | copy-done | bytes 2097176
  132.3 1.6 %copy-done.10 = bf16[1024,1024]{1,0:T(8,128)(2,1)S(1)} copy-done((bf16[1024,1024]{1,0:T(8,128)(2,1)S(1)}, bf16[1024,1024]{1,0:T(8,128)(2,1)}, u32[]{:S(2)}) %copy-start.10) | copy-done | bytes 2097176
  133.9 3.1 %token_gradient.3 = f32[192,1024]{1,0:T(8,128)} custom-call(bf16[16,144,128]{2,1,0:T(8,128)(2,1)S(1)} %all-to-all-done.3.x_ref, f32[192,1024]{1,0:T(8,128)S(1)} %token_gradient.2.base_ref, bf16[1024,1024]{1,0:T(8,128)(2,1)S(1)} %copy-done.10, bf16[1024,1024]{1,0:T(8,128)(2,1)S(1)} %copy-done.1, bf16[1024,1024]{1,0:T(8,128)(2,1)S(1)} %copy-done.6), custom_call_target="tpu_custom_call" | custom-call | flops 603979776 | bytes 5242880 | tf_op jit(solution)/shard_map/token_gradient/pallas_call | solution.py:455
  (75 shorter events, 11.9 us)
Async XLA Ops:
  0.6 1.6 %copy-start = (bf16[1024,1024]{1,0:T(8,128)(2,1)S(1)}, bf16[1024,1024]{1,0:T(8,128)(2,1)}, u32[]{:S(2)}) copy-start(bf16[1024,1024]{1,0:T(8,128)(2,1)} %wk_ref.9) | copy-start | bytes 6291460
  6.4 10.2 %copy-start.12 = (bf16[3,2,32,1024]{3,2,1,0:T(8,128)(2,1)S(1)}, bf16[3,2,32,1024]{3,2,1,0:T(8,128)(2,1)}, u32[]{:S(2)}) copy-start(bf16[3,2,32,1024]{3,2,1,0:T(8,128)(2,1)} %param.8) | copy-start | bytes 1179652
  8.7 35.5 %copy-start.1 = (bf16[1024,1024]{1,0:T(8,128)(2,1)S(1)}, bf16[1024,1024]{1,0:T(8,128)(2,1)}, u32[]{:S(2)}) copy-start(bf16[1024,1024]{1,0:T(8,128)(2,1)} %wk_ref.9) | copy-start | bytes 6291460
  8.7 22.4 %all-to-all-start = ((bf16[16,144,128]{2,1,0:T(8,128)(2,1)}), bf16[16,144,128]{2,1,0:T(8,128)(2,1)S(1)}, u32[]{:S(2)}, u32[]{:S(2)}) async-start(bf16[16,144,128]{2,1,0:T(8,128)(2,1)} %band_projection.1), calls=%async_computation | async-start | bytes 1179648 | tf_op jit(solution)/shard_map/band_qkv_exchange/all_to_all | solution.py:468
  16.6 32.2 %collective-permute-start.1 = (bf16[192,1024]{1,0:T(8,128)(2,1)S(1)}, bf16[192,1024]{1,0:T(8,128)(2,1)S(1)}, u32[]{:S(2)}, u32[]{:S(2)}) collective-permute-start(bf16[192,1024]{1,0:T(8,128)(2,1)S(1)} %bitcast.7), channel_id=1, source_target_pairs={{1,0},{2,1},{3,2},{4,3},{5,4},{6,5},{7,6},{0,7},{9,8},{10,9},{11,1... | collective-permute-start | bytes 1179656 | tf_op jit(solution)/shard_map/halo_tokens/ppermute | solution.py:486
  20.2 28.7 %collective-permute-start = (bf16[192,1024]{1,0:T(8,128)(2,1)S(1)}, bf16[192,1024]{1,0:T(8,128)(2,1)}, u32[]{:S(2)}, u32[]{:S(2)}) collective-permute-start(bf16[192,1024]{1,0:T(8,128)(2,1)S(1)} %bitcast.8), channel_id=1, source_target_pairs={{0,1},{1,2},{2,3},{3,4},{4,5},{5,6},{6,7},{7,0},{8,9},{9,10},{10,1... | collective-permute-start | bytes 1179656 | tf_op jit(solution)/shard_map/halo_tokens/ppermute | solution.py:485
  31.1 3.5 %copy-start.23 = (bf16[16,144,128]{2,1,0:T(8,128)(2,1)}, bf16[16,144,128]{2,1,0:T(8,128)(2,1)S(1)}, u32[]{:S(2)}) copy-start(bf16[16,144,128]{2,1,0:T(8,128)(2,1)S(1)} %all-to-all-done.x_ref) | copy-start | bytes 1769476
  34.7 21.1 %all-to-all-start.1 = ((bf16[16,48,128]{2,1,0:T(8,128)(2,1)}), bf16[16,48,128]{2,1,0:T(8,128)(2,1)S(1)}, u32[]{:S(2)}, u32[]{:S(2)}) async-start(bf16[16,48,128]{2,1,0:T(8,128)(2,1)} %copy-done.32), calls=%async_computation.1 | async-start | bytes 393216 | tf_op jit(solution)/shard_map/band_forward/all_to_all | solution.py:468
  44.2 1.6 %copy-start.3 = (bf16[1024,1024]{1,0:T(8,128)(2,1)S(1)}, bf16[1024,1024]{1,0:T(8,128)(2,1)}, u32[]{:S(2)}) copy-start(bf16[1024,1024]{1,0:T(8,128)(2,1)} %wv_ref.9) | copy-start | bytes 6291460
  45.8 1.6 %copy-start.8 = (bf16[1024,1024]{1,0:T(8,128)(2,1)S(1)}, bf16[1024,1024]{1,0:T(8,128)(2,1)}, u32[]{:S(2)}) copy-start(bf16[1024,1024]{1,0:T(8,128)(2,1)} %wq_ref.7) | copy-start | bytes 6291460
  47.3 1.6 %copy-start.4 = (bf16[1024,1024]{1,0:T(8,128)(2,1)S(1)}, bf16[1024,1024]{1,0:T(8,128)(2,1)}, u32[]{:S(2)}) copy-start(bf16[1024,1024]{1,0:T(8,128)(2,1)} %wv_ref.9) | copy-start | bytes 6291460
  48.8 2.5 %copy-start.16 = (bf16[192,512]{1,0:T(8,128)(2,1)}, bf16[192,512]{1,0:T(8,128)(2,1)S(1)}, u32[]{:S(2)}) copy-start(bf16[192,512]{1,0:T(8,128)(2,1)S(1)} %get-tuple-element.24.q_ref) | copy-start | bytes 589828
  48.8 2.5 %copy-start.18 = (bf16[192,512]{1,0:T(8,128)(2,1)}, bf16[192,512]{1,0:T(8,128)(2,1)S(1)}, u32[]{:S(2)}) copy-start(bf16[192,512]{1,0:T(8,128)(2,1)S(1)} %get-tuple-element.25.k_ref) | copy-start | bytes 589828
  48.8 2.5 %copy-start.20 = (bf16[192,512]{1,0:T(8,128)(2,1)}, bf16[192,512]{1,0:T(8,128)(2,1)S(1)}, u32[]{:S(2)}) copy-start(bf16[192,512]{1,0:T(8,128)(2,1)S(1)} %get-tuple-element.26.v_ref) | copy-start | bytes 589828
  48.8 2.5 %copy-start.34 = (s32[8]{0:T(128)S(1)}, s32[8]{0:T(128)}, u32[]{:S(2)}) copy-start(s32[8]{0:T(128)} %reach_ref.3) | copy-start | bytes 100
  48.9 6.9 %copy-start.35 = (s32[4]{0:T(128)S(1)}, s32[4]{0:T(128)}, u32[]{:S(2)}) copy-start(s32[4]{0:T(128)} %table_ref.1) | copy-start | bytes 52
  55.8 1.6 %copy-start.13 = (bf16[1024,1024]{1,0:T(8,128)(2,1)S(1)}, bf16[1024,1024]{1,0:T(8,128)(2,1)}, u32[]{:S(2)}) copy-start(bf16[1024,1024]{1,0:T(8,128)(2,1)} %wo_ref.1) | copy-start | bytes 6291460
  58.4 19.1 %copy-start.24 = (bf16[16,144,128]{2,1,0:T(8,128)(2,1)S(1)}, bf16[16,144,128]{2,1,0:T(8,128)(2,1)}, u32[]{:S(2)}) copy-start(bf16[16,144,128]{2,1,0:T(8,128)(2,1)} %copy-done.23) | copy-start | bytes 1769476
  60.9 20.5 %copy-start.25 = (bf16[192,1024]{1,0:T(8,128)(2,1)}, bf16[192,1024]{1,0:T(8,128)(2,1)S(1)}, u32[]{:S(2)}) copy-start(bf16[192,1024]{1,0:T(8,128)(2,1)S(1)} %get-tuple-element.34.dm_ref) | copy-start | bytes 1179652
  60.9 20.5 %copy-start.30 = (bf16[192,512]{1,0:T(8,128)(2,1)}, bf16[192,512]{1,0:T(8,128)(2,1)S(1)}, u32[]{:S(2)}) copy-start(bf16[192,512]{1,0:T(8,128)(2,1)S(1)} %get-tuple-element.37.do_ref) | copy-start | bytes 589828
  60.9 24.9 %copy-start.15 = (bf16[384,512]{1,0:T(8,128)(2,1)S(1)}, bf16[384,512]{1,0:T(8,128)(2,1)}, u32[]{:S(2)}) copy-start(bf16[384,512]{1,0:T(8,128)(2,1)} %copy-done.14) | copy-start | bytes 1179652
  82.3 48.4 %all-to-all-start.3 = ((bf16[16,144,128]{2,1,0:T(8,128)(2,1)}), bf16[16,144,128]{2,1,0:T(8,128)(2,1)S(1)}, u32[]{:S(2)}, u32[]{:S(2)}) async-start(bf16[16,144,128]{2,1,0:T(8,128)(2,1)} %copy-done.22), calls=%async_computation.3 | async-start | bytes 1179648 | tf_op jit(solution)/shard_map/band_backward/all_to_all | solution.py:468
  90.5 34.9 %copy-start.26 = (bf16[192,1024]{1,0:T(8,128)(2,1)S(1)}, bf16[192,1024]{1,0:T(8,128)(2,1)}, u32[]{:S(2)}) copy-start(bf16[192,1024]{1,0:T(8,128)(2,1)} %copy-done.25) | copy-start | bytes 1179652
  94.9 30.5 %collective-permute-start.2 = (bf16[2,192,512]{2,1,0:T(8,128)(2,1)S(1)}, bf16[2,192,512]{2,1,0:T(8,128)(2,1)S(1)}, u32[]{:S(2)}, u32[]{:S(2)}) collective-permute-start(bf16[2,192,512]{2,1,0:T(8,128)(2,1)S(1)} %get-tuple-element.40), channel_id=1, source_target_pairs={{0,1},{1,2},{2,3},{3,4},{4,5},{5,6},{6,7},{7,0},{8,9},{9,10},{10,1... | collective-permute-start | bytes 1179656 | tf_op jit(solution)/shard_map/window_backward/ppermute | solution.py:504
  95.6 29.8 %collective-permute-start.3 = (bf16[2,192,512]{2,1,0:T(8,128)(2,1)S(1)}, bf16[2,192,512]{2,1,0:T(8,128)(2,1)S(1)}, u32[]{:S(2)}, u32[]{:S(2)}) collective-permute-start(bf16[2,192,512]{2,1,0:T(8,128)(2,1)S(1)} %get-tuple-element.41), channel_id=1, source_target_pairs={{1,0},{2,1},{3,2},{4,3},{5,4},{6,5},{7,6},{0,7},{9,8},{10,9},{11,1... | collective-permute-start | bytes 1179656 | tf_op jit(solution)/shard_map/window_backward/ppermute | solution.py:505
  99.1 16.4 %collective-permute-start.4 = (f32[8,128]{1,0:T(8,128)S(1)}, f32[8,128]{1,0:T(8,128)S(1)}, u32[]{:S(2)}, u32[]{:S(2)}) collective-permute-start(f32[8,128]{1,0:T(8,128)S(1)} %get-tuple-element.42), channel_id=1, source_target_pairs={{0,1},{1,0},{2,3},{3,2},{4,5},{5,4},{6,7},{7,6},{8,9},{9,8},{10,11... | collective-permute-start | bytes 12296 | tf_op jit(solution)/shard_map/loss_sum/ppermute | solution.py:511
  115.5 3.6 %collective-permute-start.5 = (f32[8,128]{1,0:T(8,128)S(1)}, f32[8,128]{1,0:T(8,128)S(1)}, u32[]{:S(2)}, u32[]{:S(2)}) collective-permute-start(f32[8,128]{1,0:T(8,128)S(1)} %add.9), channel_id=1, source_target_pairs={{0,2},{1,3},{2,0},{3,1},{4,6},{5,7},{6,4},{7,5},{8,10},{9,11},{10,... | collective-permute-start | bytes 12296 | tf_op jit(solution)/shard_map/loss_sum/ppermute | solution.py:511
  119.1 5.1 %collective-permute-start.6 = (f32[8,128]{1,0:T(8,128)S(1)}, f32[8,128]{1,0:T(8,128)S(1)}, u32[]{:S(2)}, u32[]{:S(2)}) collective-permute-start(f32[8,128]{1,0:T(8,128)S(1)} %add.10), channel_id=1, source_target_pairs={{0,4},{1,5},{2,6},{3,7},{4,0},{5,1},{6,2},{7,3},{8,12},{9,13},{10,... | collective-permute-start | bytes 12296 | tf_op jit(solution)/shard_map/loss_sum/ppermute | solution.py:511
  125.4 1.6 %copy-start.5 = (bf16[1024,1024]{1,0:T(8,128)(2,1)S(1)}, bf16[1024,1024]{1,0:T(8,128)(2,1)}, u32[]{:S(2)}) copy-start(bf16[1024,1024]{1,0:T(8,128)(2,1)} %wv_ref.9) | copy-start | bytes 6291460
  127.0 1.6 %copy-start.9 = (bf16[1024,1024]{1,0:T(8,128)(2,1)S(1)}, bf16[1024,1024]{1,0:T(8,128)(2,1)}, u32[]{:S(2)}) copy-start(bf16[1024,1024]{1,0:T(8,128)(2,1)} %wq_ref.7) | copy-start | bytes 6291460
  130.7 1.6 %copy-start.6 = (bf16[1024,1024]{1,0:T(8,128)(2,1)S(1)}, bf16[1024,1024]{1,0:T(8,128)(2,1)}, u32[]{:S(2)}) copy-start(bf16[1024,1024]{1,0:T(8,128)(2,1)} %wv_ref.9) | copy-start | bytes 6291460
  132.3 1.6 %copy-start.10 = (bf16[1024,1024]{1,0:T(8,128)(2,1)S(1)}, bf16[1024,1024]{1,0:T(8,128)(2,1)}, u32[]{:S(2)}) copy-start(bf16[1024,1024]{1,0:T(8,128)(2,1)} %wq_ref.7) | copy-start | bytes 6291460
  (14 other events, 13.7 us)

commit v2 on v1

v2 whole, which is shorter than its diff:
```python
import functools
import math

import jax
import jax.numpy as jnp
from jax import lax
from jax.experimental import pallas as pl
from jax.experimental.pallas import tpu as pltpu
from jax.sharding import PartitionSpec as P

HEADS = 16
HALF = 8
HD = 64
LEVELS = 3
N_LON = 16
N_LAT = 8
TOK = 192
WIDTH = 1024
BAND = 512
SCALE = 0.125
LOG2E = math.log2(math.e)
NEG = -1e30
BF = jnp.bfloat16
F32 = jnp.float32
VMEM = 32 * 1024 * 1024


def call(kernel, outs, flops, nbytes, ins, scratch=()):
    return pl.pallas_call(
        kernel,
        grid=(1,),
        in_specs=[spec for spec, _ in ins],
        out_specs=tuple(spec for spec, _ in outs),
        out_shape=tuple(shape for _, shape in outs),
        scratch_shapes=list(scratch),
        compiler_params=pltpu.CompilerParams(vmem_limit_bytes=VMEM),
        cost_estimate=pl.CostEstimate(flops=50 * flops, bytes_accessed=nbytes, transcendentals=0),
    )(*[x for _, x in ins])


def in_smem(x):
    return (pl.BlockSpec(memory_space=pltpu.SMEM), x)


def in_vmem(x):
    return (pl.BlockSpec(memory_space=pltpu.VMEM), x)


def in_hbm(x):
    return (pl.BlockSpec(memory_space=pltpu.HBM), hbm(x))


def out_vmem(shape, dtype):
    return (pl.BlockSpec(memory_space=pltpu.VMEM), pltpu.VMEM(shape, dtype))


def out_hbm(shape, dtype):
    return (pl.BlockSpec(memory_space=pltpu.HBM), jax.ShapeDtypeStruct(shape, dtype))


def out_block(shape, dtype):
    zeros = (0,) * len(shape)
    return (pl.BlockSpec(shape, lambda g: zeros), jax.ShapeDtypeStruct(shape, dtype))


def begin(pairs, sems):
    copies = [pltpu.make_async_copy(a, b, sems.at[n]) for n, (a, b) in enumerate(pairs)]
    for copy in copies:
        copy.start()
    return copies


def hbm(x):
    return pltpu.with_memory_space_constraint(x, pltpu.HBM)


def dot(a, b):
    return jnp.dot(a, b, preferred_element_type=F32)


def dot_nt(a, b):
    return lax.dot_general(a, b, (((1,), (1,)), ((), ())), preferred_element_type=F32)


def tr(x):
    return jnp.transpose(x)


def band_proj_kernel(
    tok_hbm, wq_hbm, wk_hbm, wv_hbm, out_ref, tok_ref, wq_ref, wk_ref, wv_ref, sems
):
    lanes = pl.ds(0, BAND)
    copies = begin(
        [
            (tok_hbm, tok_ref),
            (wq_hbm.at[:, lanes], wq_ref),
            (wk_hbm.at[:, lanes], wk_ref),
            (wv_hbm.at[:, lanes], wv_ref),
        ],
        sems,
    )
    copies[0].wait()
    tok = tok_ref[...]
    copies[1].wait()
    q = dot(tok, wq_ref[...]).astype(BF)
    copies[2].wait()
    k = dot(tok, wk_ref[...]).astype(BF)
    copies[3].wait()
    v = dot(tok, wv_ref[...]).astype(BF)
    for h in range(HALF):
        lanes = slice(64 * h, 64 * h + 64)
        qk = jnp.concatenate([q[:, lanes], k[:, lanes]], axis=1)
        vh = v[:, lanes]
        for l in range(LEVELS):
            for r in range(2):
                base = l * 64 + r * 32
                out_ref[2 * h + r, 48 * l : 48 * l + 32, :] = qk[base : base + 32]
                out_ref[2 * h + r, 48 * l + 32 : 48 * l + 48, :] = jnp.concatenate(
                    [vh[base : base + 16], vh[base + 16 : base + 32]], axis=1
                )


WEIGHT_HALF = pltpu.VMEM((WIDTH, BAND), BF)


def band_proj(tok, wq, wk, wv):
    return call(
        band_proj_kernel,
        [out_block((N_LON, 144, 128), BF)],
        6 * TOK * WIDTH * BAND,
        4 * 1024 * 1024,
        [in_hbm(x) for x in (tok, wq, wk, wv)],
        [pltpu.VMEM((TOK, WIDTH), BF)] + [WEIGHT_HALF] * 3 + [pltpu.SemaphoreType.DMA((4,))],
    )[0]


def unpack_qkv(x):
    qk = x[:, 0:32, :].reshape(512, 128)
    v = x[:, 32:48, :]
    v = jnp.concatenate([v[:, :, 0:64], v[:, :, 64:128]], axis=1).reshape(512, 64)
    return qk[:, 0:64], qk[:, 64:128], v


def unpack_one(x):
    return jnp.concatenate([x[:, :, 0:64], x[:, :, 64:128]], axis=1).reshape(512, 64)


def pack_one(x):
    x = x.reshape(N_LON, 32, 64)
    return jnp.concatenate([x[:, 0:16, :], x[:, 16:32, :]], axis=2)


def band_fwd_kernel(x_ref, o_ref, stat_ref):
    for l in range(LEVELS):
        q, k, v = unpack_qkv(x_ref[:, 48 * l : 48 * l + 48, :])
        s = dot_nt(k, q) * (SCALE * LOG2E)
        top = jnp.max(s, axis=0, keepdims=True)
        e = jnp.exp2(s - top)
        rtot = 1.0 / jnp.sum(e, axis=0, keepdims=True)
        w = (e * rtot).astype(BF)
        o = tr(dot(tr(v), w)).astype(BF)
        o_ref[:, 16 * l : 16 * l + 16, :] = pack_one(o)
        stat_ref[l, 0:1, :] = top
        stat_ref[l, 1:2, :] = rtot


def band_fwd(x):
    return call(
        band_fwd_kernel,
        [out_block((N_LON, 48, 128), BF), out_vmem((LEVELS, 2, 512), F32)],
        12 * 512 * 512 * 64,
        1024 * 1024,
        [in_vmem(x)],
    )


def band_bwd_kernel(x_ref, o_ref, stat_ref, do_ref, mine_ref, other_ref, out_ref):
    total = jnp.broadcast_to(mine_ref[0:1, :] + other_ref[0:1, :], (16, 128))
    high = total.astype(BF).astype(F32)
    mid = (total - high).astype(BF).astype(F32)
    low = total - high - mid
    at = lax.broadcasted_iota(jnp.int32, (16, 128), 1)
    parts = jnp.where(at == 0, high, jnp.where(at == 1, mid, jnp.where(at == 2, low, 0.0)))
    parts = parts.astype(BF)
    for j in range(N_LON):
        out_ref[j, 144:160, :] = parts
    for l in range(LEVELS):
        q, k, v = unpack_qkv(x_ref[:, 48 * l : 48 * l + 48, :])
        o = unpack_one(o_ref[:, 16 * l : 16 * l + 16, :])
        do = unpack_one(do_ref[:, 16 * l : 16 * l + 16, :])
        s = dot_nt(k, q) * (SCALE * LOG2E)
        p = jnp.exp2(s - stat_ref[l, 0:1, :]) * stat_ref[l, 1:2, :]
        w = p.astype(BF)
        dp = dot_nt(v, do)
        delta = jnp.sum(tr(do.astype(F32) * o.astype(F32)), axis=0, keepdims=True)
        ds = (p * (dp - delta) * SCALE).astype(BF)
        dv = dot(w, do).astype(BF)
        dk = dot(ds, q).astype(BF)
        dq = tr(dot(tr(k), ds)).astype(BF)
        out_ref[:, 48 * l : 48 * l + 32, :] = jnp.concatenate([dq, dk], axis=1).reshape(
            N_LON, 32, 128
        )
        out_ref[:, 48 * l + 32 : 48 * l + 48, :] = pack_one(dv)


def band_bwd(x, o, stat, do, mine, other):
    return call(
        band_bwd_kernel,
        [out_block((N_LON, 160, 128), BF)],
        30 * 512 * 512 * 64,
        2 * 1024 * 1024,
        [in_vmem(y) for y in (x, o, stat, do, mine, other)],
    )[0]


def to_halves(x):
    return jnp.concatenate(
        [x[32 * i + 16 * s : 32 * i + 16 * s + 16] for s in range(2) for i in range(6)], axis=0
    )


def from_halves(x):
    return jnp.concatenate(
        [x[96 * s + 16 * i : 96 * s + 16 * i + 16] for i in range(6) for s in range(2)], axis=0
    )


def win_proj_kernel(
    tok_hbm, wq_hbm, wk_hbm, wv_hbm, q_ref, k_ref, v_ref, tok_ref, wq_ref, wk_ref, wv_ref, sems
):
    lanes = pl.ds(BAND, BAND)
    copies = begin(
        [
            (tok_hbm, tok_ref),
            (wq_hbm.at[:, lanes], wq_ref),
            (wk_hbm.at[:, lanes], wk_ref),
            (wv_hbm.at[:, lanes], wv_ref),
        ],
        sems,
    )
    copies[0].wait()
    tok = to_halves(tok_ref[...])
    copies[1].wait()
    q_ref[...] = dot(tok, wq_ref[...]).astype(BF)
    copies[2].wait()
    k_ref[...] = dot(tok, wk_ref[...]).astype(BF)
    copies[3].wait()
    v_ref[...] = dot(tok, wv_ref[...]).astype(BF)


def win_proj(tok, wq, wk, wv):
    return call(
        win_proj_kernel,
        [out_vmem((TOK, BAND), BF)] * 3,
        6 * TOK * WIDTH * BAND,
        4 * 1024 * 1024,
        [in_hbm(x) for x in (tok, wq, wk, wv)],
        [pltpu.VMEM((TOK, WIDTH), BF)] + [WEIGHT_HALF] * 3 + [pltpu.SemaphoreType.DMA((4,))],
    )


def window_distance(pos):
    key = lax.broadcasted_iota(jnp.int32, (288, 96), 0)
    query = lax.broadcasted_iota(jnp.int32, (288, 96), 1)
    block = (key >= 96).astype(jnp.int32) + (key >= 192).astype(jnp.int32)
    inner = key - 96 * block
    shift = jnp.where(block == 1, -2, jnp.where(block == 2, 2, 0))
    offset = shift + ((inner >> 4) & 1) - ((query >> 4) & 1)
    allowed = (inner & 15) == (query & 15)
    allowed = allowed & ((block != 1) | (pos > 0)) & ((block != 2) | (pos < N_LAT - 1))
    return jnp.where(allowed, jnp.abs(offset), 99)


def extended(own, halo, half):
    rows = slice(96 * half, 96 * half + 96)
    nrows = slice(TOK + 96 * half, TOK + 96 * half + 96)
    return jnp.concatenate([own[rows], halo[rows], halo[nrows]], axis=0)


def win_fwd_kernel(
    pos_ref, reach_ref, q_ref, k_ref, v_ref, prev_ref, next_ref,
    wk_hbm, wv_hbm, o_ref, ot_ref, stat_ref, hk_ref, hv_ref, wk_ref, wv_ref, sems,
):
    lanes = pl.ds(BAND, BAND)
    copies = begin([(wk_hbm.at[:, lanes], wk_ref), (wv_hbm.at[:, lanes], wv_ref)], sems)
    dist = window_distance(pos_ref[0])
    near = jnp.concatenate([to_halves(prev_ref[...]), to_halves(next_ref[...])], axis=0)
    copies[0].wait()
    hk_ref[...] = dot(near, wk_ref[...]).astype(BF)
    copies[1].wait()
    hv_ref[...] = dot(near, wv_ref[...]).astype(BF)
    for half in range(2):
        rows = slice(96 * half, 96 * half + 96)
        q = q_ref[rows]
        k = extended(k_ref[...], hk_ref[...], half)
        vt = tr(extended(v_ref[...], hv_ref[...], half))
        outs = []
        for h in range(HALF):
            lanes = slice(64 * h, 64 * h + 64)
            s = dot_nt(k[:, lanes], q[:, lanes]) * (SCALE * LOG2E)
            s = jnp.where(dist <= reach_ref[h], s, NEG)
            top = jnp.max(s, axis=0, keepdims=True)
            e = jnp.exp2(s - top)
            rtot = 1.0 / jnp.sum(e, axis=0, keepdims=True)
            w = (e * rtot).astype(BF)
            ot = dot(vt[lanes], w)
            outs.append(ot)
            stat_ref[half, 2 * h : 2 * h + 1, :] = top
            stat_ref[half, 2 * h + 1 : 2 * h + 2, :] = rtot
        ot = jnp.concatenate(outs, axis=0)
        ot_ref[half] = ot.astype(BF)
        o_ref[rows] = tr(ot).astype(BF)


def win_fwd(pos, reach, q, k, v, prev, nxt, wk, wv):
    return call(
        win_fwd_kernel,
        [
            out_vmem((TOK, BAND), BF),
            out_vmem((2, BAND, 96), BF),
            out_vmem((2, 16, 96), F32),
            out_vmem((2 * TOK, BAND), BF),
            out_vmem((2 * TOK, BAND), BF),
        ],
        64 * 288 * 128 * 64 + 8 * TOK * WIDTH * BAND,
        6 * 1024 * 1024,
        [in_smem(pos), in_smem(reach)]
        + [in_vmem(x) for x in (q, k, v, prev, nxt)]
        + [in_hbm(x) for x in (wk, wv)],
        [WEIGHT_HALF] * 2 + [pltpu.SemaphoreType.DMA((2,))],
    )


def win_bwd_kernel(
    pos_ref, reach_ref, q_ref, k_ref, v_ref, hk_ref, hv_ref, ot_ref, stat_ref, do_ref,
    p0_ref, p1_ref, p2_ref, p3_ref, dq_ref, own_ref, prev_ref, next_ref, sum_ref,
):
    sum_ref[...] = p0_ref[...] + p1_ref[...] + p2_ref[...] + p3_ref[...]
    dist = window_distance(pos_ref[0])
    do_all = to_halves(do_ref[...])
    for half in range(2):
        rows = slice(96 * half, 96 * half + 96)
        q = q_ref[rows]
        k = extended(k_ref[...], hk_ref[...], half)
        v = extended(v_ref[...], hv_ref[...], half)
        kt = tr(k)
        do = do_all[rows]
        dot_t = tr(do)
        ot = ot_ref[half]
        dqs = []
        for pair in range(HALF // 2):
            dks = []
            dvs = []
            for h in (2 * pair, 2 * pair + 1):
                lanes = slice(64 * h, 64 * h + 64)
                s = dot_nt(k[:, lanes], q[:, lanes]) * (SCALE * LOG2E)
                e = jnp.exp2(s - stat_ref[half, 2 * h : 2 * h + 1, :])
                p = jnp.where(dist <= reach_ref[h], e, 0.0) * stat_ref[half, 2 * h + 1 : 2 * h + 2, :]
                w = p.astype(BF)
                dp = dot_nt(v[:, lanes], do[:, lanes])
                delta = jnp.sum(
                    dot_t[lanes].astype(F32) * ot[lanes].astype(F32), axis=0, keepdims=True
                )
                ds = (p * (dp - delta) * SCALE).astype(BF)
                dvs.append(dot(w, do[:, lanes]))
                dks.append(dot(ds, q[:, lanes]))
                dqs.append(dot(kt[lanes], ds))
            out = slice(128 * pair, 128 * pair + 128)
            for n, parts in enumerate((dks, dvs)):
                both = jnp.concatenate(parts, axis=1)
                own_ref[n, rows, out] = both[0:96]
                prev_ref[n, rows, out] = both[96:192].astype(BF)
                next_ref[n, rows, out] = both[192:288].astype(BF)
        dq_ref[rows] = tr(jnp.concatenate(dqs, axis=0)).astype(BF)


def win_bwd(pos, reach, q, k, v, hk, hv, ot, stat, do, losses):
    return call(
        win_bwd_kernel,
        [
            out_vmem((TOK, BAND), BF),
            out_block((2, TOK, BAND), F32),
            out_block((2, TOK, BAND), BF),
            out_block((2, TOK, BAND), BF),
            out_block((8, 128), F32),
        ],
        160 * 288 * 128 * 64,
        4 * 1024 * 1024,
        [in_smem(pos), in_smem(reach)]
        + [in_vmem(x) for x in (q, k, v, hk, hv, ot, stat, do, *losses)],
    )


def mid_kernel(
    table_ref, tok_hbm, tgt_hbm, wo_hbm, o_ref, win_ref, mixed_hbm, dm_hbm, send_ref, dwin_ref, sum_ref,
    tok_ref, tgt_ref, wo_ref, mixed_ref, dm_ref, att_s, sems,
):
    copies = begin([(wo_hbm, wo_ref), (tok_hbm, tok_ref), (tgt_hbm, tgt_ref)], sems)
    for pair in range(HALF // 2):
        lanes = slice(128 * pair, 128 * pair + 128)
        for l in range(LEVELS):
            for r in range(2):
                base = 64 * l + 32 * r
                a = o_ref[4 * pair + r, 16 * l : 16 * l + 16, :]
                b = o_ref[4 * pair + 2 + r, 16 * l : 16 * l + 16, :]
                att_s[base : base + 16, lanes] = jnp.concatenate([a[:, 0:64], b[:, 0:64]], axis=1)
                att_s[base + 16 : base + 32, lanes] = jnp.concatenate(
                    [a[:, 64:128], b[:, 64:128]], axis=1
                )
    att_s[:, BAND:] = from_halves(win_ref[...])
    att = att_s[...]
    for copy in copies:
        copy.wait()
    d_att = jnp.zeros((TOK, WIDTH), F32)
    total = jnp.zeros((8, 256), F32)
    for g in range(4):
        lanes = slice(256 * g, 256 * g + 256)
        mixed = (tok_ref[:, lanes].astype(F32) + dot(att, wo_ref[:, lanes])).astype(BF)
        mixed_ref[:, lanes] = mixed
        diff = mixed.astype(F32) - tgt_ref[:, lanes].astype(F32)
        weighted = (table_ref[g].astype(F32) * 0.25) * diff
        total = total + jnp.sum((weighted * diff).reshape(TOK // 8, 8, 256), axis=0)
        dm = weighted.astype(BF)
        dm_ref[:, lanes] = dm
        d_att = d_att + dot_nt(dm, wo_ref[:, lanes])
    copies = begin([(mixed_ref, mixed_hbm), (dm_ref, dm_hbm)], sems)
    d_att = d_att.astype(BF)
    dwin_ref[...] = d_att[:, BAND:]
    for h in range(HALF):
        dh = d_att[:, 64 * h : 64 * h + 64]
        for l in range(LEVELS):
            for r in range(2):
                base = 64 * l + 32 * r
                send_ref[2 * h + r, 16 * l : 16 * l + 16, :] = jnp.concatenate(
                    [dh[base : base + 16], dh[base + 16 : base + 32]], axis=1
                )
    sum_ref[...] = jnp.broadcast_to(jnp.sum(total), (8, 128))
    for copy in copies:
        copy.wait()


def mid(table, tok, tgt, o, win, wo):
    return call(
        mid_kernel,
        [
            out_hbm((TOK, WIDTH), BF),
            out_hbm((TOK, WIDTH), BF),
            out_block((N_LON, 48, 128), BF),
            out_vmem((TOK, BAND), BF),
            out_block((8, 128), F32),
        ],
        4 * TOK * WIDTH * WIDTH,
        4 * 1024 * 1024,
        [in_smem(table)]
        + [in_hbm(x) for x in (tok, tgt, wo)]
        + [in_vmem(x) for x in (o, win)],
        [pltpu.VMEM((TOK, WIDTH), BF)] * 2
        + [pltpu.VMEM((WIDTH, WIDTH), BF)]
        + [pltpu.VMEM((TOK, WIDTH), BF)] * 3
        + [pltpu.SemaphoreType.DMA((3,))],
    )


def win_grad_kernel(
    dq_ref, dm_hbm, own_hbm, fp_hbm, fn_hbm, wq_hbm, wk_hbm, wv_hbm,
    out_ref, dm_ref, own_ref, fp_ref, fn_ref, wq_ref, wk_ref, wv_ref, sems,
):
    window = pl.ds(BAND, BAND)
    copies = begin(
        [
            (wq_hbm.at[:, window], wq_ref),
            (wk_hbm.at[:, window], wk_ref),
            (wv_hbm.at[:, window], wv_ref),
            (own_hbm, own_ref),
            (fp_hbm, fp_ref),
            (fn_hbm, fn_ref),
            (dm_hbm, dm_ref),
        ],
        sems,
    )
    dq = dq_ref[...]
    for copy in copies[3:6]:
        copy.wait()
    dk = (own_ref[0] + fp_ref[0].astype(F32) + fn_ref[0].astype(F32)).astype(BF)
    dv = (own_ref[1] + fp_ref[1].astype(F32) + fn_ref[1].astype(F32)).astype(BF)
    for copy in copies[:3]:
        copy.wait()
    g = dot_nt(dq, wq_ref[...]) + dot_nt(dk, wk_ref[...]) + dot_nt(dv, wv_ref[...])
    copies[6].wait()
    out_ref[...] = dm_ref[...].astype(F32) + from_halves(g)


def win_grad(dm, dq, own, fp, fn, wq, wk, wv):
    return call(
        win_grad_kernel,
        [out_block((TOK, WIDTH), F32)],
        6 * TOK * WIDTH * BAND,
        8 * 1024 * 1024,
        [in_vmem(dq)] + [in_hbm(x) for x in (dm, own, fp, fn, wq, wk, wv)],
        [
            pltpu.VMEM((TOK, WIDTH), BF),
            pltpu.VMEM((2, TOK, BAND), F32),
            pltpu.VMEM((2, TOK, BAND), BF),
            pltpu.VMEM((2, TOK, BAND), BF),
        ]
        + [WEIGHT_HALF] * 3
        + [pltpu.SemaphoreType.DMA((7,))],
    )[0]


def band_grad_kernel(
    x_ref, base_hbm, wq_hbm, wk_hbm, wv_hbm, out_hbm, loss_ref,
    base_ref, wq_ref, wk_ref, wv_ref, dq_s, dk_s, dv_s, out_s, sems,
):
    band = pl.ds(0, BAND)
    loads = begin(
        [
            (wq_hbm.at[:, band], wq_ref),
            (wk_hbm.at[:, band], wk_ref),
            (wv_hbm.at[:, band], wv_ref),
            (base_hbm, base_ref),
        ],
        sems,
    )
    for pair in range(HALF // 2):
        lanes = slice(128 * pair, 128 * pair + 128)
        for l in range(LEVELS):
            for r in range(2):
                base = 64 * l + 32 * r
                a = x_ref[4 * pair + r, 48 * l : 48 * l + 48, :]
                b = x_ref[4 * pair + 2 + r, 48 * l : 48 * l + 48, :]
                first = jnp.concatenate([a[:, 0:64], b[:, 0:64]], axis=1)
                second = jnp.concatenate([a[:, 64:128], b[:, 64:128]], axis=1)
                dq_s[base : base + 32, lanes] = first[0:32]
                dk_s[base : base + 32, lanes] = second[0:32]
                dv_s[base : base + 16, lanes] = first[32:48]
                dv_s[base + 16 : base + 32, lanes] = second[32:48]
    dq = dq_s[...]
    dk = dk_s[...]
    dv = dv_s[...]
    for load in loads:
        load.wait()
    copies = []
    for n in range(4):
        rows = slice(256 * n, 256 * n + 256)
        g = dot_nt(dq, wq_ref[rows, :]) + dot_nt(dk, wk_ref[rows, :])
        out_s[:, rows] = base_ref[:, rows] + g + dot_nt(dv, wv_ref[rows, :])
        lanes = pl.ds(256 * n, 256)
        copy = pltpu.make_async_copy(out_s.at[:, lanes], out_hbm.at[:, lanes], sems.at[n])
        copy.start()
        copies.append(copy)
    loss_ref[0, 0] = jnp.sum(x_ref[:, 144, :].astype(F32)) * (1.0 / 25165824)
    for copy in copies:
        copy.wait()


def band_grad(x, base, wq, wk, wv):
    return call(
        band_grad_kernel,
        [
            out_hbm((TOK, WIDTH), F32),
            (pl.BlockSpec(memory_space=pltpu.SMEM), jax.ShapeDtypeStruct((1, 1), F32)),
        ],
        6 * TOK * WIDTH * BAND,
        5 * 1024 * 1024,
        [in_vmem(x)] + [in_hbm(y) for y in (base, wq, wk, wv)],
        [pltpu.VMEM((TOK, WIDTH), F32)]
        + [WEIGHT_HALF] * 3
        + [pltpu.VMEM((TOK, BAND), BF)] * 3
        + [pltpu.VMEM((TOK, WIDTH), F32), pltpu.SemaphoreType.DMA((4,))],
    )


def swap(x):
    return lax.all_to_all(x, "lon", 0, 0, tiled=True)


UP = [(i, (i + 1) % N_LAT) for i in range(N_LAT)]
DOWN = [((i + 1) % N_LAT, i) for i in range(N_LAT)]


def per_device(tokens, targets, w_query, w_key, w_value, w_out, window_reach, loss_table):
    levels, rows, cols, width = tokens.shape
    count = levels * rows * cols
    tok = tokens.reshape(count, width)
    tgt = targets.reshape(count, width)
    pos = lax.axis_index("lat").astype(jnp.int32).reshape(1)
    with jax.named_scope("band_projection"):
        sent = band_proj(tok, w_query, w_key, w_value)
    with jax.named_scope("halo_tokens"):
        prev = lax.ppermute(tok, "lat", UP)
        nxt = lax.ppermute(tok, "lat", DOWN)
    with jax.named_scope("band_qkv_exchange"):
        x = swap(sent)
    with jax.named_scope("window_projection"):
        q, k, v = win_proj(tok, w_query, w_key, w_value)
        x, q, k, v = lax.optimization_barrier((x, q, k, v))
    with jax.named_scope("band_forward"):
        o, stat = band_fwd(x)
        o_back = swap(o)
    with jax.named_scope("window_forward"):
        win, ot, wstat, hk, hv = win_fwd(pos, window_reach, q, k, v, prev, nxt, w_key, w_value)
    with jax.named_scope("middle"):
        mixed, dm, dsend, dwin, part = mid(loss_table, tok, tgt, o_back, win, w_out)
        losses = [part] + [
            lax.ppermute(part, "lat", [(i, i ^ step) for i in range(N_LAT)]) for step in (1, 2, 3)
        ]
        do = swap(dsend)
    with jax.named_scope("window_backward"):
        dqw, own, rim_prev, rim_next, four = win_bwd(
            pos, window_reach, q, k, v, hk, hv, ot, wstat, dwin, losses
        )
        far = lax.ppermute(four, "lat", [(i, i ^ 4) for i in range(N_LAT)])
        from_prev = lax.ppermute(rim_next, "lat", UP)
        from_next = lax.ppermute(rim_prev, "lat", DOWN)
    with jax.named_scope("band_backward"):
        dsent = band_bwd(x, o, stat, do, four, far)
        dx = swap(dsent)
    with jax.named_scope("token_gradient"):
        base = win_grad(dm, dqw, own, from_prev, from_next, w_query, w_key, w_value)
        grad, loss = band_grad(dx, base, w_query, w_key, w_value)
    full = (levels, rows, cols, width)
    return (mixed.reshape(full), grad.reshape(full), loss.reshape(()))


def solution(mesh):
    spec = P(None, "lat", "lon", None)
    return jax.shard_map(
        per_device,
        mesh=mesh,
        in_specs=(spec, spec, P(), P(), P(), P(), P(), P()),
        out_specs=(spec, spec, P()),
        check_vma=False,
    )
```

time: 139 us -> 106 us (0.76)
  local copies, waits for them, and re-layouts: 27 us -> 4.89 us
  blocking collectives: 16.5 us -> 0 us
  Pallas kernels: 27 us -> 36.2 us
  waiting for transfers between devices: 31.7 us -> 26 us
  starting transfers between devices: 33.1 us -> 37.3 us
  between operations: 2.75 us -> 0.97 us
    unnamed x72 -> x18, local copies, waits for them, and re-layouts: 26.5 us -> 4.89 us
    ppermute x3 -> x4, waiting for transfers between devices: 20.7 us -> 0.01 us  [the longest x3 0.01 us: per_device(): lax.ppermute(part, 'lat', [(i, i ^ step) for i in range(N_LAT)])]
    all_to_all x1 -> x0, blocking collectives: 16.5 us -> none  [swap(): return lax.all_to_all(x, 'lon', 0, 0, tiled=True)]
    pallas_call x10 -> x9, Pallas kernels: 27 us -> 36.2 us  [call(): pl.pallas_call(kernel, grid=(1,), in_specs=[spec for spec, _ in ins], out...]
    ppermute x1, waiting for transfers between devices: 0.01 us -> 7.99 us  [per_device(): from_next = lax.ppermute(rim_prev, 'lat', DOWN)]
    all_to_all x3 -> x4, waiting for transfers between devices: 10.9 us -> 15.7 us  [swap(): return lax.all_to_all(x, 'lon', 0, 0, tiled=True)]
    ppermute x1, waiting for transfers between devices: 0.01 us -> 2.37 us  [per_device(): from_prev = lax.ppermute(rim_next, 'lat', UP)]
    all_to_all x3 -> x4, starting transfers between devices: 21 us -> 23 us  [swap(): return lax.all_to_all(x, 'lon', 0, 0, tiled=True)]
  transfers between devices with their start and end apart: 10 -> 12, of which waited for: 4 -> 4; matrix products, arithmetic and copies ran while one was open for 0% -> 0% of each run, Pallas kernels for 12% -> 25%
where the time goes in v2:
time: 106 us; the launch traced here: 105 us
  starting transfers between devices  37.3 us (35%)
  Pallas kernels  36.2 us (34%)
  waiting for transfers between devices  26 us (25%)
  local copies, waits for them, and re-layouts  4.89 us (5%)
    pallas_call x9, Pallas kernels, call(): pl.pallas_call(kernel, grid=(1,), in_specs=[spec for spec, _ in ins], out...  36.2 us
    all_to_all x4, starting transfers between devices, swap(): return lax.all_to_all(x, 'lon', 0, 0, tiled=True)  23 us
    all_to_all x4, waiting for transfers between devices, swap(): return lax.all_to_all(x, 'lon', 0, 0, tiled=True)  15.7 us
    ppermute x1, waiting for transfers between devices, per_device(): from_next = lax.ppermute(rim_prev, 'lat', DOWN)  7.99 us
    unnamed x18, local copies, waits for them, and re-layouts  4.89 us
    ppermute x1, starting transfers between devices, per_device(): nxt = lax.ppermute(tok, 'lat', DOWN)  4.52 us
    ppermute x1, starting transfers between devices, per_device(): from_next = lax.ppermute(rim_prev, 'lat', DOWN)  4.13 us
    ppermute x3, starting transfers between devices, per_device(): lax.ppermute(part, 'lat', [(i, i ^ step) for i in range(N_LAT)])  3.49 us
  transfers between devices with their start and end apart: 12, of which 4 were waited for; matrix products, arithmetic and copies ran while one was open for 0% of the time, Pallas kernels for 25%

profile of v2, /device:TPU:0, one launch (start us, length us, event | category | flops | bytes accessed | tf_op | source)
XLA Modules:
  0.0 105.3 jit_solution(7172846719556051681)
XLA Ops:
  0.6 4.5 %collective-permute-start.1 = (bf16[192,1024]{1,0:T(8,128)(2,1)}, bf16[192,1024]{1,0:T(8,128)(2,1)S(1)}, u32[]{:S(2)}, u32[]{:S(2)}) collective-permute-start(bf16[192,1024]{1,0:T(8,128)(2,1)} %bitcast.6), channel_id=1, source_target_pairs={{1,0},{2,1},{3,2},{4,3},{5,4},{6,5},{7,6},{0,7},{9,8},{10,9},{11,1... | collective-permute-start | bytes 1179656 | tf_op jit(solution)/shard_map/halo_tokens/ppermute | solution.py:592
  5.2 3.4 %band_projection.1 = bf16[16,144,128]{2,1,0:T(8,128)(2,1)} custom-call(bf16[192,1024]{1,0:T(8,128)(2,1)} %bitcast.8, bf16[1024,1024]{1,0:T(8,128)(2,1)} %wq_hbm.7, bf16[1024,1024]{1,0:T(8,128)(2,1)} %wk_hbm.9, bf16[1024,1024]{1,0:T(8,128)(2,1)} %wv_hbm.9), custom_call_target="tpu_custom_call" | custom-call | flops 30198988800 | bytes 4194304 | tf_op jit(solution)/shard_map/band_projection/pallas_call | solution.py:29
  8.6 7.4 %all-to-all-start = ((bf16[16,144,128]{2,1,0:T(8,128)(2,1)}), bf16[16,144,128]{2,1,0:T(8,128)(2,1)S(1)}, u32[]{:S(2)}, u32[]{:S(2)}) async-start(bf16[16,144,128]{2,1,0:T(8,128)(2,1)} %band_projection.1), calls=%async_computation | async-start | bytes 1179648 | tf_op jit(solution)/shard_map/band_qkv_exchange/all_to_all | solution.py:575
  16.0 2.5 %window_projection.1 = (bf16[192,512]{1,0:T(8,128)(2,1)S(1)}, bf16[192,512]{1,0:T(8,128)(2,1)S(1)}, bf16[192,512]{1,0:T(8,128)(2,1)S(1)}) custom-call(bf16[192,1024]{1,0:T(8,128)(2,1)} %bitcast.9, bf16[1024,1024]{1,0:T(8,128)(2,1)} %wq_hbm.7, bf16[1024,1024]{1,0:T(8,128)(2,1)} %wk_hbm.9, bf16[1024,1024]{1,0:T(8,128)(2,1)} %wv_hbm.9), custom_call_target="tpu_custom_call" | custom-call | flops 30198988800 | bytes 4194304 | tf_op jit(solution)/shard_map/window_projection/pallas_call | solution.py:29
  18.6 12.3 %all-to-all-done.x_ref = bf16[16,144,128]{2,1,0:T(8,128)(2,1)S(1)} async-done(((bf16[16,144,128]{2,1,0:T(8,128)(2,1)}), bf16[16,144,128]{2,1,0:T(8,128)(2,1)S(1)}, u32[]{:S(2)}, u32[]{:S(2)}) %all-to-all-start) | async-done | bytes 589856 | tf_op jit(solution)/shard_map/band_qkv_exchange/all_to_all | solution.py:575
  30.9 2.7 %band_forward.1 = (bf16[16,48,128]{2,1,0:T(8,128)(2,1)}, f32[3,2,512]{2,1,0:T(2,128)S(1)}) custom-call(bf16[16,144,128]{2,1,0:T(8,128)(2,1)S(1)} %all-to-all-done.x_ref), custom_call_target="tpu_custom_call" | custom-call | flops 10066329600 | bytes 1048576 | tf_op jit(solution)/shard_map/band_forward/pallas_call | solution.py:29
  33.6 4.4 %all-to-all-start.1 = ((bf16[16,48,128]{2,1,0:T(8,128)(2,1)}), bf16[16,48,128]{2,1,0:T(8,128)(2,1)S(1)}, u32[]{:S(2)}, u32[]{:S(2)}) async-start(bf16[16,48,128]{2,1,0:T(8,128)(2,1)} %get-tuple-element.33.o_ref), calls=%async_computation.1 | async-start | bytes 393216 | tf_op jit(solution)/shard_map/band_forward/all_to_all | solution.py:575
  38.0 0.0 copy-start
  38.1 5.2 %window_forward.1 = (bf16[192,512]{1,0:T(8,128)(2,1)S(1)}, bf16[2,512,96]{2,1,0:T(8,128)(2,1)S(1)}, f32[2,16,96]{2,1,0:T(8,128)S(1)}, bf16[384,512]{1,0:T(8,128)(2,1)S(1)}, bf16[384,512]{1,0:T(8,128)(2,1)S(1)}) custom-call(s32[1]{0:T(128)} %bitcast.2.pos_ref, s32[8]{0:T(128)S(1)} %copy-done.1, bf16[192,512]{1,0:T(8,128)(2,1)S(1)} %get-tuple-element.34.q_ref, ...), custom_call_target="tpu_custom_call" | custom-call | flops 47815065600 | bytes 6291456 | tf_op jit(solution)/shard_map/window_forward/pallas_call | solution.py:29
  43.3 3.3 %all-to-all-done.1.o_ref = bf16[16,48,128]{2,1,0:T(8,128)(2,1)S(1)} async-done(((bf16[16,48,128]{2,1,0:T(8,128)(2,1)}), bf16[16,48,128]{2,1,0:T(8,128)(2,1)S(1)}, u32[]{:S(2)}, u32[]{:S(2)}) %all-to-all-start.1) | async-done | bytes 196640 | tf_op jit(solution)/shard_map/band_forward/all_to_all | solution.py:575
  46.6 5.2 %middle.1 = (bf16[192,1024]{1,0:T(8,128)(2,1)}, bf16[192,1024]{1,0:T(8,128)(2,1)S(1)}, bf16[16,48,128]{2,1,0:T(8,128)(2,1)}, bf16[192,512]{1,0:T(8,128)(2,1)S(1)}, f32[8,128]{1,0:T(8,128)S(1)}) custom-call(s32[4]{0:T(128)S(1)} %copy-done, bf16[192,1024]{1,0:T(8,128)(2,1)} %bitcast.10, bf16[192,1024]{1,0:T(8,128)(2,1)} %bitcast.11, ...), custom_call_target="tpu_custom_call" | custom-call | flops 40265318400 | bytes 4194304 | tf_op jit(solution)/shard_map/middle/pallas_call | solution.py:29
  51.9 0.0 copy-start.4
  51.9 0.7 copy-done.4
  52.5 0.8 copy-done.6
  53.3 0.5 collective-permute-start.3
  53.8 3.0 %collective-permute-start.2 = (f32[8,128]{1,0:T(8,128)S(1)}, f32[8,128]{1,0:T(8,128)S(1)}, u32[]{:S(2)}, u32[]{:S(2)}) collective-permute-start(f32[8,128]{1,0:T(8,128)S(1)} %get-tuple-element.46.p0_ref), channel_id=1, source_target_pairs={{0,1},{1,0},{2,3},{3,2},{4,5},{5,4},{6,7},{7,6},{8,9},{9,8},{10,11... | collective-permute-start | bytes 12296 | tf_op jit(solution)/shard_map/middle/ppermute | solution.py:606
  56.8 3.9 %all-to-all-start.2 = ((bf16[16,48,128]{2,1,0:T(8,128)(2,1)}), bf16[16,48,128]{2,1,0:T(8,128)(2,1)S(1)}, u32[]{:S(2)}, u32[]{:S(2)}) async-start(bf16[16,48,128]{2,1,0:T(8,128)(2,1)} %get-tuple-element.40), calls=%async_computation.2 | async-start | bytes 393216 | tf_op jit(solution)/shard_map/middle/all_to_all | solution.py:575
  60.7 0.0 copy-start.5
  60.8 0.9 copy-done.5
  61.7 4.3 %window_backward.1 = (bf16[192,512]{1,0:T(8,128)(2,1)S(1)}, f32[2,192,512]{2,1,0:T(8,128)S(1)}, bf16[2,192,512]{2,1,0:T(8,128)(2,1)S(1)}, bf16[2,192,512]{2,1,0:T(8,128)(2,1)S(1)}, f32[8,128]{1,0:T(8,128)S(1)}) custom-call(s32[1]{0:T(128)} %bitcast.2.pos_ref, s32[8]{0:T(128)S(1)} %copy-done.1, bf16[192,512]{1,0:T(8,128)(2,1)S(1)} %get-tuple-element.34.q_ref, ...), custom_call_target="tpu_custom_call" | custom-call | flops 18874368000 | bytes 4194304 | tf_op jit(solution)/shard_map/window_backward/pallas_call | solution.py:29
  66.0 0.0 copy-start.2
  66.0 0.9 copy-done.2
  66.9 2.1 %collective-permute-start.5 = (f32[8,128]{1,0:T(8,128)S(1)}, f32[8,128]{1,0:T(8,128)S(1)}, u32[]{:S(2)}, u32[]{:S(2)}) collective-permute-start(f32[8,128]{1,0:T(8,128)S(1)} %get-tuple-element.47.mine_ref), channel_id=1, source_target_pairs={{0,4},{1,5},{2,6},{3,7},{4,0},{5,1},{6,2},{7,3},{8,12},{9,13},{10,... | collective-permute-start | bytes 12296 | tf_op jit(solution)/shard_map/window_backward/ppermute | solution.py:613
  69.1 4.1 %collective-permute-start.7 = (bf16[2,192,512]{2,1,0:T(8,128)(2,1)S(1)}, bf16[2,192,512]{2,1,0:T(8,128)(2,1)S(1)}, u32[]{:S(2)}, u32[]{:S(2)}) collective-permute-start(bf16[2,192,512]{2,1,0:T(8,128)(2,1)S(1)} %get-tuple-element.52), channel_id=1, source_target_pairs={{1,0},{2,1},{3,2},{4,3},{5,4},{6,5},{7,6},{0,7},{9,8},{10,9},{11,1... | collective-permute-start | bytes 1179656 | tf_op jit(solution)/shard_map/window_backward/ppermute | solution.py:615
  73.2 4.2 %band_backward.1 = bf16[16,160,128]{2,1,0:T(8,128)(2,1)} custom-call(bf16[16,144,128]{2,1,0:T(8,128)(2,1)S(1)} %all-to-all-done.x_ref, bf16[16,48,128]{2,1,0:T(8,128)(2,1)} %get-tuple-element.33.o_ref, f32[3,2,512]{2,1,0:T(2,128)S(1)} %get-tuple-element.39.stat_ref, bf16[16,48,128]{2,1,0:T(8,128)(2,1)S(1)} %all-to-all-done.2.do_ref, ...), custom_call_target="tpu_custom_call" | custom-call | flops 25165824000 | bytes 2097152 | tf_op jit(solution)/shard_map/band_backward/pallas_call | solution.py:29
  77.4 7.2 %all-to-all-start.3 = ((bf16[16,160,128]{2,1,0:T(8,128)(2,1)}), bf16[16,160,128]{2,1,0:T(8,128)(2,1)S(1)}, u32[]{:S(2)}, u32[]{:S(2)}) async-start(bf16[16,160,128]{2,1,0:T(8,128)(2,1)} %band_backward.1), calls=%async_computation.3 | async-start | bytes 1310720 | tf_op jit(solution)/shard_map/band_backward/all_to_all | solution.py:575
  84.6 2.4 %collective-permute-done.6.fp_hbm = bf16[2,192,512]{2,1,0:T(8,128)(2,1)S(1)} collective-permute-done((bf16[2,192,512]{2,1,0:T(8,128)(2,1)S(1)}, bf16[2,192,512]{2,1,0:T(8,128)(2,1)S(1)}, u32[]{:S(2)}, u32[]{:S(2)}) %collective-permute-start.6) | collective-permute-done | bytes 393248 | tf_op jit(solution)/shard_map/window_backward/ppermute | solution.py:614
  86.9 8.0 %collective-permute-done.7.fn_hbm = bf16[2,192,512]{2,1,0:T(8,128)(2,1)S(1)} collective-permute-done((bf16[2,192,512]{2,1,0:T(8,128)(2,1)S(1)}, bf16[2,192,512]{2,1,0:T(8,128)(2,1)S(1)}, u32[]{:S(2)}, u32[]{:S(2)}) %collective-permute-start.7) | collective-permute-done | bytes 393248 | tf_op jit(solution)/shard_map/window_backward/ppermute | solution.py:615
  94.9 0.8 copy-done.8
  95.7 3.8 %token_gradient.2.base_hbm = f32[192,1024]{1,0:T(8,128)S(1)} custom-call(bf16[192,512]{1,0:T(8,128)(2,1)S(1)} %get-tuple-element.48.dq_ref, bf16[192,1024]{1,0:T(8,128)(2,1)} %copy-done.6, f32[2,192,512]{2,1,0:T(8,128)} %copy-done.2, bf16[2,192,512]{2,1,0:T(8,128)(2,1)} %copy-done.7, bf16[2,192,512]{2,1,0:T(8,128)(2,1)} %copy-done.8, ...), custom_call_target="tpu_custom_call" | custom-call | flops 30198988800 | bytes 8388608 | tf_op jit(solution)/shard_map/token_gradient/pallas_call | solution.py:29
  99.5 0.9 copy-done.3
  100.4 4.7 %token_gradient.3 = (f32[192,1024]{1,0:T(8,128)}, f32[1,1]{1,0:T(1,128)}) custom-call(bf16[16,160,128]{2,1,0:T(8,128)(2,1)S(1)} %all-to-all-done.3.x_ref, f32[192,1024]{1,0:T(8,128)} %copy-done.3, bf16[1024,1024]{1,0:T(8,128)(2,1)} %wq_hbm.7, bf16[1024,1024]{1,0:T(8,128)(2,1)} %wk_hbm.9, bf16[1024,1024]{1,0:T(8,128)(2,1)} %wv_hbm.9), custom_call_target="tpu_custom_call" | custom-call | flops 30198988800 | bytes 5242880 | tf_op jit(solution)/shard_map/token_gradient/pallas_call | solution.py:29
  (19 shorter events, 0.0 us)
Async XLA Ops:
  0.6 37.4 %collective-permute-start.1 = (bf16[192,1024]{1,0:T(8,128)(2,1)}, bf16[192,1024]{1,0:T(8,128)(2,1)S(1)}, u32[]{:S(2)}, u32[]{:S(2)}) collective-permute-start(bf16[192,1024]{1,0:T(8,128)(2,1)} %bitcast.6), channel_id=1, source_target_pairs={{1,0},{2,1},{3,2},{4,3},{5,4},{6,5},{7,6},{0,7},{9,8},{10,9},{11,1... | collective-permute-start | bytes 1179656 | tf_op jit(solution)/shard_map/halo_tokens/ppermute | solution.py:592
  5.1 32.9 %collective-permute-start = (bf16[192,1024]{1,0:T(8,128)(2,1)}, bf16[192,1024]{1,0:T(8,128)(2,1)S(1)}, u32[]{:S(2)}, u32[]{:S(2)}) collective-permute-start(bf16[192,1024]{1,0:T(8,128)(2,1)} %bitcast.7), channel_id=1, source_target_pairs={{0,1},{1,2},{2,3},{3,4},{4,5},{5,6},{6,7},{7,0},{8,9},{9,10},{10,1... | collective-permute-start | bytes 1179656 | tf_op jit(solution)/shard_map/halo_tokens/ppermute | solution.py:591
  8.6 22.3 %all-to-all-start = ((bf16[16,144,128]{2,1,0:T(8,128)(2,1)}), bf16[16,144,128]{2,1,0:T(8,128)(2,1)S(1)}, u32[]{:S(2)}, u32[]{:S(2)}) async-start(bf16[16,144,128]{2,1,0:T(8,128)(2,1)} %band_projection.1), calls=%async_computation | async-start | bytes 1179648 | tf_op jit(solution)/shard_map/band_qkv_exchange/all_to_all | solution.py:575
  30.9 7.2 %copy-start.1 = (s32[8]{0:T(128)S(1)}, s32[8]{0:T(128)}, u32[]{:S(2)}) copy-start(s32[8]{0:T(128)} %reach_ref.3) | copy-start | bytes 100
  33.6 13.0 %all-to-all-start.1 = ((bf16[16,48,128]{2,1,0:T(8,128)(2,1)}), bf16[16,48,128]{2,1,0:T(8,128)(2,1)S(1)}, u32[]{:S(2)}, u32[]{:S(2)}) async-start(bf16[16,48,128]{2,1,0:T(8,128)(2,1)} %get-tuple-element.33.o_ref), calls=%async_computation.1 | async-start | bytes 393216 | tf_op jit(solution)/shard_map/band_forward/all_to_all | solution.py:575
  38.0 8.6 %copy-start = (s32[4]{0:T(128)S(1)}, s32[4]{0:T(128)}, u32[]{:S(2)}) copy-start(s32[4]{0:T(128)} %table_ref.1) | copy-start | bytes 52
  51.9 0.7 copy-start.4
  52.5 0.8 copy-start.6
  53.3 7.4 %collective-permute-start.4 = (f32[8,128]{1,0:T(8,128)S(1)}, f32[8,128]{1,0:T(8,128)S(1)}, u32[]{:S(2)}, u32[]{:S(2)}) collective-permute-start(f32[8,128]{1,0:T(8,128)S(1)} %get-tuple-element.46.p0_ref), channel_id=1, source_target_pairs={{0,3},{1,2},{2,1},{3,0},{4,7},{5,6},{6,5},{7,4},{8,11},{9,10},{10,... | collective-permute-start | bytes 12296 | tf_op jit(solution)/shard_map/middle/ppermute | solution.py:606
  53.3 7.4 %collective-permute-start.3 = (f32[8,128]{1,0:T(8,128)S(1)}, f32[8,128]{1,0:T(8,128)S(1)}, u32[]{:S(2)}, u32[]{:S(2)}) collective-permute-start(f32[8,128]{1,0:T(8,128)S(1)} %get-tuple-element.46.p0_ref), channel_id=1, source_target_pairs={{0,2},{1,3},{2,0},{3,1},{4,6},{5,7},{6,4},{7,5},{8,10},{9,11},{10,... | collective-permute-start | bytes 12296 | tf_op jit(solution)/shard_map/middle/ppermute | solution.py:606
  53.8 6.9 %collective-permute-start.2 = (f32[8,128]{1,0:T(8,128)S(1)}, f32[8,128]{1,0:T(8,128)S(1)}, u32[]{:S(2)}, u32[]{:S(2)}) collective-permute-start(f32[8,128]{1,0:T(8,128)S(1)} %get-tuple-element.46.p0_ref), channel_id=1, source_target_pairs={{0,1},{1,0},{2,3},{3,2},{4,5},{5,4},{6,7},{7,6},{8,9},{9,8},{10,11... | collective-permute-start | bytes 12296 | tf_op jit(solution)/shard_map/middle/ppermute | solution.py:606
  56.8 16.4 %all-to-all-start.2 = ((bf16[16,48,128]{2,1,0:T(8,128)(2,1)}), bf16[16,48,128]{2,1,0:T(8,128)(2,1)S(1)}, u32[]{:S(2)}, u32[]{:S(2)}) async-start(bf16[16,48,128]{2,1,0:T(8,128)(2,1)} %get-tuple-element.40), calls=%async_computation.2 | async-start | bytes 393216 | tf_op jit(solution)/shard_map/middle/all_to_all | solution.py:575
  60.7 0.9 copy-start.5
  66.0 0.9 copy-start.2
  66.9 6.3 %collective-permute-start.5 = (f32[8,128]{1,0:T(8,128)S(1)}, f32[8,128]{1,0:T(8,128)S(1)}, u32[]{:S(2)}, u32[]{:S(2)}) collective-permute-start(f32[8,128]{1,0:T(8,128)S(1)} %get-tuple-element.47.mine_ref), channel_id=1, source_target_pairs={{0,4},{1,5},{2,6},{3,7},{4,0},{5,1},{6,2},{7,3},{8,12},{9,13},{10,... | collective-permute-start | bytes 12296 | tf_op jit(solution)/shard_map/window_backward/ppermute | solution.py:613
  69.1 17.9 %collective-permute-start.6 = (bf16[2,192,512]{2,1,0:T(8,128)(2,1)S(1)}, bf16[2,192,512]{2,1,0:T(8,128)(2,1)S(1)}, u32[]{:S(2)}, u32[]{:S(2)}) collective-permute-start(bf16[2,192,512]{2,1,0:T(8,128)(2,1)S(1)} %get-tuple-element.51), channel_id=1, source_target_pairs={{0,1},{1,2},{2,3},{3,4},{4,5},{5,6},{6,7},{7,0},{8,9},{9,10},{10,1... | collective-permute-start | bytes 1179656 | tf_op jit(solution)/shard_map/window_backward/ppermute | solution.py:614
  69.1 25.9 %collective-permute-start.7 = (bf16[2,192,512]{2,1,0:T(8,128)(2,1)S(1)}, bf16[2,192,512]{2,1,0:T(8,128)(2,1)S(1)}, u32[]{:S(2)}, u32[]{:S(2)}) collective-permute-start(bf16[2,192,512]{2,1,0:T(8,128)(2,1)S(1)} %get-tuple-element.52), channel_id=1, source_target_pairs={{1,0},{2,1},{3,2},{4,3},{5,4},{6,5},{7,6},{0,7},{9,8},{10,9},{11,1... | collective-permute-start | bytes 1179656 | tf_op jit(solution)/shard_map/window_backward/ppermute | solution.py:615
  77.4 23.0 %all-to-all-start.3 = ((bf16[16,160,128]{2,1,0:T(8,128)(2,1)}), bf16[16,160,128]{2,1,0:T(8,128)(2,1)S(1)}, u32[]{:S(2)}, u32[]{:S(2)}) async-start(bf16[16,160,128]{2,1,0:T(8,128)(2,1)} %band_backward.1), calls=%async_computation.3 | async-start | bytes 1310720 | tf_op jit(solution)/shard_map/band_backward/all_to_all | solution.py:575
  86.9 8.0 %copy-start.7 = (bf16[2,192,512]{2,1,0:T(8,128)(2,1)}, bf16[2,192,512]{2,1,0:T(8,128)(2,1)S(1)}, u32[]{:S(2)}) copy-start(bf16[2,192,512]{2,1,0:T(8,128)(2,1)S(1)} %collective-permute-done.6.fp_hbm) | copy-start | bytes 1179652
  94.9 0.8 copy-start.8
  99.5 0.9 copy-start.3

commit v3 on v2

--- a/solution.py
+++ b/solution.py
@@ -55,12 +55,12 @@
 
 
 def out_hbm(shape, dtype):
-    return (pl.BlockSpec(memory_space=pltpu.HBM), jax.ShapeDtypeStruct(shape, dtype))
+    return (pl.BlockSpec(memory_space=pltpu.HBM), pltpu.HBM(shape, dtype))
 
 
 def out_block(shape, dtype):
     zeros = (0,) * len(shape)
-    return (pl.BlockSpec(shape, lambda g: zeros), jax.ShapeDtypeStruct(shape, dtype))
+    return (pl.BlockSpec(shape, lambda g: zeros), pltpu.HBM(shape, dtype))
 
 
 def begin(pairs, sems):
@@ -251,7 +251,7 @@
 def win_proj(tok, wq, wk, wv):
     return call(
         win_proj_kernel,
-        [out_vmem((TOK, BAND), BF)] * 3,
+        [out_block((TOK, BAND), BF)] * 3,
         6 * TOK * WIDTH * BAND,
         4 * 1024 * 1024,
         [in_hbm(x) for x in (tok, wq, wk, wv)],
@@ -278,23 +278,40 @@
 
 
 def win_fwd_kernel(
-    pos_ref, reach_ref, q_ref, k_ref, v_ref, prev_ref, next_ref,
-    wk_hbm, wv_hbm, o_ref, ot_ref, stat_ref, hk_ref, hv_ref, wk_ref, wv_ref, sems,
+    pos_ref, reach_ref, prev_ref, next_ref, wk_hbm, wv_hbm, wq_hbm, q_hbm, k_hbm, v_hbm,
+    o_ref, stat_ref, hq_ref, hk_ref, hv_ref,
+    wk_ref, wv_ref, wq_ref, q_ref, k_ref, v_ref, sems,
 ):
     lanes = pl.ds(BAND, BAND)
-    copies = begin([(wk_hbm.at[:, lanes], wk_ref), (wv_hbm.at[:, lanes], wv_ref)], sems)
+    copies = begin(
+        [
+            (wk_hbm.at[:, lanes], wk_ref),
+            (wv_hbm.at[:, lanes], wv_ref),
+            (wq_hbm.at[:, lanes], wq_ref),
+            (q_hbm, q_ref),
+            (k_hbm, k_ref),
+            (v_hbm, v_ref),
+        ],
+        sems,
+    )
     dist = window_distance(pos_ref[0])
     near = jnp.concatenate([to_halves(prev_ref[...]), to_halves(next_ref[...])], axis=0)
     copies[0].wait()
     hk_ref[...] = dot(near, wk_ref[...]).astype(BF)
     copies[1].wait()
     hv_ref[...] = dot(near, wv_ref[...]).astype(BF)
+    copies[2].wait()
+    hq_ref[...] = dot(near, wq_ref[...]).astype(BF)
+    for copy in copies[3:6]:
+        copy.wait()
     for half in range(2):
         rows = slice(96 * half, 96 * half + 96)
         q = q_ref[rows]
         k = extended(k_ref[...], hk_ref[...], half)
         vt = tr(extended(v_ref[...], hv_ref[...], half))
         outs = []
+        tops = []
+        rtots = []
         for h in range(HALF):
             lanes = slice(64 * h, 64 * h + 64)
             s = dot_nt(k[:, lanes], q[:, lanes]) * (SCALE * LOG2E)
@@ -303,96 +320,148 @@
             e = jnp.exp2(s - top)
             rtot = 1.0 / jnp.sum(e, axis=0, keepdims=True)
             w = (e * rtot).astype(BF)
-            ot = dot(vt[lanes], w)
-            outs.append(ot)
-            stat_ref[half, 2 * h : 2 * h + 1, :] = top
-            stat_ref[half, 2 * h + 1 : 2 * h + 2, :] = rtot
-        ot = jnp.concatenate(outs, axis=0)
-        ot_ref[half] = ot.astype(BF)
-        o_ref[rows] = tr(ot).astype(BF)
-
-
-def win_fwd(pos, reach, q, k, v, prev, nxt, wk, wv):
+            outs.append(dot(vt[lanes], w))
+            tops.append(top)
+            rtots.append(rtot)
+        o_ref[rows] = tr(jnp.concatenate(outs, axis=0)).astype(BF)
+        stats = jnp.concatenate(tops + rtots + [jnp.zeros((112, 96), F32)], axis=0)
+        stat_ref[rows] = tr(stats)
+
+def win_fwd(pos, reach, q, k, v, prev, nxt, wq, wk, wv):
     return call(
         win_fwd_kernel,
         [
             out_vmem((TOK, BAND), BF),
-            out_vmem((2, BAND, 96), BF),
-            out_vmem((2, 16, 96), F32),
-            out_vmem((2 * TOK, BAND), BF),
-            out_vmem((2 * TOK, BAND), BF),
-        ],
-        64 * 288 * 128 * 64 + 8 * TOK * WIDTH * BAND,
+            out_vmem((TOK, 128), F32),
+            out_block((2 * TOK, BAND), BF),
+            out_block((2 * TOK, BAND), BF),
+            out_block((2 * TOK, BAND), BF),
+        ],
+        64 * 288 * 128 * 64 + 12 * TOK * WIDTH * BAND,
         6 * 1024 * 1024,
         [in_smem(pos), in_smem(reach)]
-        + [in_vmem(x) for x in (q, k, v, prev, nxt)]
-        + [in_hbm(x) for x in (wk, wv)],
-        [WEIGHT_HALF] * 2 + [pltpu.SemaphoreType.DMA((2,))],
-    )
-
-
-def win_bwd_kernel(
-    pos_ref, reach_ref, q_ref, k_ref, v_ref, hk_ref, hv_ref, ot_ref, stat_ref, do_ref,
-    p0_ref, p1_ref, p2_ref, p3_ref, dq_ref, own_ref, prev_ref, next_ref, sum_ref,
+        + [in_vmem(prev), in_vmem(nxt)]
+        + [in_hbm(x) for x in (wk, wv, wq, q, k, v)],
+        [WEIGHT_HALF] * 3
+        + [pltpu.VMEM((TOK, BAND), BF)] * 3
+        + [pltpu.SemaphoreType.DMA((9,))],
+    )
+
+
+def statistics(rows):
+    parts = tr(rows.astype(F32))
+    return parts[0:32] + parts[32:64] + parts[64:96]
+
+
+def neighbour_distance(pos):
+    key = lax.broadcasted_iota(jnp.int32, (96, 192), 0)
+    lane = lax.broadcasted_iota(jnp.int32, (96, 192), 1)
+    after = lane >= 96
+    query = lane - jnp.where(after, 96, 0)
+    offset = ((key >> 4) & 1) - ((query >> 4) & 1) + jnp.where(after, -2, 2)
+    allowed = (key & 15) == (query & 15)
+    allowed = allowed & (after | (pos > 0)) & (~after | (pos < N_LAT - 1))
+    return jnp.where(allowed, jnp.abs(offset), 99)
+
+
+def win_grad_kernel(
+    pos_ref, reach_ref, prev_ref, next_ref, q_hbm, k_hbm, v_hbm, hk_hbm, hv_hbm, pay_hbm, hq_hbm,
+    dm_hbm, wq_hbm, wk_hbm, wv_hbm, out_ref,
+    q_ref, k_ref, v_ref, hk_ref, hv_ref, pay_ref, hq_ref, dm_ref, wq_ref, wk_ref, wv_ref,
+    dq_s, dk_s, dv_s, sems,
 ):
-    sum_ref[...] = p0_ref[...] + p1_ref[...] + p2_ref[...] + p3_ref[...]
+    window = pl.ds(BAND, BAND)
+    copies = begin(
+        [
+            (q_hbm, q_ref),
+            (k_hbm, k_ref),
+            (v_hbm, v_ref),
+            (hk_hbm, hk_ref),
+            (hv_hbm, hv_ref),
+            (pay_hbm, pay_ref),
+            (hq_hbm, hq_ref),
+            (wq_hbm.at[:, window], wq_ref),
+            (wk_hbm.at[:, window], wk_ref),
+            (wv_hbm.at[:, window], wv_ref),
+            (dm_hbm, dm_ref),
+        ],
+        sems,
+    )
     dist = window_distance(pos_ref[0])
-    do_all = to_halves(do_ref[...])
+    near_dist = neighbour_distance(pos_ref[0])
+    for copy in copies[:7]:
+        copy.wait()
     for half in range(2):
         rows = slice(96 * half, 96 * half + 96)
+        nrows = slice(TOK + 96 * half, TOK + 96 * half + 96)
         q = q_ref[rows]
         k = extended(k_ref[...], hk_ref[...], half)
         v = extended(v_ref[...], hv_ref[...], half)
         kt = tr(k)
-        do = do_all[rows]
-        dot_t = tr(do)
-        ot = ot_ref[half]
+        do = pay_ref[rows, 0:BAND]
+        stat = statistics(pay_ref[rows, BAND:])
+        near_q = jnp.concatenate([hq_ref[rows], hq_ref[nrows]], axis=0)
+        near_pay = jnp.concatenate([prev_ref[rows], next_ref[rows]], axis=0)
+        near_do = near_pay[:, 0:BAND]
+        near_stat = statistics(near_pay[:, BAND:])
         dqs = []
         for pair in range(HALF // 2):
             dks = []
             dvs = []
             for h in (2 * pair, 2 * pair + 1):
                 lanes = slice(64 * h, 64 * h + 64)
-                s = dot_nt(k[:, lanes], q[:, lanes]) * (SCALE * LOG2E)
-                e = jnp.exp2(s - stat_ref[half, 2 * h : 2 * h + 1, :])
-                p = jnp.where(dist <= reach_ref[h], e, 0.0) * stat_ref[half, 2 * h + 1 : 2 * h + 2, :]
-                w = p.astype(BF)
-                dp = dot_nt(v[:, lanes], do[:, lanes])
-                delta = jnp.sum(
-                    dot_t[lanes].astype(F32) * ot[lanes].astype(F32), axis=0, keepdims=True
-                )
-                ds = (p * (dp - delta) * SCALE).astype(BF)
-                dvs.append(dot(w, do[:, lanes]))
-                dks.append(dot(ds, q[:, lanes]))
+                qh, kh, vh, doh = q[:, lanes], k[:, lanes], v[:, lanes], do[:, lanes]
+                s = dot_nt(kh, qh) * (SCALE * LOG2E)
+                e = jnp.exp2(s - stat[h : h + 1])
+                p = jnp.where(dist <= reach_ref[h], e * stat[8 + h : 9 + h], 0.0)
+                dp = dot_nt(vh, doh)
+                ds = (p * (dp - stat[16 + h : 17 + h]) * SCALE).astype(BF)
                 dqs.append(dot(kt[lanes], ds))
+                qn, don = near_q[:, lanes], near_do[:, lanes]
+                s = dot_nt(kh[0:96], qn) * (SCALE * LOG2E)
+                e = jnp.exp2(s - near_stat[h : h + 1])
+                pn = jnp.where(near_dist <= reach_ref[h], e * near_stat[8 + h : 9 + h], 0.0)
+                dp = dot_nt(vh[0:96], don)
+                dsn = (pn * (dp - near_stat[16 + h : 17 + h]) * SCALE).astype(BF)
+                dvs.append(dot(p[0:96].astype(BF), doh) + dot(pn.astype(BF), don))
+                dks.append(dot(ds[0:96], qh) + dot(dsn, qn))
             out = slice(128 * pair, 128 * pair + 128)
-            for n, parts in enumerate((dks, dvs)):
-                both = jnp.concatenate(parts, axis=1)
-                own_ref[n, rows, out] = both[0:96]
-                prev_ref[n, rows, out] = both[96:192].astype(BF)
-                next_ref[n, rows, out] = both[192:288].astype(BF)
-        dq_ref[rows] = tr(jnp.concatenate(dqs, axis=0)).astype(BF)
-
-
-def win_bwd(pos, reach, q, k, v, hk, hv, ot, stat, do, losses):
-    return call(
-        win_bwd_kernel,
-        [
-            out_vmem((TOK, BAND), BF),
-            out_block((2, TOK, BAND), F32),
-            out_block((2, TOK, BAND), BF),
-            out_block((2, TOK, BAND), BF),
-            out_block((8, 128), F32),
-        ],
-        160 * 288 * 128 * 64,
-        4 * 1024 * 1024,
+            dk_s[rows, out] = jnp.concatenate(dks, axis=1).astype(BF)
+            dv_s[rows, out] = jnp.concatenate(dvs, axis=1).astype(BF)
+        dq_s[rows] = tr(jnp.concatenate(dqs, axis=0)).astype(BF)
+    for copy in copies[7:]:
+        copy.wait()
+    g = dot_nt(dq_s[...], wq_ref[...])
+    g = g + dot_nt(dk_s[...], wk_ref[...]) + dot_nt(dv_s[...], wv_ref[...])
+    out_ref[...] = dm_ref[...].astype(F32) + from_halves(g)
+
+
+def win_grad(pos, reach, q, k, v, hk, hv, pay, hq, prev, nxt, dm, wq, wk, wv):
+    return call(
+        win_grad_kernel,
+        [out_block((TOK, WIDTH), F32)],
+        6 * TOK * WIDTH * BAND + 200 * 288 * 128 * 64,
+        8 * 1024 * 1024,
         [in_smem(pos), in_smem(reach)]
-        + [in_vmem(x) for x in (q, k, v, hk, hv, ot, stat, do, *losses)],
-    )
+        + [in_vmem(prev), in_vmem(nxt)]
+        + [in_hbm(x) for x in (q, k, v, hk, hv, pay, hq, dm, wq, wk, wv)],
+        [pltpu.VMEM((TOK, BAND), BF)] * 3
+        + [
+            pltpu.VMEM((2 * TOK, BAND), BF),
+            pltpu.VMEM((2 * TOK, BAND), BF),
+            pltpu.VMEM((TOK, BAND + 128), BF),
+            pltpu.VMEM((2 * TOK, BAND), BF),
+            pltpu.VMEM((TOK, WIDTH), BF),
+        ]
+        + [WEIGHT_HALF] * 3
+        + [pltpu.VMEM((TOK, BAND), BF)] * 3
+        + [pltpu.SemaphoreType.DMA((11,))],
+    )[0]
 
 
 def mid_kernel(
-    table_ref, tok_hbm, tgt_hbm, wo_hbm, o_ref, win_ref, mixed_hbm, dm_hbm, send_ref, dwin_ref, sum_ref,
+    table_ref, tok_hbm, tgt_hbm, wo_hbm, o_ref, win_ref, stat_ref,
+    mixed_hbm, dm_hbm, send_ref, pay_ref, sum_ref,
     tok_ref, tgt_ref, wo_ref, mixed_ref, dm_ref, att_s, sems,
 ):
     copies = begin([(wo_hbm, wo_ref), (tok_hbm, tok_ref), (tgt_hbm, tgt_ref)], sems)
@@ -425,7 +494,20 @@
         d_att = d_att + dot_nt(dm, wo_ref[:, lanes])
     copies = begin([(mixed_ref, mixed_hbm), (dm_ref, dm_hbm)], sems)
     d_att = d_att.astype(BF)
-    dwin_ref[...] = d_att[:, BAND:]
+    dwin = to_halves(d_att[:, BAND:])
+    pay_ref[:, 0:BAND] = dwin
+    terms = dwin.astype(F32) * win_ref[...].astype(F32)
+    first = terms.astype(BF)
+    second = (terms - first.astype(F32)).astype(BF)
+    feature = lax.broadcasted_iota(jnp.int32, (BAND, 128), 0)
+    lane = lax.broadcasted_iota(jnp.int32, (BAND, 128), 1)
+    gather = ((feature >> 6) + 16 == lane).astype(F32).astype(BF)
+    stat = stat_ref[...] + dot(first, gather) + dot(second, gather)
+    high = stat.astype(BF).astype(F32)
+    middle = (stat - high).astype(BF).astype(F32)
+    low = stat - high - middle
+    packed = high + pltpu.roll(middle, 32, 1) + pltpu.roll(low, 64, 1)
+    pay_ref[:, BAND:] = packed.astype(BF)
     for h in range(HALF):
         dh = d_att[:, 64 * h : 64 * h + 64]
         for l in range(LEVELS):
@@ -439,73 +521,26 @@
         copy.wait()
 
 
-def mid(table, tok, tgt, o, win, wo):
+def mid(table, tok, tgt, o, win, stat, wo):
     return call(
         mid_kernel,
         [
             out_hbm((TOK, WIDTH), BF),
             out_hbm((TOK, WIDTH), BF),
             out_block((N_LON, 48, 128), BF),
-            out_vmem((TOK, BAND), BF),
+            out_block((TOK, BAND + 128), BF),
             out_block((8, 128), F32),
         ],
         4 * TOK * WIDTH * WIDTH,
         4 * 1024 * 1024,
         [in_smem(table)]
         + [in_hbm(x) for x in (tok, tgt, wo)]
-        + [in_vmem(x) for x in (o, win)],
+        + [in_vmem(x) for x in (o, win, stat)],
         [pltpu.VMEM((TOK, WIDTH), BF)] * 2
         + [pltpu.VMEM((WIDTH, WIDTH), BF)]
         + [pltpu.VMEM((TOK, WIDTH), BF)] * 3
         + [pltpu.SemaphoreType.DMA((3,))],
     )
-
-
-def win_grad_kernel(
-    dq_ref, dm_hbm, own_hbm, fp_hbm, fn_hbm, wq_hbm, wk_hbm, wv_hbm,
-    out_ref, dm_ref, own_ref, fp_ref, fn_ref, wq_ref, wk_ref, wv_ref, sems,
-):
-    window = pl.ds(BAND, BAND)
-    copies = begin(
-        [
-            (wq_hbm.at[:, window], wq_ref),
-            (wk_hbm.at[:, window], wk_ref),
-            (wv_hbm.at[:, window], wv_ref),
-            (own_hbm, own_ref),
-            (fp_hbm, fp_ref),
-            (fn_hbm, fn_ref),
-            (dm_hbm, dm_ref),
-        ],
-        sems,
-    )
-    dq = dq_ref[...]
-    for copy in copies[3:6]:
-        copy.wait()
-    dk = (own_ref[0] + fp_ref[0].astype(F32) + fn_ref[0].astype(F32)).astype(BF)
-    dv = (own_ref[1] + fp_ref[1].astype(F32) + fn_ref[1].astype(F32)).astype(BF)
-    for copy in copies[:3]:
-        copy.wait()
-    g = dot_nt(dq, wq_ref[...]) + dot_nt(dk, wk_ref[...]) + dot_nt(dv, wv_ref[...])
-    copies[6].wait()
-    out_ref[...] = dm_ref[...].astype(F32) + from_halves(g)
-
-
-def win_grad(dm, dq, own, fp, fn, wq, wk, wv):
-    return call(
-        win_grad_kernel,
-        [out_block((TOK, WIDTH), F32)],
-        6 * TOK * WIDTH * BAND,
-        8 * 1024 * 1024,
-        [in_vmem(dq)] + [in_hbm(x) for x in (dm, own, fp, fn, wq, wk, wv)],
-        [
-            pltpu.VMEM((TOK, WIDTH), BF),
-            pltpu.VMEM((2, TOK, BAND), F32),
-            pltpu.VMEM((2, TOK, BAND), BF),
-            pltpu.VMEM((2, TOK, BAND), BF),
-        ]
-        + [WEIGHT_HALF] * 3
-        + [pltpu.SemaphoreType.DMA((7,))],
-    )[0]
 
 
 def band_grad_kernel(
@@ -589,35 +624,38 @@
         sent = band_proj(tok, w_query, w_key, w_value)
     with jax.named_scope("halo_tokens"):
         prev = lax.ppermute(tok, "lat", UP)
-        nxt = lax.ppermute(tok, "lat", DOWN)
     with jax.named_scope("band_qkv_exchange"):
         x = swap(sent)
     with jax.named_scope("window_projection"):
         q, k, v = win_proj(tok, w_query, w_key, w_value)
-        x, q, k, v = lax.optimization_barrier((x, q, k, v))
+        x, q, k, v, tok_later = lax.optimization_barrier((x, q, k, v, tok))
+        nxt = lax.ppermute(tok_later, "lat", DOWN)
     with jax.named_scope("band_forward"):
         o, stat = band_fwd(x)
         o_back = swap(o)
     with jax.named_scope("window_forward"):
-        win, ot, wstat, hk, hv = win_fwd(pos, window_reach, q, k, v, prev, nxt, w_key, w_value)
+        win, wstat, hq, hk, hv = win_fwd(
+            pos, window_reach, q, k, v, prev, nxt, w_query, w_key, w_value
+        )
     with jax.named_scope("middle"):
-        mixed, dm, dsend, dwin, part = mid(loss_table, tok, tgt, o_back, win, w_out)
+        mixed, dm, dsend, pay, part = mid(loss_table, tok, tgt, o_back, win, wstat, w_out)
         losses = [part] + [
             lax.ppermute(part, "lat", [(i, i ^ step) for i in range(N_LAT)]) for step in (1, 2, 3)
         ]
         do = swap(dsend)
-    with jax.named_scope("window_backward"):
-        dqw, own, rim_prev, rim_next, four = win_bwd(
-            pos, window_reach, q, k, v, hk, hv, ot, wstat, dwin, losses
-        )
+        pay_prev = lax.ppermute(pay, "lat", UP)
+        pay_next = lax.ppermute(pay, "lat", DOWN)
+    with jax.named_scope("band_backward"):
+        four = losses[0] + losses[1] + losses[2] + losses[3]
         far = lax.ppermute(four, "lat", [(i, i ^ 4) for i in range(N_LAT)])
-        from_prev = lax.ppermute(rim_next, "lat", UP)
-        from_next = lax.ppermute(rim_prev, "lat", DOWN)
-    with jax.named_scope("band_backward"):
         dsent = band_bwd(x, o, stat, do, four, far)
         dx = swap(dsent)
+    with jax.named_scope("window_gradient"):
+        base = win_grad(
+            pos, window_reach, q, k, v, hk, hv, pay, hq, pay_prev, pay_next, dm,
+            w_query, w_key, w_value,
+        )
     with jax.named_scope("token_gradient"):
-        base = win_grad(dm, dqw, own, from_prev, from_next, w_query, w_key, w_value)
         grad, loss = band_grad(dx, base, w_query, w_key, w_value)
     full = (levels, rows, cols, width)
     return (mixed.reshape(full), grad.reshape(full), loss.reshape(()))

time: 106 us -> 93.6 us (0.88)
  waiting for transfers between devices: 26 us -> 18.5 us
  starting transfers between devices: 37.3 us -> 31.8 us
  local copies, waits for them, and re-layouts: 4.89 us -> 0.02 us
  Pallas kernels: 36.2 us -> 40.5 us
    ppermute x3, waiting for transfers between devices: 10.4 us -> 2.68 us  [the longest x1 2.56 us: per_device(): nxt = lax.ppermute(tok_later, 'lat', DOWN)]
    unnamed x18 -> x8, local copies, waits for them, and re-layouts: 4.89 us -> 0.02 us
    ppermute x3, starting transfers between devices: 8.65 us -> 4.09 us  [the longest x1 2.18 us: per_device(): pay_next = lax.ppermute(pay, 'lat', DOWN)]
    pallas_call x9 -> x8, Pallas kernels: 36.2 us -> 40.5 us  [call(): pl.pallas_call(kernel, grid=(1,), in_specs=[spec for spec, _ in ins], out...]
    all_to_all x4, starting transfers between devices: 23 us -> 20 us  [swap(): return lax.all_to_all(x, 'lon', 0, 0, tiled=True)]
    ppermute x1, starting transfers between devices: 0.01 us -> 2.07 us  [per_device(): prev = lax.ppermute(tok, 'lat', UP)]
  transfers between devices with their start and end apart: 12 -> 12, of which waited for: 4 -> 6; matrix products, arithmetic and copies ran while one was open for 0% -> 1% of each run, Pallas kernels for 25% -> 32%
where the time goes in v3:
time: 93.6 us; the launch traced here: 92.5 us
  Pallas kernels  40.5 us (43%)
  starting transfers between devices  31.8 us (34%)
  waiting for transfers between devices  18.5 us (20%)
  between operations  0.94 us (1%)
    pallas_call x8, Pallas kernels, call(): pl.pallas_call(kernel, grid=(1,), in_specs=[spec for spec, _ in ins], out...  40.5 us
    all_to_all x4, starting transfers between devices, swap(): return lax.all_to_all(x, 'lon', 0, 0, tiled=True)  20 us
    all_to_all x4, waiting for transfers between devices, swap(): return lax.all_to_all(x, 'lon', 0, 0, tiled=True)  15 us
    ppermute x3, starting transfers between devices, per_device(): lax.ppermute(part, 'lat', [(i, i ^ step) for i in range(N_LAT)])  3.57 us
    ppermute x1, waiting for transfers between devices, per_device(): nxt = lax.ppermute(tok_later, 'lat', DOWN)  2.56 us
    ppermute x1, starting transfers between devices, per_device(): pay_next = lax.ppermute(pay, 'lat', DOWN)  2.18 us
    ppermute x1, starting transfers between devices, per_device(): far = lax.ppermute(four, 'lat', [(i, i ^ 4) for i in range(N_LAT)])  2.08 us
    ppermute x1, starting transfers between devices, per_device(): prev = lax.ppermute(tok, 'lat', UP)  2.07 us
  transfers between devices with their start and end apart: 12, of which 6 were waited for; matrix products, arithmetic and copies ran while one was open for 1% of the time, Pallas kernels for 32%

profile of v3, /device:TPU:0, one launch (start us, length us, event | category | flops | bytes accessed | tf_op | source)
XLA Modules:
  0.0 92.5 jit_solution(14735299613184173296)
XLA Ops:
  0.6 2.1 %collective-permute-start = (bf16[192,1024]{1,0:T(8,128)(2,1)}, bf16[192,1024]{1,0:T(8,128)(2,1)S(1)}, u32[]{:S(2)}, u32[]{:S(2)}) collective-permute-start(bf16[192,1024]{1,0:T(8,128)(2,1)} %bitcast.6), channel_id=1, source_target_pairs={{0,1},{1,2},{2,3},{3,4},{4,5},{5,6},{6,7},{7,0},{8,9},{9,10},{10,1... | collective-permute-start | bytes 1179656 | tf_op jit(solution)/shard_map/halo_tokens/ppermute | solution.py:626
  2.7 3.4 %band_projection.1 = bf16[16,144,128]{2,1,0:T(8,128)(2,1)} custom-call(bf16[192,1024]{1,0:T(8,128)(2,1)} %bitcast.7, bf16[1024,1024]{1,0:T(8,128)(2,1)} %wq_hbm.9, bf16[1024,1024]{1,0:T(8,128)(2,1)} %wk_hbm.9, bf16[1024,1024]{1,0:T(8,128)(2,1)} %wv_hbm.9), custom_call_target="tpu_custom_call" | custom-call | flops 30198988800 | bytes 4194304 | tf_op jit(solution)/shard_map/band_projection/pallas_call | solution.py:29
  6.1 7.4 %all-to-all-start = ((bf16[16,144,128]{2,1,0:T(8,128)(2,1)}), bf16[16,144,128]{2,1,0:T(8,128)(2,1)S(1)}, u32[]{:S(2)}, u32[]{:S(2)}) async-start(bf16[16,144,128]{2,1,0:T(8,128)(2,1)} %band_projection.1), calls=%async_computation | async-start | bytes 1179648 | tf_op jit(solution)/shard_map/band_qkv_exchange/all_to_all | solution.py:610
  13.6 0.0 copy-start.3
  13.6 3.2 %window_projection.1 = (bf16[192,512]{1,0:T(8,128)(2,1)}, bf16[192,512]{1,0:T(8,128)(2,1)}, bf16[192,512]{1,0:T(8,128)(2,1)}) custom-call(bf16[192,1024]{1,0:T(8,128)(2,1)} %bitcast.8, bf16[1024,1024]{1,0:T(8,128)(2,1)} %wq_hbm.9, bf16[1024,1024]{1,0:T(8,128)(2,1)} %wk_hbm.9, bf16[1024,1024]{1,0:T(8,128)(2,1)} %wv_hbm.9), custom_call_target="tpu_custom_call" | custom-call | flops 30198988800 | bytes 4194304 | tf_op jit(solution)/shard_map/window_projection/pallas_call | solution.py:29
  16.8 9.8 %all-to-all-done.x_ref = bf16[16,144,128]{2,1,0:T(8,128)(2,1)S(1)} async-done(((bf16[16,144,128]{2,1,0:T(8,128)(2,1)}), bf16[16,144,128]{2,1,0:T(8,128)(2,1)S(1)}, u32[]{:S(2)}, u32[]{:S(2)}) %all-to-all-start) | async-done | bytes 589856 | tf_op jit(solution)/shard_map/band_qkv_exchange/all_to_all | solution.py:610
  26.6 1.9 %collective-permute-start.1 = (bf16[192,1024]{1,0:T(8,128)(2,1)S(1)}, bf16[192,1024]{1,0:T(8,128)(2,1)S(1)}, u32[]{:S(2)}, u32[]{:S(2)}) collective-permute-start(bf16[192,1024]{1,0:T(8,128)(2,1)S(1)} %bitcast.10), channel_id=1, source_target_pairs={{1,0},{2,1},{3,2},{4,3},{5,4},{6,5},{7,6},{0,7},{9,8},{10,9},{11,1... | collective-permute-start | bytes 1179656 | tf_op jit(solution)/shard_map/window_projection/ppermute | solution.py:632
  28.5 2.7 %band_forward.1 = (bf16[16,48,128]{2,1,0:T(8,128)(2,1)}, f32[3,2,512]{2,1,0:T(2,128)S(1)}) custom-call(bf16[16,144,128]{2,1,0:T(8,128)(2,1)S(1)} %all-to-all-done.x_ref), custom_call_target="tpu_custom_call" | custom-call | flops 10066329600 | bytes 1048576 | tf_op jit(solution)/shard_map/band_forward/pallas_call | solution.py:29
  31.3 3.5 %all-to-all-start.1 = ((bf16[16,48,128]{2,1,0:T(8,128)(2,1)}), bf16[16,48,128]{2,1,0:T(8,128)(2,1)S(1)}, u32[]{:S(2)}, u32[]{:S(2)}) async-start(bf16[16,48,128]{2,1,0:T(8,128)(2,1)} %get-tuple-element.29.o_ref), calls=%async_computation.1 | async-start | bytes 393216 | tf_op jit(solution)/shard_map/band_forward/all_to_all | solution.py:610
  34.8 0.0 collective-permute-done.prev_ref
  34.8 2.6 %collective-permute-done.1.next_ref = bf16[192,1024]{1,0:T(8,128)(2,1)S(1)} collective-permute-done((bf16[192,1024]{1,0:T(8,128)(2,1)S(1)}, bf16[192,1024]{1,0:T(8,128)(2,1)S(1)}, u32[]{:S(2)}, u32[]{:S(2)}) %collective-permute-start.1) | collective-permute-done | bytes 393248 | tf_op jit(solution)/shard_map/window_projection/ppermute | solution.py:632
  37.4 6.0 %window_forward.1 = (bf16[192,512]{1,0:T(8,128)(2,1)S(1)}, f32[192,128]{1,0:T(8,128)S(1)}, bf16[384,512]{1,0:T(8,128)(2,1)}, bf16[384,512]{1,0:T(8,128)(2,1)}, bf16[384,512]{1,0:T(8,128)(2,1)}) custom-call(s32[1]{0:T(128)} %bitcast.2.pos_ref, s32[8]{0:T(128)S(1)} %copy-done.2, bf16[192,1024]{1,0:T(8,128)(2,1)S(1)} %collective-permute-done.prev_ref, ...), custom_call_target="tpu_custom_call" | custom-call | flops 67947724800 | bytes 6291456 | tf_op jit(solution)/shard_map/window_forward/pallas_call | solution.py:29
  43.4 0.0 all-to-all-done.1.o_ref
  43.4 0.0 copy-start
  43.5 5.9 %middle.1 = (bf16[192,1024]{1,0:T(8,128)(2,1)}, bf16[192,1024]{1,0:T(8,128)(2,1)}, bf16[16,48,128]{2,1,0:T(8,128)(2,1)}, bf16[192,640]{1,0:T(8,128)(2,1)}, f32[8,128]{1,0:T(8,128)}) custom-call(s32[4]{0:T(128)S(1)} %copy-done.1, bf16[192,1024]{1,0:T(8,128)(2,1)} %bitcast.9, bf16[192,1024]{1,0:T(8,128)(2,1)} %bitcast.11, bf16[1024,1024]{1,0:T(8,128)(2,1)} %wo_hbm.1, ...), custom_call_target="tpu_custom_call" | custom-call | flops 40265318400 | bytes 4194304 | tf_op jit(solution)/shard_map/middle/pallas_call | solution.py:29
  49.4 2.8 %collective-permute-start.4 = (f32[8,128]{1,0:T(8,128)}, f32[8,128]{1,0:T(8,128)S(1)}, u32[]{:S(2)}, u32[]{:S(2)}) collective-permute-start(f32[8,128]{1,0:T(8,128)} %get-tuple-element.39), channel_id=1, source_target_pairs={{0,3},{1,2},{2,1},{3,0},{4,7},{5,6},{6,5},{7,4},{8,11},{9,10},{10,... | collective-permute-start | bytes 12296 | tf_op jit(solution)/shard_map/middle/ppermute | solution.py:643
  52.2 0.3 collective-permute-start.3
  52.4 0.5 collective-permute-start.2
  52.9 4.6 %all-to-all-start.2 = ((bf16[16,48,128]{2,1,0:T(8,128)(2,1)}), bf16[16,48,128]{2,1,0:T(8,128)(2,1)S(1)}, u32[]{:S(2)}, u32[]{:S(2)}) async-start(bf16[16,48,128]{2,1,0:T(8,128)(2,1)} %get-tuple-element.38), calls=%async_computation.2 | async-start | bytes 393216 | tf_op jit(solution)/shard_map/middle/all_to_all | solution.py:610
  57.6 0.0 collective-permute-done.3
  57.6 0.7 add_add_fusion.mine_ref
  58.3 2.1 %collective-permute-start.5 = (f32[8,128]{1,0:T(8,128)S(1)}, f32[8,128]{1,0:T(8,128)S(1)}, u32[]{:S(2)}, u32[]{:S(2)}) collective-permute-start(f32[8,128]{1,0:T(8,128)S(1)} %add_add_fusion.mine_ref), channel_id=1, source_target_pairs={{0,4},{1,5},{2,6},{3,7},{4,0},{5,1},{6,2},{7,3},{8,12},{9,13},{10,... | collective-permute-start | bytes 12296 | tf_op jit(solution)/shard_map/band_backward/ppermute | solution.py:650
  60.4 2.2 %collective-permute-start.7 = (bf16[192,640]{1,0:T(8,128)(2,1)}, bf16[192,640]{1,0:T(8,128)(2,1)S(1)}, u32[]{:S(2)}, u32[]{:S(2)}) collective-permute-start(bf16[192,640]{1,0:T(8,128)(2,1)} %get-tuple-element.40.pay_hbm), channel_id=1, source_target_pairs={{1,0},{2,1},{3,2},{4,3},{5,4},{6,5},{7,6},{0,7},{9,8},{10,9},{11,1... | collective-permute-start | bytes 737288 | tf_op jit(solution)/shard_map/middle/ppermute | solution.py:647
  62.6 0.0 collective-permute-start.6
  62.6 0.8 collective-permute-done.5.other_ref
  63.4 2.8 %all-to-all-done.2.do_ref = bf16[16,48,128]{2,1,0:T(8,128)(2,1)S(1)} async-done(((bf16[16,48,128]{2,1,0:T(8,128)(2,1)}), bf16[16,48,128]{2,1,0:T(8,128)(2,1)S(1)}, u32[]{:S(2)}, u32[]{:S(2)}) %all-to-all-start.2) | async-done | bytes 196640 | tf_op jit(solution)/shard_map/middle/all_to_all | solution.py:610
  66.2 3.2 %band_backward.1 = bf16[16,160,128]{2,1,0:T(8,128)(2,1)} custom-call(bf16[16,144,128]{2,1,0:T(8,128)(2,1)S(1)} %all-to-all-done.x_ref, bf16[16,48,128]{2,1,0:T(8,128)(2,1)S(1)} %copy-done, f32[3,2,512]{2,1,0:T(2,128)S(1)} %get-tuple-element.37.stat_ref, bf16[16,48,128]{2,1,0:T(8,128)(2,1)S(1)} %all-to-all-done.2.do_ref, f32[8,128]{1,0:T(8,128)S(1)} %add_add_fusion.mine_ref, ...), custom_call_target="tpu_custom_call" | custom-call | flops 25165824000 | bytes 2097152 | tf_op jit(solution)/shard_map/band_backward/pallas_call | solution.py:29
  69.4 4.4 %all-to-all-start.3 = ((bf16[16,160,128]{2,1,0:T(8,128)(2,1)}), bf16[16,160,128]{2,1,0:T(8,128)(2,1)S(1)}, u32[]{:S(2)}, u32[]{:S(2)}) async-start(bf16[16,160,128]{2,1,0:T(8,128)(2,1)} %band_backward.1), calls=%async_computation.3 | async-start | bytes 1310720 | tf_op jit(solution)/shard_map/band_backward/all_to_all | solution.py:610
  73.9 0.1 collective-permute-done.7.next_ref
  74.0 11.2 %window_gradient.1.base_hbm = f32[192,1024]{1,0:T(8,128)} custom-call(s32[1]{0:T(128)} %bitcast.2.pos_ref, s32[8]{0:T(128)S(1)} %copy-done.2, bf16[192,640]{1,0:T(8,128)(2,1)S(1)} %collective-permute-done.6.prev_ref, bf16[192,640]{1,0:T(8,128)(2,1)S(1)} %collective-permute-done.7.next_ref, bf16[192,512]{1,0:T(8,128)(2,1)} %get-tuple-element.31.q_hbm, ...), custom_call_target="tpu_custom_call" | custom-call | flops 53791948800 | bytes 8388608 | tf_op jit(solution)/shard_map/window_gradient/pallas_call | solution.py:29
  85.2 2.4 %all-to-all-done.3.x_ref = bf16[16,160,128]{2,1,0:T(8,128)(2,1)S(1)} async-done(((bf16[16,160,128]{2,1,0:T(8,128)(2,1)}), bf16[16,160,128]{2,1,0:T(8,128)(2,1)S(1)}, u32[]{:S(2)}, u32[]{:S(2)}) %all-to-all-start.3) | async-done | bytes 655392 | tf_op jit(solution)/shard_map/band_backward/all_to_all | solution.py:610
  87.7 4.7 %token_gradient.1 = (f32[192,1024]{1,0:T(8,128)}, f32[1,1]{1,0:T(1,128)}) custom-call(bf16[16,160,128]{2,1,0:T(8,128)(2,1)S(1)} %all-to-all-done.3.x_ref, f32[192,1024]{1,0:T(8,128)} %window_gradient.1.base_hbm, bf16[1024,1024]{1,0:T(8,128)(2,1)} %wq_hbm.9, bf16[1024,1024]{1,0:T(8,128)(2,1)} %wk_hbm.9, bf16[1024,1024]{1,0:T(8,128)(2,1)} %wv_hbm.9), custom_call_target="tpu_custom_call" | custom-call | flops 30198988800 | bytes 5242880 | tf_op jit(solution)/shard_map/token_gradient/pallas_call | solution.py:29
  (9 shorter events, 0.0 us)
Async XLA Ops:
  0.6 34.2 %collective-permute-start = (bf16[192,1024]{1,0:T(8,128)(2,1)}, bf16[192,1024]{1,0:T(8,128)(2,1)S(1)}, u32[]{:S(2)}, u32[]{:S(2)}) collective-permute-start(bf16[192,1024]{1,0:T(8,128)(2,1)} %bitcast.6), channel_id=1, source_target_pairs={{0,1},{1,2},{2,3},{3,4},{4,5},{5,6},{6,7},{7,0},{8,9},{9,10},{10,1... | collective-permute-start | bytes 1179656 | tf_op jit(solution)/shard_map/halo_tokens/ppermute | solution.py:626
  6.1 20.5 %all-to-all-start = ((bf16[16,144,128]{2,1,0:T(8,128)(2,1)}), bf16[16,144,128]{2,1,0:T(8,128)(2,1)S(1)}, u32[]{:S(2)}, u32[]{:S(2)}) async-start(bf16[16,144,128]{2,1,0:T(8,128)(2,1)} %band_projection.1), calls=%async_computation | async-start | bytes 1179648 | tf_op jit(solution)/shard_map/band_qkv_exchange/all_to_all | solution.py:610
  13.6 13.1 %copy-start.3 = (bf16[3,2,32,1024]{3,2,1,0:T(8,128)(2,1)S(1)}, bf16[3,2,32,1024]{3,2,1,0:T(8,128)(2,1)}, u32[]{:S(2)}) copy-start(bf16[3,2,32,1024]{3,2,1,0:T(8,128)(2,1)} %param.8) | copy-start | bytes 1179652
  26.6 10.8 %copy-start.2 = (s32[8]{0:T(128)S(1)}, s32[8]{0:T(128)}, u32[]{:S(2)}) copy-start(s32[8]{0:T(128)} %reach_ref.3) | copy-start | bytes 100
  26.6 10.8 %collective-permute-start.1 = (bf16[192,1024]{1,0:T(8,128)(2,1)S(1)}, bf16[192,1024]{1,0:T(8,128)(2,1)S(1)}, u32[]{:S(2)}, u32[]{:S(2)}) collective-permute-start(bf16[192,1024]{1,0:T(8,128)(2,1)S(1)} %bitcast.10), channel_id=1, source_target_pairs={{1,0},{2,1},{3,2},{4,3},{5,4},{6,5},{7,6},{0,7},{9,8},{10,9},{11,1... | collective-permute-start | bytes 1179656 | tf_op jit(solution)/shard_map/window_projection/ppermute | solution.py:632
  31.3 12.1 %all-to-all-start.1 = ((bf16[16,48,128]{2,1,0:T(8,128)(2,1)}), bf16[16,48,128]{2,1,0:T(8,128)(2,1)S(1)}, u32[]{:S(2)}, u32[]{:S(2)}) async-start(bf16[16,48,128]{2,1,0:T(8,128)(2,1)} %get-tuple-element.29.o_ref), calls=%async_computation.1 | async-start | bytes 393216 | tf_op jit(solution)/shard_map/band_forward/all_to_all | solution.py:610
  37.4 6.1 %copy-start.1 = (s32[4]{0:T(128)S(1)}, s32[4]{0:T(128)}, u32[]{:S(2)}) copy-start(s32[4]{0:T(128)} %table_ref.1) | copy-start | bytes 52
  43.4 22.8 %copy-start = (bf16[16,48,128]{2,1,0:T(8,128)(2,1)S(1)}, bf16[16,48,128]{2,1,0:T(8,128)(2,1)}, u32[]{:S(2)}) copy-start(bf16[16,48,128]{2,1,0:T(8,128)(2,1)} %get-tuple-element.29.o_ref) | copy-start | bytes 589828
  49.4 8.2 %collective-permute-start.4 = (f32[8,128]{1,0:T(8,128)}, f32[8,128]{1,0:T(8,128)S(1)}, u32[]{:S(2)}, u32[]{:S(2)}) collective-permute-start(f32[8,128]{1,0:T(8,128)} %get-tuple-element.39), channel_id=1, source_target_pairs={{0,3},{1,2},{2,1},{3,0},{4,7},{5,6},{6,5},{7,4},{8,11},{9,10},{10,... | collective-permute-start | bytes 12296 | tf_op jit(solution)/shard_map/middle/ppermute | solution.py:643
  52.2 5.4 %collective-permute-start.3 = (f32[8,128]{1,0:T(8,128)}, f32[8,128]{1,0:T(8,128)S(1)}, u32[]{:S(2)}, u32[]{:S(2)}) collective-permute-start(f32[8,128]{1,0:T(8,128)} %get-tuple-element.39), channel_id=1, source_target_pairs={{0,2},{1,3},{2,0},{3,1},{4,6},{5,7},{6,4},{7,5},{8,10},{9,11},{10,... | collective-permute-start | bytes 12296 | tf_op jit(solution)/shard_map/middle/ppermute | solution.py:643
  52.4 5.2 %collective-permute-start.2 = (f32[8,128]{1,0:T(8,128)}, f32[8,128]{1,0:T(8,128)S(1)}, u32[]{:S(2)}, u32[]{:S(2)}) collective-permute-start(f32[8,128]{1,0:T(8,128)} %get-tuple-element.39), channel_id=1, source_target_pairs={{0,1},{1,0},{2,3},{3,2},{4,5},{5,4},{6,7},{7,6},{8,9},{9,8},{10,11... | collective-permute-start | bytes 12296 | tf_op jit(solution)/shard_map/middle/ppermute | solution.py:643
  52.9 13.3 %all-to-all-start.2 = ((bf16[16,48,128]{2,1,0:T(8,128)(2,1)}), bf16[16,48,128]{2,1,0:T(8,128)(2,1)S(1)}, u32[]{:S(2)}, u32[]{:S(2)}) async-start(bf16[16,48,128]{2,1,0:T(8,128)(2,1)} %get-tuple-element.38), calls=%async_computation.2 | async-start | bytes 393216 | tf_op jit(solution)/shard_map/middle/all_to_all | solution.py:610
  58.3 5.1 %collective-permute-start.5 = (f32[8,128]{1,0:T(8,128)S(1)}, f32[8,128]{1,0:T(8,128)S(1)}, u32[]{:S(2)}, u32[]{:S(2)}) collective-permute-start(f32[8,128]{1,0:T(8,128)S(1)} %add_add_fusion.mine_ref), channel_id=1, source_target_pairs={{0,4},{1,5},{2,6},{3,7},{4,0},{5,1},{6,2},{7,3},{8,12},{9,13},{10,... | collective-permute-start | bytes 12296 | tf_op jit(solution)/shard_map/band_backward/ppermute | solution.py:650
  60.4 13.6 %collective-permute-start.7 = (bf16[192,640]{1,0:T(8,128)(2,1)}, bf16[192,640]{1,0:T(8,128)(2,1)S(1)}, u32[]{:S(2)}, u32[]{:S(2)}) collective-permute-start(bf16[192,640]{1,0:T(8,128)(2,1)} %get-tuple-element.40.pay_hbm), channel_id=1, source_target_pairs={{1,0},{2,1},{3,2},{4,3},{5,4},{6,5},{7,6},{0,7},{9,8},{10,9},{11,1... | collective-permute-start | bytes 737288 | tf_op jit(solution)/shard_map/middle/ppermute | solution.py:647
  62.6 11.4 %collective-permute-start.6 = (bf16[192,640]{1,0:T(8,128)(2,1)}, bf16[192,640]{1,0:T(8,128)(2,1)S(1)}, u32[]{:S(2)}, u32[]{:S(2)}) collective-permute-start(bf16[192,640]{1,0:T(8,128)(2,1)} %get-tuple-element.40.pay_hbm), channel_id=1, source_target_pairs={{0,1},{1,2},{2,3},{3,4},{4,5},{5,6},{6,7},{7,0},{8,9},{9,10},{10,1... | collective-permute-start | bytes 737288 | tf_op jit(solution)/shard_map/middle/ppermute | solution.py:646
  69.4 18.2 %all-to-all-start.3 = ((bf16[16,160,128]{2,1,0:T(8,128)(2,1)}), bf16[16,160,128]{2,1,0:T(8,128)(2,1)S(1)}, u32[]{:S(2)}, u32[]{:S(2)}) async-start(bf16[16,160,128]{2,1,0:T(8,128)(2,1)} %band_backward.1), calls=%async_computation.3 | async-start | bytes 1310720 | tf_op jit(solution)/shard_map/band_backward/all_to_all | solution.py:610

commit v4 on v3

--- a/solution.py
+++ b/solution.py
@@ -226,7 +226,8 @@
 
 
 def win_proj_kernel(
-    tok_hbm, wq_hbm, wk_hbm, wv_hbm, q_ref, k_ref, v_ref, tok_ref, wq_ref, wk_ref, wv_ref, sems
+    prev_ref, tok_hbm, wq_hbm, wk_hbm, wv_hbm, q_ref, k_ref, v_ref,
+    tok_ref, wq_ref, wk_ref, wv_ref, sems,
 ):
     lanes = pl.ds(BAND, BAND)
     copies = begin(
@@ -239,7 +240,7 @@
         sems,
     )
     copies[0].wait()
-    tok = to_halves(tok_ref[...])
+    tok = jnp.concatenate([to_halves(tok_ref[...]), to_halves(prev_ref[...])], axis=0)
     copies[1].wait()
     q_ref[...] = dot(tok, wq_ref[...]).astype(BF)
     copies[2].wait()
@@ -248,13 +249,13 @@
     v_ref[...] = dot(tok, wv_ref[...]).astype(BF)
 
 
-def win_proj(tok, wq, wk, wv):
+def win_proj(tok, prev, wq, wk, wv):
     return call(
         win_proj_kernel,
-        [out_block((TOK, BAND), BF)] * 3,
-        6 * TOK * WIDTH * BAND,
+        [out_block((2 * TOK, BAND), BF)] * 3,
+        12 * TOK * WIDTH * BAND,
         4 * 1024 * 1024,
-        [in_hbm(x) for x in (tok, wq, wk, wv)],
+        [in_vmem(prev)] + [in_hbm(x) for x in (tok, wq, wk, wv)],
         [pltpu.VMEM((TOK, WIDTH), BF)] + [WEIGHT_HALF] * 3 + [pltpu.SemaphoreType.DMA((4,))],
     )
 
@@ -271,14 +272,14 @@
     return jnp.where(allowed, jnp.abs(offset), 99)
 
 
-def extended(own, halo, half):
+def extended(two, nxt, half):
     rows = slice(96 * half, 96 * half + 96)
-    nrows = slice(TOK + 96 * half, TOK + 96 * half + 96)
-    return jnp.concatenate([own[rows], halo[rows], halo[nrows]], axis=0)
+    prows = slice(TOK + 96 * half, TOK + 96 * half + 96)
+    return jnp.concatenate([two[rows], two[prows], nxt[rows]], axis=0)
 
 
 def win_fwd_kernel(
-    pos_ref, reach_ref, prev_ref, next_ref, wk_hbm, wv_hbm, wq_hbm, q_hbm, k_hbm, v_hbm,
+    pos_ref, reach_ref, next_ref, wk_hbm, wv_hbm, wq_hbm, q_hbm, k_hbm, v_hbm,
     o_ref, stat_ref, hq_ref, hk_ref, hv_ref,
     wk_ref, wv_ref, wq_ref, q_ref, k_ref, v_ref, sems,
 ):
@@ -295,7 +296,7 @@
         sems,
     )
     dist = window_distance(pos_ref[0])
-    near = jnp.concatenate([to_halves(prev_ref[...]), to_halves(next_ref[...])], axis=0)
+    near = to_halves(next_ref[...])
     copies[0].wait()
     hk_ref[...] = dot(near, wk_ref[...]).astype(BF)
     copies[1].wait()
@@ -327,24 +328,24 @@
         stats = jnp.concatenate(tops + rtots + [jnp.zeros((112, 96), F32)], axis=0)
         stat_ref[rows] = tr(stats)
 
-def win_fwd(pos, reach, q, k, v, prev, nxt, wq, wk, wv):
+def win_fwd(pos, reach, q, k, v, nxt, wq, wk, wv):
     return call(
         win_fwd_kernel,
         [
-            out_vmem((TOK, BAND), BF),
-            out_vmem((TOK, 128), F32),
-            out_block((2 * TOK, BAND), BF),
-            out_block((2 * TOK, BAND), BF),
-            out_block((2 * TOK, BAND), BF),
-        ],
-        64 * 288 * 128 * 64 + 12 * TOK * WIDTH * BAND,
+            out_block((TOK, BAND), BF),
+            out_block((TOK, 128), F32),
+            out_block((TOK, BAND), BF),
+            out_block((TOK, BAND), BF),
+            out_block((TOK, BAND), BF),
+        ],
+        64 * 288 * 128 * 64 + 6 * TOK * WIDTH * BAND,
         6 * 1024 * 1024,
         [in_smem(pos), in_smem(reach)]
-        + [in_vmem(prev), in_vmem(nxt)]
+        + [in_vmem(nxt)]
         + [in_hbm(x) for x in (wk, wv, wq, q, k, v)],
         [WEIGHT_HALF] * 3
-        + [pltpu.VMEM((TOK, BAND), BF)] * 3
-        + [pltpu.SemaphoreType.DMA((9,))],
+        + [pltpu.VMEM((2 * TOK, BAND), BF)] * 3
+        + [pltpu.SemaphoreType.DMA((6,))],
     )
 
 
@@ -393,14 +394,14 @@
         copy.wait()
     for half in range(2):
         rows = slice(96 * half, 96 * half + 96)
-        nrows = slice(TOK + 96 * half, TOK + 96 * half + 96)
+        prows = slice(TOK + 96 * half, TOK + 96 * half + 96)
         q = q_ref[rows]
         k = extended(k_ref[...], hk_ref[...], half)
         v = extended(v_ref[...], hv_ref[...], half)
         kt = tr(k)
         do = pay_ref[rows, 0:BAND]
         stat = statistics(pay_ref[rows, BAND:])
-        near_q = jnp.concatenate([hq_ref[rows], hq_ref[nrows]], axis=0)
+        near_q = jnp.concatenate([q_ref[prows], hq_ref[rows]], axis=0)
         near_pay = jnp.concatenate([prev_ref[rows], next_ref[rows]], axis=0)
         near_do = near_pay[:, 0:BAND]
         near_stat = statistics(near_pay[:, BAND:])
@@ -445,12 +446,12 @@
         [in_smem(pos), in_smem(reach)]
         + [in_vmem(prev), in_vmem(nxt)]
         + [in_hbm(x) for x in (q, k, v, hk, hv, pay, hq, dm, wq, wk, wv)],
-        [pltpu.VMEM((TOK, BAND), BF)] * 3
+        [pltpu.VMEM((2 * TOK, BAND), BF)] * 3
         + [
-            pltpu.VMEM((2 * TOK, BAND), BF),
-            pltpu.VMEM((2 * TOK, BAND), BF),
+            pltpu.VMEM((TOK, BAND), BF),
+            pltpu.VMEM((TOK, BAND), BF),
             pltpu.VMEM((TOK, BAND + 128), BF),
-            pltpu.VMEM((2 * TOK, BAND), BF),
+            pltpu.VMEM((TOK, BAND), BF),
             pltpu.VMEM((TOK, WIDTH), BF),
         ]
         + [WEIGHT_HALF] * 3
@@ -460,11 +461,13 @@
 
 
 def mid_kernel(
-    table_ref, tok_hbm, tgt_hbm, wo_hbm, o_ref, win_ref, stat_ref,
+    table_ref, tok_hbm, tgt_hbm, win_hbm, stat_hbm, wo_ref, o_ref,
     mixed_hbm, dm_hbm, send_ref, pay_ref, sum_ref,
-    tok_ref, tgt_ref, wo_ref, mixed_ref, dm_ref, att_s, sems,
+    tok_ref, tgt_ref, win_ref, stat_ref, mixed_ref, dm_ref, att_s, sems,
 ):
-    copies = begin([(wo_hbm, wo_ref), (tok_hbm, tok_ref), (tgt_hbm, tgt_ref)], sems)
+    copies = begin(
+        [(win_hbm, win_ref), (tok_hbm, tok_ref), (tgt_hbm, tgt_ref), (stat_hbm, stat_ref)], sems
+    )
     for pair in range(HALF // 2):
         lanes = slice(128 * pair, 128 * pair + 128)
         for l in range(LEVELS):
@@ -476,9 +479,10 @@
                 att_s[base + 16 : base + 32, lanes] = jnp.concatenate(
                     [a[:, 64:128], b[:, 64:128]], axis=1
                 )
+    copies[0].wait()
     att_s[:, BAND:] = from_halves(win_ref[...])
     att = att_s[...]
-    for copy in copies:
+    for copy in copies[1:]:
         copy.wait()
     d_att = jnp.zeros((TOK, WIDTH), F32)
     total = jnp.zeros((8, 256), F32)
@@ -534,12 +538,12 @@
         4 * TOK * WIDTH * WIDTH,
         4 * 1024 * 1024,
         [in_smem(table)]
-        + [in_hbm(x) for x in (tok, tgt, wo)]
-        + [in_vmem(x) for x in (o, win, stat)],
+        + [in_hbm(x) for x in (tok, tgt, win, stat)]
+        + [in_vmem(x) for x in (wo, o)],
         [pltpu.VMEM((TOK, WIDTH), BF)] * 2
-        + [pltpu.VMEM((WIDTH, WIDTH), BF)]
+        + [pltpu.VMEM((TOK, BAND), BF), pltpu.VMEM((TOK, 128), F32)]
         + [pltpu.VMEM((TOK, WIDTH), BF)] * 3
-        + [pltpu.SemaphoreType.DMA((3,))],
+        + [pltpu.SemaphoreType.DMA((4,))],
     )
 
 
@@ -573,13 +577,16 @@
     dq = dq_s[...]
     dk = dk_s[...]
     dv = dv_s[...]
-    for load in loads:
-        load.wait()
+    loads[0].wait()
+    out_s[...] = dot_nt(dq, wq_ref[...])
+    loads[1].wait()
+    out_s[...] += dot_nt(dk, wk_ref[...])
+    loads[2].wait()
+    loads[3].wait()
     copies = []
     for n in range(4):
         rows = slice(256 * n, 256 * n + 256)
-        g = dot_nt(dq, wq_ref[rows, :]) + dot_nt(dk, wk_ref[rows, :])
-        out_s[:, rows] = base_ref[:, rows] + g + dot_nt(dv, wv_ref[rows, :])
+        out_s[:, rows] += base_ref[:, rows] + dot_nt(dv, wv_ref[rows, :])
         lanes = pl.ds(256 * n, 256)
         copy = pltpu.make_async_copy(out_s.at[:, lanes], out_hbm.at[:, lanes], sems.at[n])
         copy.start()
@@ -627,7 +634,7 @@
     with jax.named_scope("band_qkv_exchange"):
         x = swap(sent)
     with jax.named_scope("window_projection"):
-        q, k, v = win_proj(tok, w_query, w_key, w_value)
+        q, k, v = win_proj(tok, prev, w_query, w_key, w_value)
         x, q, k, v, tok_later = lax.optimization_barrier((x, q, k, v, tok))
         nxt = lax.ppermute(tok_later, "lat", DOWN)
     with jax.named_scope("band_forward"):
@@ -635,16 +642,16 @@
         o_back = swap(o)
     with jax.named_scope("window_forward"):
         win, wstat, hq, hk, hv = win_fwd(
-            pos, window_reach, q, k, v, prev, nxt, w_query, w_key, w_value
+            pos, window_reach, q, k, v, nxt, w_query, w_key, w_value
         )
     with jax.named_scope("middle"):
         mixed, dm, dsend, pay, part = mid(loss_table, tok, tgt, o_back, win, wstat, w_out)
+        do = swap(dsend)
+        pay_prev = lax.ppermute(pay, "lat", UP)
+        pay_next = lax.ppermute(pay, "lat", DOWN)
         losses = [part] + [
             lax.ppermute(part, "lat", [(i, i ^ step) for i in range(N_LAT)]) for step in (1, 2, 3)
         ]
-        do = swap(dsend)
-        pay_prev = lax.ppermute(pay, "lat", UP)
-        pay_next = lax.ppermute(pay, "lat", DOWN)
     with jax.named_scope("band_backward"):
         four = losses[0] + losses[1] + losses[2] + losses[3]
         far = lax.ppermute(four, "lat", [(i, i ^ 4) for i in range(N_LAT)])

time: 93.6 us -> 92.1 us (0.984)
  Pallas kernels: 40.5 us -> 39.5 us
    all_to_all x4, waiting for transfers between devices: 15 us -> 13.5 us  [swap(): return lax.all_to_all(x, 'lon', 0, 0, tiled=True)]
    pallas_call x8, Pallas kernels: 40.5 us -> 39.5 us  [call(): pl.pallas_call(kernel, grid=(1,), in_specs=[spec for spec, _ in ins], out...]
  transfers between devices with their start and end apart: 12 -> 12, of which waited for: 6 -> 7; matrix products, arithmetic and copies ran while one was open for 1% -> 1% of each run, Pallas kernels for 32% -> 34%
where the time goes in v4:
time: 92.1 us; the launch traced here: 91 us
  Pallas kernels  39.5 us (43%)
  starting transfers between devices  31.8 us (35%)
  waiting for transfers between devices  18 us (20%)
  between operations  0.94 us (1%)
    pallas_call x8, Pallas kernels, call(): pl.pallas_call(kernel, grid=(1,), in_specs=[spec for spec, _ in ins], out...  39.5 us
    all_to_all x4, starting transfers between devices, swap(): return lax.all_to_all(x, 'lon', 0, 0, tiled=True)  20 us
    all_to_all x4, waiting for transfers between devices, swap(): return lax.all_to_all(x, 'lon', 0, 0, tiled=True)  13.5 us
    ppermute x3, starting transfers between devices, per_device(): lax.ppermute(part, 'lat', [(i, i ^ step) for i in range(N_LAT)])  3.57 us
    ppermute x1, waiting for transfers between devices, per_device(): nxt = lax.ppermute(tok_later, 'lat', DOWN)  2.59 us
    ppermute x1, starting transfers between devices, per_device(): pay_next = lax.ppermute(pay, 'lat', DOWN)  2.18 us
    ppermute x1, starting transfers between devices, per_device(): far = lax.ppermute(four, 'lat', [(i, i ^ 4) for i in range(N_LAT)])  2.13 us
    ppermute x1, starting transfers between devices, per_device(): prev = lax.ppermute(tok, 'lat', UP)  2.07 us
  transfers between devices with their start and end apart: 12, of which 7 were waited for; matrix products, arithmetic and copies ran while one was open for 1% of the time, Pallas kernels for 34%

profile of v4, /device:TPU:0, one launch (start us, length us, event | category | flops | bytes accessed | tf_op | source)
XLA Modules:
  0.0 91.0 jit_solution(571997574970476410)
XLA Ops:
  0.6 2.1 %collective-permute-start = (bf16[192,1024]{1,0:T(8,128)(2,1)}, bf16[192,1024]{1,0:T(8,128)(2,1)S(1)}, u32[]{:S(2)}, u32[]{:S(2)}) collective-permute-start(bf16[192,1024]{1,0:T(8,128)(2,1)} %bitcast.6), channel_id=1, source_target_pairs={{0,1},{1,2},{2,3},{3,4},{4,5},{5,6},{6,7},{7,0},{8,9},{9,10},{10,1... | collective-permute-start | bytes 1179656 | tf_op jit(solution)/shard_map/halo_tokens/ppermute | solution.py:633
  2.7 3.4 %band_projection.1 = bf16[16,144,128]{2,1,0:T(8,128)(2,1)} custom-call(bf16[192,1024]{1,0:T(8,128)(2,1)} %bitcast.7, bf16[1024,1024]{1,0:T(8,128)(2,1)} %wq_hbm.9, bf16[1024,1024]{1,0:T(8,128)(2,1)} %wk_hbm.9, bf16[1024,1024]{1,0:T(8,128)(2,1)} %wv_hbm.9), custom_call_target="tpu_custom_call" | custom-call | flops 30198988800 | bytes 4194304 | tf_op jit(solution)/shard_map/band_projection/pallas_call | solution.py:29
  6.1 7.4 %all-to-all-start = ((bf16[16,144,128]{2,1,0:T(8,128)(2,1)}), bf16[16,144,128]{2,1,0:T(8,128)(2,1)S(1)}, u32[]{:S(2)}, u32[]{:S(2)}) async-start(bf16[16,144,128]{2,1,0:T(8,128)(2,1)} %band_projection.1), calls=%async_computation | async-start | bytes 1179648 | tf_op jit(solution)/shard_map/band_qkv_exchange/all_to_all | solution.py:617
  13.6 0.0 copy-start.4
  13.6 0.9 collective-permute-done.prev_ref
  14.5 3.9 %window_projection.1 = (bf16[384,512]{1,0:T(8,128)(2,1)}, bf16[384,512]{1,0:T(8,128)(2,1)}, bf16[384,512]{1,0:T(8,128)(2,1)}) custom-call(bf16[192,1024]{1,0:T(8,128)(2,1)S(1)} %collective-permute-done.prev_ref, bf16[192,1024]{1,0:T(8,128)(2,1)} %bitcast.8, bf16[1024,1024]{1,0:T(8,128)(2,1)} %wq_hbm.9, bf16[1024,1024]{1,0:T(8,128)(2,1)} %wk_hbm.9, ...), custom_call_target="tpu_custom_call" | custom-call | flops 60397977600 | bytes 4194304 | tf_op jit(solution)/shard_map/window_projection/pallas_call | solution.py:29
  18.4 8.3 %all-to-all-done.x_ref = bf16[16,144,128]{2,1,0:T(8,128)(2,1)S(1)} async-done(((bf16[16,144,128]{2,1,0:T(8,128)(2,1)}), bf16[16,144,128]{2,1,0:T(8,128)(2,1)S(1)}, u32[]{:S(2)}, u32[]{:S(2)}) %all-to-all-start) | async-done | bytes 589856 | tf_op jit(solution)/shard_map/band_qkv_exchange/all_to_all | solution.py:617
  26.6 1.9 %collective-permute-start.1 = (bf16[192,1024]{1,0:T(8,128)(2,1)S(1)}, bf16[192,1024]{1,0:T(8,128)(2,1)S(1)}, u32[]{:S(2)}, u32[]{:S(2)}) collective-permute-start(bf16[192,1024]{1,0:T(8,128)(2,1)S(1)} %bitcast.10), channel_id=1, source_target_pairs={{1,0},{2,1},{3,2},{4,3},{5,4},{6,5},{7,6},{0,7},{9,8},{10,9},{11,1... | collective-permute-start | bytes 1179656 | tf_op jit(solution)/shard_map/window_projection/ppermute | solution.py:639
  28.5 2.7 %band_forward.1 = (bf16[16,48,128]{2,1,0:T(8,128)(2,1)}, f32[3,2,512]{2,1,0:T(2,128)S(1)}) custom-call(bf16[16,144,128]{2,1,0:T(8,128)(2,1)S(1)} %all-to-all-done.x_ref), custom_call_target="tpu_custom_call" | custom-call | flops 10066329600 | bytes 1048576 | tf_op jit(solution)/shard_map/band_forward/pallas_call | solution.py:29
  31.3 3.5 %all-to-all-start.1 = ((bf16[16,48,128]{2,1,0:T(8,128)(2,1)}), bf16[16,48,128]{2,1,0:T(8,128)(2,1)S(1)}, u32[]{:S(2)}, u32[]{:S(2)}) async-start(bf16[16,48,128]{2,1,0:T(8,128)(2,1)} %get-tuple-element.35.o_ref), calls=%async_computation.1 | async-start | bytes 393216 | tf_op jit(solution)/shard_map/band_forward/all_to_all | solution.py:617
  34.8 2.6 %collective-permute-done.1.next_ref = bf16[192,1024]{1,0:T(8,128)(2,1)S(1)} collective-permute-done((bf16[192,1024]{1,0:T(8,128)(2,1)S(1)}, bf16[192,1024]{1,0:T(8,128)(2,1)S(1)}, u32[]{:S(2)}, u32[]{:S(2)}) %collective-permute-start.1) | collective-permute-done | bytes 393248 | tf_op jit(solution)/shard_map/window_projection/ppermute | solution.py:639
  37.4 6.2 %window_forward.1 = (bf16[192,512]{1,0:T(8,128)(2,1)}, f32[192,128]{1,0:T(8,128)}, bf16[192,512]{1,0:T(8,128)(2,1)}, bf16[192,512]{1,0:T(8,128)(2,1)}, bf16[192,512]{1,0:T(8,128)(2,1)}) custom-call(s32[1]{0:T(128)} %bitcast.2.pos_ref, s32[8]{0:T(128)S(1)} %copy-done.3, bf16[192,1024]{1,0:T(8,128)(2,1)S(1)} %collective-permute-done.1.next_ref, ...), custom_call_target="tpu_custom_call" | custom-call | flops 37748736000 | bytes 6291456 | tf_op jit(solution)/shard_map/window_forward/pallas_call | solution.py:29
  43.7 4.9 %middle.1 = (bf16[192,1024]{1,0:T(8,128)(2,1)}, bf16[192,1024]{1,0:T(8,128)(2,1)}, bf16[16,48,128]{2,1,0:T(8,128)(2,1)}, bf16[192,640]{1,0:T(8,128)(2,1)}, f32[8,128]{1,0:T(8,128)}) custom-call(s32[4]{0:T(128)S(1)} %copy-done.2, bf16[192,1024]{1,0:T(8,128)(2,1)} %bitcast.9, bf16[192,1024]{1,0:T(8,128)(2,1)} %bitcast.11, ...), custom_call_target="tpu_custom_call" | custom-call | flops 40265318400 | bytes 4194304 | tf_op jit(solution)/shard_map/middle/pallas_call | solution.py:29
  48.6 2.8 %collective-permute-start.4 = (f32[8,128]{1,0:T(8,128)}, f32[8,128]{1,0:T(8,128)S(1)}, u32[]{:S(2)}, u32[]{:S(2)}) collective-permute-start(f32[8,128]{1,0:T(8,128)} %get-tuple-element.39), channel_id=1, source_target_pairs={{0,3},{1,2},{2,1},{3,0},{4,7},{5,6},{6,5},{7,4},{8,11},{9,10},{10,... | collective-permute-start | bytes 12296 | tf_op jit(solution)/shard_map/middle/ppermute | solution.py:653
  51.4 0.3 collective-permute-start.3
  51.6 0.5 collective-permute-start.2
  52.2 4.6 %all-to-all-start.2 = ((bf16[16,48,128]{2,1,0:T(8,128)(2,1)}), bf16[16,48,128]{2,1,0:T(8,128)(2,1)S(1)}, u32[]{:S(2)}, u32[]{:S(2)}) async-start(bf16[16,48,128]{2,1,0:T(8,128)(2,1)} %get-tuple-element.38), calls=%async_computation.2 | async-start | bytes 393216 | tf_op jit(solution)/shard_map/middle/all_to_all | solution.py:617
  56.8 0.0 collective-permute-done.3
  56.8 0.0 collective-permute-done.2
  56.8 0.7 add_add_fusion.mine_ref
  57.5 2.1 %collective-permute-start.5 = (f32[8,128]{1,0:T(8,128)S(1)}, f32[8,128]{1,0:T(8,128)S(1)}, u32[]{:S(2)}, u32[]{:S(2)}) collective-permute-start(f32[8,128]{1,0:T(8,128)S(1)} %add_add_fusion.mine_ref), channel_id=1, source_target_pairs={{0,4},{1,5},{2,6},{3,7},{4,0},{5,1},{6,2},{7,3},{8,12},{9,13},{10,... | collective-permute-start | bytes 12296 | tf_op jit(solution)/shard_map/band_backward/ppermute | solution.py:657
  59.6 2.2 %collective-permute-start.7 = (bf16[192,640]{1,0:T(8,128)(2,1)}, bf16[192,640]{1,0:T(8,128)(2,1)S(1)}, u32[]{:S(2)}, u32[]{:S(2)}) collective-permute-start(bf16[192,640]{1,0:T(8,128)(2,1)} %get-tuple-element.40.pay_hbm), channel_id=1, source_target_pairs={{1,0},{2,1},{3,2},{4,3},{5,4},{6,5},{7,6},{0,7},{9,8},{10,9},{11,1... | collective-permute-start | bytes 737288 | tf_op jit(solution)/shard_map/middle/ppermute | solution.py:651
  61.8 0.0 collective-permute-start.6
  61.8 0.8 collective-permute-done.5.other_ref
  62.6 2.8 %all-to-all-done.2.do_ref = bf16[16,48,128]{2,1,0:T(8,128)(2,1)S(1)} async-done(((bf16[16,48,128]{2,1,0:T(8,128)(2,1)}), bf16[16,48,128]{2,1,0:T(8,128)(2,1)S(1)}, u32[]{:S(2)}, u32[]{:S(2)}) %all-to-all-start.2) | async-done | bytes 196640 | tf_op jit(solution)/shard_map/middle/all_to_all | solution.py:617
  65.4 3.2 %band_backward.1 = bf16[16,160,128]{2,1,0:T(8,128)(2,1)} custom-call(bf16[16,144,128]{2,1,0:T(8,128)(2,1)S(1)} %all-to-all-done.x_ref, bf16[16,48,128]{2,1,0:T(8,128)(2,1)S(1)} %copy-done, f32[3,2,512]{2,1,0:T(2,128)S(1)} %get-tuple-element.37.stat_ref, bf16[16,48,128]{2,1,0:T(8,128)(2,1)S(1)} %all-to-all-done.2.do_ref, f32[8,128]{1,0:T(8,128)S(1)} %add_add_fusion.mine_ref, ...), custom_call_target="tpu_custom_call" | custom-call | flops 25165824000 | bytes 2097152 | tf_op jit(solution)/shard_map/band_backward/pallas_call | solution.py:29
  68.6 4.4 %all-to-all-start.3 = ((bf16[16,160,128]{2,1,0:T(8,128)(2,1)}), bf16[16,160,128]{2,1,0:T(8,128)(2,1)S(1)}, u32[]{:S(2)}, u32[]{:S(2)}) async-start(bf16[16,160,128]{2,1,0:T(8,128)(2,1)} %band_backward.1), calls=%async_computation.3 | async-start | bytes 1310720 | tf_op jit(solution)/shard_map/band_backward/all_to_all | solution.py:617
  73.0 0.2 collective-permute-done.7.next_ref
  73.2 0.0 collective-permute-done.6.prev_ref
  73.2 11.1 %window_gradient.1.base_hbm = f32[192,1024]{1,0:T(8,128)} custom-call(s32[1]{0:T(128)} %bitcast.2.pos_ref, s32[8]{0:T(128)S(1)} %copy-done.3, bf16[192,640]{1,0:T(8,128)(2,1)S(1)} %collective-permute-done.6.prev_ref, bf16[192,640]{1,0:T(8,128)(2,1)S(1)} %collective-permute-done.7.next_ref, bf16[384,512]{1,0:T(8,128)(2,1)} %get-tuple-element.29.q_hbm, ...), custom_call_target="tpu_custom_call" | custom-call | flops 53791948800 | bytes 8388608 | tf_op jit(solution)/shard_map/window_gradient/pallas_call | solution.py:29
  84.3 2.5 %all-to-all-done.3.x_ref = bf16[16,160,128]{2,1,0:T(8,128)(2,1)S(1)} async-done(((bf16[16,160,128]{2,1,0:T(8,128)(2,1)}), bf16[16,160,128]{2,1,0:T(8,128)(2,1)S(1)}, u32[]{:S(2)}, u32[]{:S(2)}) %all-to-all-start.3) | async-done | bytes 655392 | tf_op jit(solution)/shard_map/band_backward/all_to_all | solution.py:617
  86.8 4.1 %token_gradient.1 = (f32[192,1024]{1,0:T(8,128)}, f32[1,1]{1,0:T(1,128)}) custom-call(bf16[16,160,128]{2,1,0:T(8,128)(2,1)S(1)} %all-to-all-done.3.x_ref, f32[192,1024]{1,0:T(8,128)} %window_gradient.1.base_hbm, bf16[1024,1024]{1,0:T(8,128)(2,1)} %wq_hbm.9, bf16[1024,1024]{1,0:T(8,128)(2,1)} %wk_hbm.9, bf16[1024,1024]{1,0:T(8,128)(2,1)} %wv_hbm.9), custom_call_target="tpu_custom_call" | custom-call | flops 30198988800 | bytes 5242880 | tf_op jit(solution)/shard_map/token_gradient/pallas_call | solution.py:29
  (11 shorter events, 0.0 us)
Async XLA Ops:
  0.6 13.8 %collective-permute-start = (bf16[192,1024]{1,0:T(8,128)(2,1)}, bf16[192,1024]{1,0:T(8,128)(2,1)S(1)}, u32[]{:S(2)}, u32[]{:S(2)}) collective-permute-start(bf16[192,1024]{1,0:T(8,128)(2,1)} %bitcast.6), channel_id=1, source_target_pairs={{0,1},{1,2},{2,3},{3,4},{4,5},{5,6},{6,7},{7,0},{8,9},{9,10},{10,1... | collective-permute-start | bytes 1179656 | tf_op jit(solution)/shard_map/halo_tokens/ppermute | solution.py:633
  6.1 20.5 %all-to-all-start = ((bf16[16,144,128]{2,1,0:T(8,128)(2,1)}), bf16[16,144,128]{2,1,0:T(8,128)(2,1)S(1)}, u32[]{:S(2)}, u32[]{:S(2)}) async-start(bf16[16,144,128]{2,1,0:T(8,128)(2,1)} %band_projection.1), calls=%async_computation | async-start | bytes 1179648 | tf_op jit(solution)/shard_map/band_qkv_exchange/all_to_all | solution.py:617
  13.6 13.1 %copy-start.4 = (bf16[3,2,32,1024]{3,2,1,0:T(8,128)(2,1)S(1)}, bf16[3,2,32,1024]{3,2,1,0:T(8,128)(2,1)}, u32[]{:S(2)}) copy-start(bf16[3,2,32,1024]{3,2,1,0:T(8,128)(2,1)} %param.8) | copy-start | bytes 1179652
  26.6 10.8 %copy-start.3 = (s32[8]{0:T(128)S(1)}, s32[8]{0:T(128)}, u32[]{:S(2)}) copy-start(s32[8]{0:T(128)} %reach_ref.3) | copy-start | bytes 100
  26.6 10.8 %collective-permute-start.1 = (bf16[192,1024]{1,0:T(8,128)(2,1)S(1)}, bf16[192,1024]{1,0:T(8,128)(2,1)S(1)}, u32[]{:S(2)}, u32[]{:S(2)}) collective-permute-start(bf16[192,1024]{1,0:T(8,128)(2,1)S(1)} %bitcast.10), channel_id=1, source_target_pairs={{1,0},{2,1},{3,2},{4,3},{5,4},{6,5},{7,6},{0,7},{9,8},{10,9},{11,1... | collective-permute-start | bytes 1179656 | tf_op jit(solution)/shard_map/window_projection/ppermute | solution.py:639
  31.3 12.3 %all-to-all-start.1 = ((bf16[16,48,128]{2,1,0:T(8,128)(2,1)}), bf16[16,48,128]{2,1,0:T(8,128)(2,1)S(1)}, u32[]{:S(2)}, u32[]{:S(2)}) async-start(bf16[16,48,128]{2,1,0:T(8,128)(2,1)} %get-tuple-element.35.o_ref), calls=%async_computation.1 | async-start | bytes 393216 | tf_op jit(solution)/shard_map/band_forward/all_to_all | solution.py:617
  37.4 6.2 %copy-start.1 = (bf16[1024,1024]{1,0:T(8,128)(2,1)S(1)}, bf16[1024,1024]{1,0:T(8,128)(2,1)}, u32[]{:S(2)}) copy-start(bf16[1024,1024]{1,0:T(8,128)(2,1)} %wo_ref.1) | copy-start | bytes 6291460
  37.4 6.2 %copy-start.2 = (s32[4]{0:T(128)S(1)}, s32[4]{0:T(128)}, u32[]{:S(2)}) copy-start(s32[4]{0:T(128)} %table_ref.1) | copy-start | bytes 52
  43.6 21.7 %copy-start = (bf16[16,48,128]{2,1,0:T(8,128)(2,1)S(1)}, bf16[16,48,128]{2,1,0:T(8,128)(2,1)}, u32[]{:S(2)}) copy-start(bf16[16,48,128]{2,1,0:T(8,128)(2,1)} %get-tuple-element.35.o_ref) | copy-start | bytes 589828
  48.6 8.2 %collective-permute-start.4 = (f32[8,128]{1,0:T(8,128)}, f32[8,128]{1,0:T(8,128)S(1)}, u32[]{:S(2)}, u32[]{:S(2)}) collective-permute-start(f32[8,128]{1,0:T(8,128)} %get-tuple-element.39), channel_id=1, source_target_pairs={{0,3},{1,2},{2,1},{3,0},{4,7},{5,6},{6,5},{7,4},{8,11},{9,10},{10,... | collective-permute-start | bytes 12296 | tf_op jit(solution)/shard_map/middle/ppermute | solution.py:653
  51.4 5.4 %collective-permute-start.3 = (f32[8,128]{1,0:T(8,128)}, f32[8,128]{1,0:T(8,128)S(1)}, u32[]{:S(2)}, u32[]{:S(2)}) collective-permute-start(f32[8,128]{1,0:T(8,128)} %get-tuple-element.39), channel_id=1, source_target_pairs={{0,2},{1,3},{2,0},{3,1},{4,6},{5,7},{6,4},{7,5},{8,10},{9,11},{10,... | collective-permute-start | bytes 12296 | tf_op jit(solution)/shard_map/middle/ppermute | solution.py:653
  51.6 5.1 %collective-permute-start.2 = (f32[8,128]{1,0:T(8,128)}, f32[8,128]{1,0:T(8,128)S(1)}, u32[]{:S(2)}, u32[]{:S(2)}) collective-permute-start(f32[8,128]{1,0:T(8,128)} %get-tuple-element.39), channel_id=1, source_target_pairs={{0,1},{1,0},{2,3},{3,2},{4,5},{5,4},{6,7},{7,6},{8,9},{9,8},{10,11... | collective-permute-start | bytes 12296 | tf_op jit(solution)/shard_map/middle/ppermute | solution.py:653
  52.2 13.2 %all-to-all-start.2 = ((bf16[16,48,128]{2,1,0:T(8,128)(2,1)}), bf16[16,48,128]{2,1,0:T(8,128)(2,1)S(1)}, u32[]{:S(2)}, u32[]{:S(2)}) async-start(bf16[16,48,128]{2,1,0:T(8,128)(2,1)} %get-tuple-element.38), calls=%async_computation.2 | async-start | bytes 393216 | tf_op jit(solution)/shard_map/middle/all_to_all | solution.py:617
  57.5 5.1 %collective-permute-start.5 = (f32[8,128]{1,0:T(8,128)S(1)}, f32[8,128]{1,0:T(8,128)S(1)}, u32[]{:S(2)}, u32[]{:S(2)}) collective-permute-start(f32[8,128]{1,0:T(8,128)S(1)} %add_add_fusion.mine_ref), channel_id=1, source_target_pairs={{0,4},{1,5},{2,6},{3,7},{4,0},{5,1},{6,2},{7,3},{8,12},{9,13},{10,... | collective-permute-start | bytes 12296 | tf_op jit(solution)/shard_map/band_backward/ppermute | solution.py:657
  59.6 13.6 %collective-permute-start.7 = (bf16[192,640]{1,0:T(8,128)(2,1)}, bf16[192,640]{1,0:T(8,128)(2,1)S(1)}, u32[]{:S(2)}, u32[]{:S(2)}) collective-permute-start(bf16[192,640]{1,0:T(8,128)(2,1)} %get-tuple-element.40.pay_hbm), channel_id=1, source_target_pairs={{1,0},{2,1},{3,2},{4,3},{5,4},{6,5},{7,6},{0,7},{9,8},{10,9},{11,1... | collective-permute-start | bytes 737288 | tf_op jit(solution)/shard_map/middle/ppermute | solution.py:651
  61.8 11.4 %collective-permute-start.6 = (bf16[192,640]{1,0:T(8,128)(2,1)}, bf16[192,640]{1,0:T(8,128)(2,1)S(1)}, u32[]{:S(2)}, u32[]{:S(2)}) collective-permute-start(bf16[192,640]{1,0:T(8,128)(2,1)} %get-tuple-element.40.pay_hbm), channel_id=1, source_target_pairs={{0,1},{1,2},{2,3},{3,4},{4,5},{5,6},{6,7},{7,0},{8,9},{9,10},{10,1... | collective-permute-start | bytes 737288 | tf_op jit(solution)/shard_map/middle/ppermute | solution.py:650
  68.6 18.2 %all-to-all-start.3 = ((bf16[16,160,128]{2,1,0:T(8,128)(2,1)}), bf16[16,160,128]{2,1,0:T(8,128)(2,1)S(1)}, u32[]{:S(2)}, u32[]{:S(2)}) async-start(bf16[16,160,128]{2,1,0:T(8,128)(2,1)} %band_backward.1), calls=%async_computation.3 | async-start | bytes 1310720 | tf_op jit(solution)/shard_map/band_backward/all_to_all | solution.py:617

commit v5 on v4

--- a/solution.py
+++ b/solution.py
@@ -174,7 +174,7 @@
     )
 
 
-def band_bwd_kernel(x_ref, o_ref, stat_ref, do_ref, mine_ref, other_ref, out_ref):
+def band_bwd_kernel(x_ref, o_ref, stat_ref, do_ref, mine_ref, other_ref, out_hbm, out_ref, sems):
     total = jnp.broadcast_to(mine_ref[0:1, :] + other_ref[0:1, :], (16, 128))
     high = total.astype(BF).astype(F32)
     mid = (total - high).astype(BF).astype(F32)
@@ -184,6 +184,8 @@
     parts = parts.astype(BF)
     for j in range(N_LON):
         out_ref[j, 144:160, :] = parts
+    rows = pl.ds(144, 16)
+    stores = begin([(out_ref.at[:, rows], out_hbm.at[:, rows])], sems.at[pl.ds(3, 1)])
     for l in range(LEVELS):
         q, k, v = unpack_qkv(x_ref[:, 48 * l : 48 * l + 48, :])
         o = unpack_one(o_ref[:, 16 * l : 16 * l + 16, :])
@@ -201,15 +203,20 @@
             N_LON, 32, 128
         )
         out_ref[:, 48 * l + 32 : 48 * l + 48, :] = pack_one(dv)
+        rows = pl.ds(48 * l, 48)
+        stores += begin([(out_ref.at[:, rows], out_hbm.at[:, rows])], sems.at[pl.ds(l, 1)])
+    for store in stores:
+        store.wait()
 
 
 def band_bwd(x, o, stat, do, mine, other):
     return call(
         band_bwd_kernel,
-        [out_block((N_LON, 160, 128), BF)],
+        [out_hbm((N_LON, 160, 128), BF)],
         30 * 512 * 512 * 64,
         2 * 1024 * 1024,
         [in_vmem(y) for y in (x, o, stat, do, mine, other)],
+        [pltpu.VMEM((N_LON, 160, 128), BF), pltpu.SemaphoreType.DMA((4,))],
     )[0]
 
 
@@ -280,8 +287,8 @@
 
 def win_fwd_kernel(
     pos_ref, reach_ref, next_ref, wk_hbm, wv_hbm, wq_hbm, q_hbm, k_hbm, v_hbm,
-    o_ref, stat_ref, hq_ref, hk_ref, hv_ref,
-    wk_ref, wv_ref, wq_ref, q_ref, k_ref, v_ref, sems,
+    o_ref, stat_ref, hq_hbm, hk_hbm, hv_hbm,
+    hq_ref, hk_ref, hv_ref, wk_ref, wv_ref, wq_ref, q_ref, k_ref, v_ref, sems, out_sems,
 ):
     lanes = pl.ds(BAND, BAND)
     copies = begin(
@@ -295,7 +302,7 @@
         ],
         sems,
     )
-    dist = window_distance(pos_ref[0])
+    dist = window_distance(pos_ref[0:1, 0:1])
     near = to_halves(next_ref[...])
     copies[0].wait()
     hk_ref[...] = dot(near, wk_ref[...]).astype(BF)
@@ -303,6 +310,7 @@
     hv_ref[...] = dot(near, wv_ref[...]).astype(BF)
     copies[2].wait()
     hq_ref[...] = dot(near, wq_ref[...]).astype(BF)
+    stores = begin([(hk_ref, hk_hbm), (hv_ref, hv_hbm), (hq_ref, hq_hbm)], out_sems)
     for copy in copies[3:6]:
         copy.wait()
     for half in range(2):
@@ -316,7 +324,7 @@
         for h in range(HALF):
             lanes = slice(64 * h, 64 * h + 64)
             s = dot_nt(k[:, lanes], q[:, lanes]) * (SCALE * LOG2E)
-            s = jnp.where(dist <= reach_ref[h], s, NEG)
+            s = jnp.where(dist <= reach_ref[h : h + 1, 0:1], s, NEG)
             top = jnp.max(s, axis=0, keepdims=True)
             e = jnp.exp2(s - top)
             rtot = 1.0 / jnp.sum(e, axis=0, keepdims=True)
@@ -327,6 +335,8 @@
         o_ref[rows] = tr(jnp.concatenate(outs, axis=0)).astype(BF)
         stats = jnp.concatenate(tops + rtots + [jnp.zeros((112, 96), F32)], axis=0)
         stat_ref[rows] = tr(stats)
+    for store in stores:
+        store.wait()
 
 def win_fwd(pos, reach, q, k, v, nxt, wq, wk, wv):
     return call(
@@ -334,18 +344,19 @@
         [
             out_block((TOK, BAND), BF),
             out_block((TOK, 128), F32),
-            out_block((TOK, BAND), BF),
-            out_block((TOK, BAND), BF),
-            out_block((TOK, BAND), BF),
+            out_hbm((TOK, BAND), BF),
+            out_hbm((TOK, BAND), BF),
+            out_hbm((TOK, BAND), BF),
         ],
         64 * 288 * 128 * 64 + 6 * TOK * WIDTH * BAND,
         6 * 1024 * 1024,
-        [in_smem(pos), in_smem(reach)]
+        [in_vmem(pos), in_vmem(reach)]
         + [in_vmem(nxt)]
         + [in_hbm(x) for x in (wk, wv, wq, q, k, v)],
-        [WEIGHT_HALF] * 3
+        [pltpu.VMEM((TOK, BAND), BF)] * 3
+        + [WEIGHT_HALF] * 3
         + [pltpu.VMEM((2 * TOK, BAND), BF)] * 3
-        + [pltpu.SemaphoreType.DMA((6,))],
+        + [pltpu.SemaphoreType.DMA((6,)), pltpu.SemaphoreType.DMA((3,))],
     )
 
 
@@ -388,8 +399,8 @@
         ],
         sems,
     )
-    dist = window_distance(pos_ref[0])
-    near_dist = neighbour_distance(pos_ref[0])
+    dist = window_distance(pos_ref[0:1, 0:1])
+    near_dist = neighbour_distance(pos_ref[0:1, 0:1])
     for copy in copies[:7]:
         copy.wait()
     for half in range(2):
@@ -414,14 +425,14 @@
                 qh, kh, vh, doh = q[:, lanes], k[:, lanes], v[:, lanes], do[:, lanes]
                 s = dot_nt(kh, qh) * (SCALE * LOG2E)
                 e = jnp.exp2(s - stat[h : h + 1])
-                p = jnp.where(dist <= reach_ref[h], e * stat[8 + h : 9 + h], 0.0)
+                p = jnp.where(dist <= reach_ref[h : h + 1, 0:1], e * stat[8 + h : 9 + h], 0.0)
                 dp = dot_nt(vh, doh)
                 ds = (p * (dp - stat[16 + h : 17 + h]) * SCALE).astype(BF)
                 dqs.append(dot(kt[lanes], ds))
                 qn, don = near_q[:, lanes], near_do[:, lanes]
                 s = dot_nt(kh[0:96], qn) * (SCALE * LOG2E)
                 e = jnp.exp2(s - near_stat[h : h + 1])
-                pn = jnp.where(near_dist <= reach_ref[h], e * near_stat[8 + h : 9 + h], 0.0)
+                pn = jnp.where(near_dist <= reach_ref[h : h + 1, 0:1], e * near_stat[8 + h : 9 + h], 0.0)
                 dp = dot_nt(vh[0:96], don)
                 dsn = (pn * (dp - near_stat[16 + h : 17 + h]) * SCALE).astype(BF)
                 dvs.append(dot(p[0:96].astype(BF), doh) + dot(pn.astype(BF), don))
@@ -443,7 +454,7 @@
         [out_block((TOK, WIDTH), F32)],
         6 * TOK * WIDTH * BAND + 200 * 288 * 128 * 64,
         8 * 1024 * 1024,
-        [in_smem(pos), in_smem(reach)]
+        [in_vmem(pos), in_vmem(reach)]
         + [in_vmem(prev), in_vmem(nxt)]
         + [in_hbm(x) for x in (q, k, v, hk, hv, pay, hq, dm, wq, wk, wv)],
         [pltpu.VMEM((2 * TOK, BAND), BF)] * 3
@@ -491,7 +502,7 @@
         mixed = (tok_ref[:, lanes].astype(F32) + dot(att, wo_ref[:, lanes])).astype(BF)
         mixed_ref[:, lanes] = mixed
         diff = mixed.astype(F32) - tgt_ref[:, lanes].astype(F32)
-        weighted = (table_ref[g].astype(F32) * 0.25) * diff
+        weighted = (table_ref[g : g + 1, 0:1].astype(F32) * 0.25) * diff
         total = total + jnp.sum((weighted * diff).reshape(TOK // 8, 8, 256), axis=0)
         dm = weighted.astype(BF)
         dm_ref[:, lanes] = dm
@@ -537,7 +548,7 @@
         ],
         4 * TOK * WIDTH * WIDTH,
         4 * 1024 * 1024,
-        [in_smem(table)]
+        [in_vmem(table)]
         + [in_hbm(x) for x in (tok, tgt, win, stat)]
         + [in_vmem(x) for x in (wo, o)],
         [pltpu.VMEM((TOK, WIDTH), BF)] * 2
@@ -626,7 +637,9 @@
     count = levels * rows * cols
     tok = tokens.reshape(count, width)
     tgt = targets.reshape(count, width)
-    pos = lax.axis_index("lat").astype(jnp.int32).reshape(1)
+    pos = jnp.broadcast_to(lax.axis_index("lat").astype(jnp.int32), (8, 128))
+    window_reach = jnp.broadcast_to(window_reach[:, None], (8, 128))
+    loss_table = jnp.broadcast_to(jnp.tile(loss_table, 2)[:, None], (8, 128))
     with jax.named_scope("band_projection"):
         sent = band_proj(tok, w_query, w_key, w_value)
     with jax.named_scope("halo_tokens"):
@@ -647,8 +660,8 @@
     with jax.named_scope("middle"):
         mixed, dm, dsend, pay, part = mid(loss_table, tok, tgt, o_back, win, wstat, w_out)
         do = swap(dsend)
+        pay_next = lax.ppermute(pay, "lat", DOWN)
         pay_prev = lax.ppermute(pay, "lat", UP)
-        pay_next = lax.ppermute(pay, "lat", DOWN)
         losses = [part] + [
             lax.ppermute(part, "lat", [(i, i ^ step) for i in range(N_LAT)]) for step in (1, 2, 3)
         ]

time: 92.1 us -> 91.3 us (level)
  Pallas kernels: 39.5 us -> 38.1 us
    pallas_call x8, Pallas kernels: 39.5 us -> 38.1 us  [call(): pl.pallas_call(kernel, grid=(1,), in_specs=[spec for spec, _ in ins], out...]
  transfers between devices with their start and end apart: 12 -> 12, of which waited for: 7 -> 8; matrix products, arithmetic and copies ran while one was open for 1% -> 1% of each run, Pallas kernels for 34% -> 33%
where the time goes in v5:
time: 91.3 us; the launch traced here: 90.2 us
  Pallas kernels  38.1 us (42%)
  starting transfers between devices  31.8 us (35%)
  waiting for transfers between devices  18.5 us (20%)
  between operations  0.94 us (1%)
    pallas_call x8, Pallas kernels, call(): pl.pallas_call(kernel, grid=(1,), in_specs=[spec for spec, _ in ins], out...  38.1 us
    all_to_all x4, starting transfers between devices, swap(): return lax.all_to_all(x, 'lon', 0, 0, tiled=True)  19.9 us
    all_to_all x4, waiting for transfers between devices, swap(): return lax.all_to_all(x, 'lon', 0, 0, tiled=True)  14 us
    ppermute x3, starting transfers between devices, per_device(): lax.ppermute(part, 'lat', [(i, i ^ step) for i in range(N_LAT)])  3.57 us
    ppermute x1, waiting for transfers between devices, per_device(): nxt = lax.ppermute(tok_later, 'lat', DOWN)  2.6 us
    ppermute x1, starting transfers between devices, per_device(): pay_next = lax.ppermute(pay, 'lat', DOWN)  2.2 us
    ppermute x1, starting transfers between devices, per_device(): far = lax.ppermute(four, 'lat', [(i, i ^ 4) for i in range(N_LAT)])  2.11 us
    ppermute x1, starting transfers between devices, per_device(): prev = lax.ppermute(tok, 'lat', UP)  2.07 us
  transfers between devices with their start and end apart: 12, of which 8 were waited for; matrix products, arithmetic and copies ran while one was open for 1% of the time, Pallas kernels for 33%

profile of v5, /device:TPU:0, one launch (start us, length us, event | category | flops | bytes accessed | tf_op | source)
XLA Modules:
  0.0 90.2 jit_solution(70956726137366240)
XLA Ops:
  0.6 2.1 %collective-permute-start = (bf16[192,1024]{1,0:T(8,128)(2,1)}, bf16[192,1024]{1,0:T(8,128)(2,1)S(1)}, u32[]{:S(2)}, u32[]{:S(2)}) collective-permute-start(bf16[192,1024]{1,0:T(8,128)(2,1)} %bitcast.5), channel_id=1, source_target_pairs={{0,1},{1,2},{2,3},{3,4},{4,5},{5,6},{6,7},{7,0},{8,9},{9,10},{10,1... | collective-permute-start | bytes 1179656 | tf_op jit(solution)/shard_map/halo_tokens/ppermute | solution.py:646
  2.7 3.4 %band_projection.1 = bf16[16,144,128]{2,1,0:T(8,128)(2,1)} custom-call(bf16[192,1024]{1,0:T(8,128)(2,1)} %bitcast.6, bf16[1024,1024]{1,0:T(8,128)(2,1)} %wq_hbm.9, bf16[1024,1024]{1,0:T(8,128)(2,1)} %wk_hbm.9, bf16[1024,1024]{1,0:T(8,128)(2,1)} %wv_hbm.9), custom_call_target="tpu_custom_call" | custom-call | flops 30198988800 | bytes 4194304 | tf_op jit(solution)/shard_map/band_projection/pallas_call | solution.py:29
  6.1 7.4 %all-to-all-start = ((bf16[16,144,128]{2,1,0:T(8,128)(2,1)}), bf16[16,144,128]{2,1,0:T(8,128)(2,1)S(1)}, u32[]{:S(2)}, u32[]{:S(2)}) async-start(bf16[16,144,128]{2,1,0:T(8,128)(2,1)} %band_projection.1), calls=%async_computation | async-start | bytes 1179648 | tf_op jit(solution)/shard_map/band_qkv_exchange/all_to_all | solution.py:628
  13.6 0.1 broadcast_in_dim.16
  13.7 0.8 collective-permute-done.prev_ref
  14.5 3.9 %window_projection.1 = (bf16[384,512]{1,0:T(8,128)(2,1)}, bf16[384,512]{1,0:T(8,128)(2,1)}, bf16[384,512]{1,0:T(8,128)(2,1)}) custom-call(bf16[192,1024]{1,0:T(8,128)(2,1)S(1)} %collective-permute-done.prev_ref, bf16[192,1024]{1,0:T(8,128)(2,1)} %bitcast.7, bf16[1024,1024]{1,0:T(8,128)(2,1)} %wq_hbm.9, bf16[1024,1024]{1,0:T(8,128)(2,1)} %wk_hbm.9, ...), custom_call_target="tpu_custom_call" | custom-call | flops 60397977600 | bytes 4194304 | tf_op jit(solution)/shard_map/window_projection/pallas_call | solution.py:29
  18.4 8.3 %all-to-all-done.x_ref = bf16[16,144,128]{2,1,0:T(8,128)(2,1)S(1)} async-done(((bf16[16,144,128]{2,1,0:T(8,128)(2,1)}), bf16[16,144,128]{2,1,0:T(8,128)(2,1)S(1)}, u32[]{:S(2)}, u32[]{:S(2)}) %all-to-all-start) | async-done | bytes 589856 | tf_op jit(solution)/shard_map/band_qkv_exchange/all_to_all | solution.py:628
  26.6 1.9 %collective-permute-start.1 = (bf16[192,1024]{1,0:T(8,128)(2,1)S(1)}, bf16[192,1024]{1,0:T(8,128)(2,1)S(1)}, u32[]{:S(2)}, u32[]{:S(2)}) collective-permute-start(bf16[192,1024]{1,0:T(8,128)(2,1)S(1)} %bitcast.9), channel_id=1, source_target_pairs={{1,0},{2,1},{3,2},{4,3},{5,4},{6,5},{7,6},{0,7},{9,8},{10,9},{11,1... | collective-permute-start | bytes 1179656 | tf_op jit(solution)/shard_map/window_projection/ppermute | solution.py:652
  28.5 2.7 %band_forward.1 = (bf16[16,48,128]{2,1,0:T(8,128)(2,1)}, f32[3,2,512]{2,1,0:T(2,128)S(1)}) custom-call(bf16[16,144,128]{2,1,0:T(8,128)(2,1)S(1)} %all-to-all-done.x_ref), custom_call_target="tpu_custom_call" | custom-call | flops 10066329600 | bytes 1048576 | tf_op jit(solution)/shard_map/band_forward/pallas_call | solution.py:29
  31.3 3.5 %all-to-all-start.1 = ((bf16[16,48,128]{2,1,0:T(8,128)(2,1)}), bf16[16,48,128]{2,1,0:T(8,128)(2,1)S(1)}, u32[]{:S(2)}, u32[]{:S(2)}) async-start(bf16[16,48,128]{2,1,0:T(8,128)(2,1)} %get-tuple-element.35.o_ref), calls=%async_computation.1 | async-start | bytes 393216 | tf_op jit(solution)/shard_map/band_forward/all_to_all | solution.py:628
  34.8 2.6 %collective-permute-done.1.next_ref = bf16[192,1024]{1,0:T(8,128)(2,1)S(1)} collective-permute-done((bf16[192,1024]{1,0:T(8,128)(2,1)S(1)}, bf16[192,1024]{1,0:T(8,128)(2,1)S(1)}, u32[]{:S(2)}, u32[]{:S(2)}) %collective-permute-start.1) | collective-permute-done | bytes 393248 | tf_op jit(solution)/shard_map/window_projection/ppermute | solution.py:652
  37.4 0.1 broadcast_in_dim.19.reach_ref
  37.5 5.8 %window_forward.1 = (bf16[192,512]{1,0:T(8,128)(2,1)}, f32[192,128]{1,0:T(8,128)}, bf16[192,512]{1,0:T(8,128)(2,1)}, bf16[192,512]{1,0:T(8,128)(2,1)}, bf16[192,512]{1,0:T(8,128)(2,1)}) custom-call(s32[8,128]{1,0:T(8,128)S(1)} %broadcast_in_dim.18.pos_ref, s32[8,128]{1,0:T(8,128)S(1)} %broadcast_in_dim.19.reach_ref, ...), custom_call_target="tpu_custom_call" | custom-call | flops 37748736000 | bytes 6291456 | tf_op jit(solution)/shard_map/window_forward/pallas_call | solution.py:29
  43.3 0.1 all-to-all-done.1.o_ref
  43.4 0.1 broadcast_in_dim.17.table_ref
  43.5 4.5 %middle.1 = (bf16[192,1024]{1,0:T(8,128)(2,1)}, bf16[192,1024]{1,0:T(8,128)(2,1)}, bf16[16,48,128]{2,1,0:T(8,128)(2,1)}, bf16[192,640]{1,0:T(8,128)(2,1)}, f32[8,128]{1,0:T(8,128)}) custom-call(s32[8,128]{1,0:T(8,128)S(1)} %broadcast_in_dim.17.table_ref, bf16[192,1024]{1,0:T(8,128)(2,1)} %bitcast.8, bf16[192,1024]{1,0:T(8,128)(2,1)} %bitcast.10, ...), custom_call_target="tpu_custom_call" | custom-call | flops 40265318400 | bytes 4194304 | tf_op jit(solution)/shard_map/middle/pallas_call | solution.py:29
  47.9 2.7 %collective-permute-start.4 = (f32[8,128]{1,0:T(8,128)}, f32[8,128]{1,0:T(8,128)S(1)}, u32[]{:S(2)}, u32[]{:S(2)}) collective-permute-start(f32[8,128]{1,0:T(8,128)} %get-tuple-element.39), channel_id=1, source_target_pairs={{0,3},{1,2},{2,1},{3,0},{4,7},{5,6},{6,5},{7,4},{8,11},{9,10},{10,... | collective-permute-start | bytes 12296 | tf_op jit(solution)/shard_map/middle/ppermute | solution.py:666
  50.7 0.3 collective-permute-start.3
  50.9 0.6 collective-permute-start.2
  51.5 4.5 %all-to-all-start.2 = ((bf16[16,48,128]{2,1,0:T(8,128)(2,1)}), bf16[16,48,128]{2,1,0:T(8,128)(2,1)S(1)}, u32[]{:S(2)}, u32[]{:S(2)}) async-start(bf16[16,48,128]{2,1,0:T(8,128)(2,1)} %get-tuple-element.38), calls=%async_computation.2 | async-start | bytes 393216 | tf_op jit(solution)/shard_map/middle/all_to_all | solution.py:628
  56.1 0.7 add_add_fusion.mine_ref
  56.8 2.1 %collective-permute-start.5 = (f32[8,128]{1,0:T(8,128)S(1)}, f32[8,128]{1,0:T(8,128)S(1)}, u32[]{:S(2)}, u32[]{:S(2)}) collective-permute-start(f32[8,128]{1,0:T(8,128)S(1)} %add_add_fusion.mine_ref), channel_id=1, source_target_pairs={{0,4},{1,5},{2,6},{3,7},{4,0},{5,1},{6,2},{7,3},{8,12},{9,13},{10,... | collective-permute-start | bytes 12296 | tf_op jit(solution)/shard_map/band_backward/ppermute | solution.py:670
  58.9 2.2 %collective-permute-start.7 = (bf16[192,640]{1,0:T(8,128)(2,1)}, bf16[192,640]{1,0:T(8,128)(2,1)S(1)}, u32[]{:S(2)}, u32[]{:S(2)}) collective-permute-start(bf16[192,640]{1,0:T(8,128)(2,1)} %get-tuple-element.40.pay_hbm), channel_id=1, source_target_pairs={{1,0},{2,1},{3,2},{4,3},{5,4},{6,5},{7,6},{0,7},{9,8},{10,9},{11,1... | collective-permute-start | bytes 737288 | tf_op jit(solution)/shard_map/middle/ppermute | solution.py:663
  61.1 0.0 collective-permute-start.6
  61.1 0.8 collective-permute-done.5.other_ref
  61.9 2.8 %all-to-all-done.2.do_ref = bf16[16,48,128]{2,1,0:T(8,128)(2,1)S(1)} async-done(((bf16[16,48,128]{2,1,0:T(8,128)(2,1)}), bf16[16,48,128]{2,1,0:T(8,128)(2,1)S(1)}, u32[]{:S(2)}, u32[]{:S(2)}) %all-to-all-start.2) | async-done | bytes 196640 | tf_op jit(solution)/shard_map/middle/all_to_all | solution.py:628
  64.7 3.1 %band_backward.1 = bf16[16,160,128]{2,1,0:T(8,128)(2,1)} custom-call(bf16[16,144,128]{2,1,0:T(8,128)(2,1)S(1)} %all-to-all-done.x_ref, bf16[16,48,128]{2,1,0:T(8,128)(2,1)S(1)} %copy-done, f32[3,2,512]{2,1,0:T(2,128)S(1)} %get-tuple-element.37.stat_ref, bf16[16,48,128]{2,1,0:T(8,128)(2,1)S(1)} %all-to-all-done.2.do_ref, f32[8,128]{1,0:T(8,128)S(1)} %add_add_fusion.mine_ref, ...), custom_call_target="tpu_custom_call" | custom-call | flops 25165824000 | bytes 2097152 | tf_op jit(solution)/shard_map/band_backward/pallas_call | solution.py:29
  67.8 4.4 %all-to-all-start.3 = ((bf16[16,160,128]{2,1,0:T(8,128)(2,1)}), bf16[16,160,128]{2,1,0:T(8,128)(2,1)S(1)}, u32[]{:S(2)}, u32[]{:S(2)}) async-start(bf16[16,160,128]{2,1,0:T(8,128)(2,1)} %band_backward.1), calls=%async_computation.3 | async-start | bytes 1310720 | tf_op jit(solution)/shard_map/band_backward/all_to_all | solution.py:628
  72.2 0.2 collective-permute-done.7.next_ref
  72.5 10.6 %window_gradient.1.base_hbm = f32[192,1024]{1,0:T(8,128)} custom-call(s32[8,128]{1,0:T(8,128)S(1)} %broadcast_in_dim.18.pos_ref, s32[8,128]{1,0:T(8,128)S(1)} %broadcast_in_dim.19.reach_ref, bf16[192,640]{1,0:T(8,128)(2,1)S(1)} %collective-permute-done.6.prev_ref, bf16[192,640]{1,0:T(8,128)(2,1)S(1)} %collective-permute-done.7.next_ref, ...), custom_call_target="tpu_custom_call" | custom-call | flops 53791948800 | bytes 8388608 | tf_op jit(solution)/shard_map/window_gradient/pallas_call | solution.py:29
  83.1 2.9 %all-to-all-done.3.x_ref = bf16[16,160,128]{2,1,0:T(8,128)(2,1)S(1)} async-done(((bf16[16,160,128]{2,1,0:T(8,128)(2,1)}), bf16[16,160,128]{2,1,0:T(8,128)(2,1)S(1)}, u32[]{:S(2)}, u32[]{:S(2)}) %all-to-all-start.3) | async-done | bytes 655392 | tf_op jit(solution)/shard_map/band_backward/all_to_all | solution.py:628
  86.0 4.1 %token_gradient.1 = (f32[192,1024]{1,0:T(8,128)}, f32[1,1]{1,0:T(1,128)}) custom-call(bf16[16,160,128]{2,1,0:T(8,128)(2,1)S(1)} %all-to-all-done.3.x_ref, f32[192,1024]{1,0:T(8,128)} %window_gradient.1.base_hbm, bf16[1024,1024]{1,0:T(8,128)(2,1)} %wq_hbm.9, bf16[1024,1024]{1,0:T(8,128)(2,1)} %wk_hbm.9, bf16[1024,1024]{1,0:T(8,128)(2,1)} %wv_hbm.9), custom_call_target="tpu_custom_call" | custom-call | flops 30198988800 | bytes 5242880 | tf_op jit(solution)/shard_map/token_gradient/pallas_call | solution.py:29
  (16 shorter events, 0.0 us)
Async XLA Ops:
  0.6 12.9 %copy-start.4 = (s32[4]{0:T(128)S(1)}, s32[4]{0:T(128)}, u32[]{:S(2)}) copy-start(s32[4]{0:T(128)} %param.15) | copy-start | bytes 52
  0.6 13.8 %collective-permute-start = (bf16[192,1024]{1,0:T(8,128)(2,1)}, bf16[192,1024]{1,0:T(8,128)(2,1)S(1)}, u32[]{:S(2)}, u32[]{:S(2)}) collective-permute-start(bf16[192,1024]{1,0:T(8,128)(2,1)} %bitcast.5), channel_id=1, source_target_pairs={{0,1},{1,2},{2,3},{3,4},{4,5},{5,6},{6,7},{7,0},{8,9},{9,10},{10,1... | collective-permute-start | bytes 1179656 | tf_op jit(solution)/shard_map/halo_tokens/ppermute | solution.py:646
  6.1 20.5 %all-to-all-start = ((bf16[16,144,128]{2,1,0:T(8,128)(2,1)}), bf16[16,144,128]{2,1,0:T(8,128)(2,1)S(1)}, u32[]{:S(2)}, u32[]{:S(2)}) async-start(bf16[16,144,128]{2,1,0:T(8,128)(2,1)} %band_projection.1), calls=%async_computation | async-start | bytes 1179648 | tf_op jit(solution)/shard_map/band_qkv_exchange/all_to_all | solution.py:628
  13.7 13.0 %copy-start.3 = (bf16[3,2,32,1024]{3,2,1,0:T(8,128)(2,1)S(1)}, bf16[3,2,32,1024]{3,2,1,0:T(8,128)(2,1)}, u32[]{:S(2)}) copy-start(bf16[3,2,32,1024]{3,2,1,0:T(8,128)(2,1)} %param.8) | copy-start | bytes 1179652
  26.6 10.8 %copy-start.2 = (s32[8]{0:T(128)S(1)}, s32[8]{0:T(128)}, u32[]{:S(2)}) copy-start(s32[8]{0:T(128)} %param.14) | copy-start | bytes 100
  26.6 10.8 %collective-permute-start.1 = (bf16[192,1024]{1,0:T(8,128)(2,1)S(1)}, bf16[192,1024]{1,0:T(8,128)(2,1)S(1)}, u32[]{:S(2)}, u32[]{:S(2)}) collective-permute-start(bf16[192,1024]{1,0:T(8,128)(2,1)S(1)} %bitcast.9), channel_id=1, source_target_pairs={{1,0},{2,1},{3,2},{4,3},{5,4},{6,5},{7,6},{0,7},{9,8},{10,9},{11,1... | collective-permute-start | bytes 1179656 | tf_op jit(solution)/shard_map/window_projection/ppermute | solution.py:652
  31.3 12.1 %all-to-all-start.1 = ((bf16[16,48,128]{2,1,0:T(8,128)(2,1)}), bf16[16,48,128]{2,1,0:T(8,128)(2,1)S(1)}, u32[]{:S(2)}, u32[]{:S(2)}) async-start(bf16[16,48,128]{2,1,0:T(8,128)(2,1)} %get-tuple-element.35.o_ref), calls=%async_computation.1 | async-start | bytes 393216 | tf_op jit(solution)/shard_map/band_forward/all_to_all | solution.py:628
  37.5 6.0 %copy-start.1 = (bf16[1024,1024]{1,0:T(8,128)(2,1)S(1)}, bf16[1024,1024]{1,0:T(8,128)(2,1)}, u32[]{:S(2)}) copy-start(bf16[1024,1024]{1,0:T(8,128)(2,1)} %wo_ref.1) | copy-start | bytes 6291460
  43.5 21.2 %copy-start = (bf16[16,48,128]{2,1,0:T(8,128)(2,1)S(1)}, bf16[16,48,128]{2,1,0:T(8,128)(2,1)}, u32[]{:S(2)}) copy-start(bf16[16,48,128]{2,1,0:T(8,128)(2,1)} %get-tuple-element.35.o_ref) | copy-start | bytes 589828
  47.9 8.1 %collective-permute-start.4 = (f32[8,128]{1,0:T(8,128)}, f32[8,128]{1,0:T(8,128)S(1)}, u32[]{:S(2)}, u32[]{:S(2)}) collective-permute-start(f32[8,128]{1,0:T(8,128)} %get-tuple-element.39), channel_id=1, source_target_pairs={{0,3},{1,2},{2,1},{3,0},{4,7},{5,6},{6,5},{7,4},{8,11},{9,10},{10,... | collective-permute-start | bytes 12296 | tf_op jit(solution)/shard_map/middle/ppermute | solution.py:666
  50.7 5.4 %collective-permute-start.3 = (f32[8,128]{1,0:T(8,128)}, f32[8,128]{1,0:T(8,128)S(1)}, u32[]{:S(2)}, u32[]{:S(2)}) collective-permute-start(f32[8,128]{1,0:T(8,128)} %get-tuple-element.39), channel_id=1, source_target_pairs={{0,2},{1,3},{2,0},{3,1},{4,6},{5,7},{6,4},{7,5},{8,10},{9,11},{10,... | collective-permute-start | bytes 12296 | tf_op jit(solution)/shard_map/middle/ppermute | solution.py:666
  50.9 5.1 %collective-permute-start.2 = (f32[8,128]{1,0:T(8,128)}, f32[8,128]{1,0:T(8,128)S(1)}, u32[]{:S(2)}, u32[]{:S(2)}) collective-permute-start(f32[8,128]{1,0:T(8,128)} %get-tuple-element.39), channel_id=1, source_target_pairs={{0,1},{1,0},{2,3},{3,2},{4,5},{5,4},{6,7},{7,6},{8,9},{9,8},{10,11... | collective-permute-start | bytes 12296 | tf_op jit(solution)/shard_map/middle/ppermute | solution.py:666
  51.5 13.1 %all-to-all-start.2 = ((bf16[16,48,128]{2,1,0:T(8,128)(2,1)}), bf16[16,48,128]{2,1,0:T(8,128)(2,1)S(1)}, u32[]{:S(2)}, u32[]{:S(2)}) async-start(bf16[16,48,128]{2,1,0:T(8,128)(2,1)} %get-tuple-element.38), calls=%async_computation.2 | async-start | bytes 393216 | tf_op jit(solution)/shard_map/middle/all_to_all | solution.py:628
  56.8 5.1 %collective-permute-start.5 = (f32[8,128]{1,0:T(8,128)S(1)}, f32[8,128]{1,0:T(8,128)S(1)}, u32[]{:S(2)}, u32[]{:S(2)}) collective-permute-start(f32[8,128]{1,0:T(8,128)S(1)} %add_add_fusion.mine_ref), channel_id=1, source_target_pairs={{0,4},{1,5},{2,6},{3,7},{4,0},{5,1},{6,2},{7,3},{8,12},{9,13},{10,... | collective-permute-start | bytes 12296 | tf_op jit(solution)/shard_map/band_backward/ppermute | solution.py:670
  58.9 13.6 %collective-permute-start.7 = (bf16[192,640]{1,0:T(8,128)(2,1)}, bf16[192,640]{1,0:T(8,128)(2,1)S(1)}, u32[]{:S(2)}, u32[]{:S(2)}) collective-permute-start(bf16[192,640]{1,0:T(8,128)(2,1)} %get-tuple-element.40.pay_hbm), channel_id=1, source_target_pairs={{1,0},{2,1},{3,2},{4,3},{5,4},{6,5},{7,6},{0,7},{9,8},{10,9},{11,1... | collective-permute-start | bytes 737288 | tf_op jit(solution)/shard_map/middle/ppermute | solution.py:663
  61.1 11.4 %collective-permute-start.6 = (bf16[192,640]{1,0:T(8,128)(2,1)}, bf16[192,640]{1,0:T(8,128)(2,1)S(1)}, u32[]{:S(2)}, u32[]{:S(2)}) collective-permute-start(bf16[192,640]{1,0:T(8,128)(2,1)} %get-tuple-element.40.pay_hbm), channel_id=1, source_target_pairs={{0,1},{1,2},{2,3},{3,4},{4,5},{5,6},{6,7},{7,0},{8,9},{9,10},{10,1... | collective-permute-start | bytes 737288 | tf_op jit(solution)/shard_map/middle/ppermute | solution.py:664
  67.8 18.2 %all-to-all-start.3 = ((bf16[16,160,128]{2,1,0:T(8,128)(2,1)}), bf16[16,160,128]{2,1,0:T(8,128)(2,1)S(1)}, u32[]{:S(2)}, u32[]{:S(2)}) async-start(bf16[16,160,128]{2,1,0:T(8,128)(2,1)} %band_backward.1), calls=%async_computation.3 | async-start | bytes 1310720 | tf_op jit(solution)/shard_map/band_backward/all_to_all | solution.py:628

commit v6 on v5

--- a/solution.py
+++ b/solution.py
@@ -150,7 +150,8 @@
     return jnp.concatenate([x[:, 0:16, :], x[:, 16:32, :]], axis=2)
 
 
-def band_fwd_kernel(x_ref, o_ref, stat_ref):
+def band_fwd_kernel(x_ref, o_hbm, stat_ref, o_ref, sems):
+    stores = []
     for l in range(LEVELS):
         q, k, v = unpack_qkv(x_ref[:, 48 * l : 48 * l + 48, :])
         s = dot_nt(k, q) * (SCALE * LOG2E)
@@ -162,15 +163,20 @@
         o_ref[:, 16 * l : 16 * l + 16, :] = pack_one(o)
         stat_ref[l, 0:1, :] = top
         stat_ref[l, 1:2, :] = rtot
+        rows = pl.ds(16 * l, 16)
+        stores += begin([(o_ref.at[:, rows], o_hbm.at[:, rows])], sems.at[pl.ds(l, 1)])
+    for store in stores:
+        store.wait()
 
 
 def band_fwd(x):
     return call(
         band_fwd_kernel,
-        [out_block((N_LON, 48, 128), BF), out_vmem((LEVELS, 2, 512), F32)],
+        [out_hbm((N_LON, 48, 128), BF), out_vmem((LEVELS, 2, 512), F32)],
         12 * 512 * 512 * 64,
         1024 * 1024,
         [in_vmem(x)],
+        [pltpu.VMEM((N_LON, 48, 128), BF), pltpu.SemaphoreType.DMA((3,))],
     )
 
 
@@ -473,8 +479,8 @@
 
 def mid_kernel(
     table_ref, tok_hbm, tgt_hbm, win_hbm, stat_hbm, wo_ref, o_ref,
-    mixed_hbm, dm_hbm, send_ref, pay_ref, sum_ref,
-    tok_ref, tgt_ref, win_ref, stat_ref, mixed_ref, dm_ref, att_s, sems,
+    mixed_hbm, dm_hbm, send_hbm, pay_ref, sum_ref,
+    tok_ref, tgt_ref, win_ref, stat_ref, mixed_ref, dm_ref, att_s, send_ref, sems, send_sems,
 ):
     copies = begin(
         [(win_hbm, win_ref), (tok_hbm, tok_ref), (tgt_hbm, tgt_ref), (stat_hbm, stat_ref)], sems
@@ -509,6 +515,15 @@
         d_att = d_att + dot_nt(dm, wo_ref[:, lanes])
     copies = begin([(mixed_ref, mixed_hbm), (dm_ref, dm_hbm)], sems)
     d_att = d_att.astype(BF)
+    for h in range(HALF):
+        dh = d_att[:, 64 * h : 64 * h + 64]
+        for l in range(LEVELS):
+            for r in range(2):
+                base = 64 * l + 32 * r
+                send_ref[2 * h + r, 16 * l : 16 * l + 16, :] = jnp.concatenate(
+                    [dh[base : base + 16], dh[base + 16 : base + 32]], axis=1
+                )
+    stores = begin([(send_ref, send_hbm)], send_sems)
     dwin = to_halves(d_att[:, BAND:])
     pay_ref[:, 0:BAND] = dwin
     terms = dwin.astype(F32) * win_ref[...].astype(F32)
@@ -523,16 +538,8 @@
     low = stat - high - middle
     packed = high + pltpu.roll(middle, 32, 1) + pltpu.roll(low, 64, 1)
     pay_ref[:, BAND:] = packed.astype(BF)
-    for h in range(HALF):
-        dh = d_att[:, 64 * h : 64 * h + 64]
-        for l in range(LEVELS):
-            for r in range(2):
-                base = 64 * l + 32 * r
-                send_ref[2 * h + r, 16 * l : 16 * l + 16, :] = jnp.concatenate(
-                    [dh[base : base + 16], dh[base + 16 : base + 32]], axis=1
-                )
     sum_ref[...] = jnp.broadcast_to(jnp.sum(total), (8, 128))
-    for copy in copies:
+    for copy in copies + stores:
         copy.wait()
 
 
@@ -542,7 +549,7 @@
         [
             out_hbm((TOK, WIDTH), BF),
             out_hbm((TOK, WIDTH), BF),
-            out_block((N_LON, 48, 128), BF),
+            out_hbm((N_LON, 48, 128), BF),
             out_block((TOK, BAND + 128), BF),
             out_block((8, 128), F32),
         ],
@@ -554,7 +561,8 @@
         [pltpu.VMEM((TOK, WIDTH), BF)] * 2
         + [pltpu.VMEM((TOK, BAND), BF), pltpu.VMEM((TOK, 128), F32)]
         + [pltpu.VMEM((TOK, WIDTH), BF)] * 3
-        + [pltpu.SemaphoreType.DMA((4,))],
+        + [pltpu.VMEM((N_LON, 48, 128), BF)]
+        + [pltpu.SemaphoreType.DMA((4,)), pltpu.SemaphoreType.DMA((1,))],
     )
 
 

time: 91.3 us -> 91.3 us (level)
  no operation moved by 1% of the time
where the time goes in v6:
time: 91.3 us; the launch traced here: 90.2 us
  Pallas kernels  38.1 us (42%)
  starting transfers between devices  31.8 us (35%)
  waiting for transfers between devices  18.5 us (20%)
  between operations  0.94 us (1%)
    pallas_call x8, Pallas kernels, call(): pl.pallas_call(kernel, grid=(1,), in_specs=[spec for spec, _ in ins], out...  38.1 us
    all_to_all x4, starting transfers between devices, swap(): return lax.all_to_all(x, 'lon', 0, 0, tiled=True)  20 us
    all_to_all x4, waiting for transfers between devices, swap(): return lax.all_to_all(x, 'lon', 0, 0, tiled=True)  14 us
    ppermute x3, starting transfers between devices, per_device(): lax.ppermute(part, 'lat', [(i, i ^ step) for i in range(N_LAT)])  3.57 us
    ppermute x1, waiting for transfers between devices, per_device(): nxt = lax.ppermute(tok_later, 'lat', DOWN)  2.61 us
    ppermute x1, starting transfers between devices, per_device(): pay_next = lax.ppermute(pay, 'lat', DOWN)  2.2 us
    ppermute x1, starting transfers between devices, per_device(): far = lax.ppermute(four, 'lat', [(i, i ^ 4) for i in range(N_LAT)])  2.12 us
    ppermute x1, starting transfers between devices, per_device(): prev = lax.ppermute(tok, 'lat', UP)  2.07 us
  transfers between devices with their start and end apart: 12, of which 8 were waited for; matrix products, arithmetic and copies ran while one was open for 1% of the time, Pallas kernels for 33%

profile of v6, /device:TPU:0, one launch (start us, length us, event | category | flops | bytes accessed | tf_op | source)
XLA Modules:
  0.0 90.2 jit_solution(11922381868326795880)
XLA Ops:
  0.6 2.1 %collective-permute-start = (bf16[192,1024]{1,0:T(8,128)(2,1)}, bf16[192,1024]{1,0:T(8,128)(2,1)S(1)}, u32[]{:S(2)}, u32[]{:S(2)}) collective-permute-start(bf16[192,1024]{1,0:T(8,128)(2,1)} %bitcast.5), channel_id=1, source_target_pairs={{0,1},{1,2},{2,3},{3,4},{4,5},{5,6},{6,7},{7,0},{8,9},{9,10},{10,1... | collective-permute-start | bytes 1179656 | tf_op jit(solution)/shard_map/halo_tokens/ppermute | solution.py:654
  2.7 3.4 %band_projection.1 = bf16[16,144,128]{2,1,0:T(8,128)(2,1)} custom-call(bf16[192,1024]{1,0:T(8,128)(2,1)} %bitcast.6, bf16[1024,1024]{1,0:T(8,128)(2,1)} %wq_hbm.9, bf16[1024,1024]{1,0:T(8,128)(2,1)} %wk_hbm.9, bf16[1024,1024]{1,0:T(8,128)(2,1)} %wv_hbm.9), custom_call_target="tpu_custom_call" | custom-call | flops 30198988800 | bytes 4194304 | tf_op jit(solution)/shard_map/band_projection/pallas_call | solution.py:29
  6.1 7.4 %all-to-all-start = ((bf16[16,144,128]{2,1,0:T(8,128)(2,1)}), bf16[16,144,128]{2,1,0:T(8,128)(2,1)S(1)}, u32[]{:S(2)}, u32[]{:S(2)}) async-start(bf16[16,144,128]{2,1,0:T(8,128)(2,1)} %band_projection.1), calls=%async_computation | async-start | bytes 1179648 | tf_op jit(solution)/shard_map/band_qkv_exchange/all_to_all | solution.py:636
  13.6 0.1 broadcast_in_dim.16
  13.7 0.8 collective-permute-done.prev_ref
  14.5 3.9 %window_projection.1 = (bf16[384,512]{1,0:T(8,128)(2,1)}, bf16[384,512]{1,0:T(8,128)(2,1)}, bf16[384,512]{1,0:T(8,128)(2,1)}) custom-call(bf16[192,1024]{1,0:T(8,128)(2,1)S(1)} %collective-permute-done.prev_ref, bf16[192,1024]{1,0:T(8,128)(2,1)} %bitcast.7, bf16[1024,1024]{1,0:T(8,128)(2,1)} %wq_hbm.9, bf16[1024,1024]{1,0:T(8,128)(2,1)} %wk_hbm.9, ...), custom_call_target="tpu_custom_call" | custom-call | flops 60397977600 | bytes 4194304 | tf_op jit(solution)/shard_map/window_projection/pallas_call | solution.py:29
  18.4 8.3 %all-to-all-done.x_ref = bf16[16,144,128]{2,1,0:T(8,128)(2,1)S(1)} async-done(((bf16[16,144,128]{2,1,0:T(8,128)(2,1)}), bf16[16,144,128]{2,1,0:T(8,128)(2,1)S(1)}, u32[]{:S(2)}, u32[]{:S(2)}) %all-to-all-start) | async-done | bytes 589856 | tf_op jit(solution)/shard_map/band_qkv_exchange/all_to_all | solution.py:636
  26.6 1.9 %collective-permute-start.1 = (bf16[192,1024]{1,0:T(8,128)(2,1)S(1)}, bf16[192,1024]{1,0:T(8,128)(2,1)S(1)}, u32[]{:S(2)}, u32[]{:S(2)}) collective-permute-start(bf16[192,1024]{1,0:T(8,128)(2,1)S(1)} %bitcast.9), channel_id=1, source_target_pairs={{1,0},{2,1},{3,2},{4,3},{5,4},{6,5},{7,6},{0,7},{9,8},{10,9},{11,1... | collective-permute-start | bytes 1179656 | tf_op jit(solution)/shard_map/window_projection/ppermute | solution.py:660
  28.5 2.7 %band_forward.1 = (bf16[16,48,128]{2,1,0:T(8,128)(2,1)}, f32[3,2,512]{2,1,0:T(2,128)S(1)}) custom-call(bf16[16,144,128]{2,1,0:T(8,128)(2,1)S(1)} %all-to-all-done.x_ref), custom_call_target="tpu_custom_call" | custom-call | flops 10066329600 | bytes 1048576 | tf_op jit(solution)/shard_map/band_forward/pallas_call | solution.py:29
  31.3 3.5 %all-to-all-start.1 = ((bf16[16,48,128]{2,1,0:T(8,128)(2,1)}), bf16[16,48,128]{2,1,0:T(8,128)(2,1)S(1)}, u32[]{:S(2)}, u32[]{:S(2)}) async-start(bf16[16,48,128]{2,1,0:T(8,128)(2,1)} %get-tuple-element.35.o_ref), calls=%async_computation.1 | async-start | bytes 393216 | tf_op jit(solution)/shard_map/band_forward/all_to_all | solution.py:636
  34.8 2.6 %collective-permute-done.1.next_ref = bf16[192,1024]{1,0:T(8,128)(2,1)S(1)} collective-permute-done((bf16[192,1024]{1,0:T(8,128)(2,1)S(1)}, bf16[192,1024]{1,0:T(8,128)(2,1)S(1)}, u32[]{:S(2)}, u32[]{:S(2)}) %collective-permute-start.1) | collective-permute-done | bytes 393248 | tf_op jit(solution)/shard_map/window_projection/ppermute | solution.py:660
  37.4 0.1 broadcast_in_dim.19.reach_ref
  37.5 5.8 %window_forward.1 = (bf16[192,512]{1,0:T(8,128)(2,1)}, f32[192,128]{1,0:T(8,128)}, bf16[192,512]{1,0:T(8,128)(2,1)}, bf16[192,512]{1,0:T(8,128)(2,1)}, bf16[192,512]{1,0:T(8,128)(2,1)}) custom-call(s32[8,128]{1,0:T(8,128)S(1)} %broadcast_in_dim.18.pos_ref, s32[8,128]{1,0:T(8,128)S(1)} %broadcast_in_dim.19.reach_ref, ...), custom_call_target="tpu_custom_call" | custom-call | flops 37748736000 | bytes 6291456 | tf_op jit(solution)/shard_map/window_forward/pallas_call | solution.py:29
  43.3 0.1 all-to-all-done.1.o_ref
  43.4 0.1 broadcast_in_dim.17.table_ref
  43.5 4.5 %middle.1 = (bf16[192,1024]{1,0:T(8,128)(2,1)}, bf16[192,1024]{1,0:T(8,128)(2,1)}, bf16[16,48,128]{2,1,0:T(8,128)(2,1)}, bf16[192,640]{1,0:T(8,128)(2,1)}, f32[8,128]{1,0:T(8,128)}) custom-call(s32[8,128]{1,0:T(8,128)S(1)} %broadcast_in_dim.17.table_ref, bf16[192,1024]{1,0:T(8,128)(2,1)} %bitcast.8, bf16[192,1024]{1,0:T(8,128)(2,1)} %bitcast.10, ...), custom_call_target="tpu_custom_call" | custom-call | flops 40265318400 | bytes 4194304 | tf_op jit(solution)/shard_map/middle/pallas_call | solution.py:29
  47.9 2.7 %collective-permute-start.4 = (f32[8,128]{1,0:T(8,128)}, f32[8,128]{1,0:T(8,128)S(1)}, u32[]{:S(2)}, u32[]{:S(2)}) collective-permute-start(f32[8,128]{1,0:T(8,128)} %get-tuple-element.39), channel_id=1, source_target_pairs={{0,3},{1,2},{2,1},{3,0},{4,7},{5,6},{6,5},{7,4},{8,11},{9,10},{10,... | collective-permute-start | bytes 12296 | tf_op jit(solution)/shard_map/middle/ppermute | solution.py:674
  50.7 0.3 collective-permute-start.3
  50.9 0.6 collective-permute-start.2
  51.5 4.5 %all-to-all-start.2 = ((bf16[16,48,128]{2,1,0:T(8,128)(2,1)}), bf16[16,48,128]{2,1,0:T(8,128)(2,1)S(1)}, u32[]{:S(2)}, u32[]{:S(2)}) async-start(bf16[16,48,128]{2,1,0:T(8,128)(2,1)} %get-tuple-element.38), calls=%async_computation.2 | async-start | bytes 393216 | tf_op jit(solution)/shard_map/middle/all_to_all | solution.py:636
  56.1 0.7 add_add_fusion.mine_ref
  56.7 2.1 %collective-permute-start.5 = (f32[8,128]{1,0:T(8,128)S(1)}, f32[8,128]{1,0:T(8,128)S(1)}, u32[]{:S(2)}, u32[]{:S(2)}) collective-permute-start(f32[8,128]{1,0:T(8,128)S(1)} %add_add_fusion.mine_ref), channel_id=1, source_target_pairs={{0,4},{1,5},{2,6},{3,7},{4,0},{5,1},{6,2},{7,3},{8,12},{9,13},{10,... | collective-permute-start | bytes 12296 | tf_op jit(solution)/shard_map/band_backward/ppermute | solution.py:678
  58.9 2.2 %collective-permute-start.7 = (bf16[192,640]{1,0:T(8,128)(2,1)}, bf16[192,640]{1,0:T(8,128)(2,1)S(1)}, u32[]{:S(2)}, u32[]{:S(2)}) collective-permute-start(bf16[192,640]{1,0:T(8,128)(2,1)} %get-tuple-element.40.pay_hbm), channel_id=1, source_target_pairs={{1,0},{2,1},{3,2},{4,3},{5,4},{6,5},{7,6},{0,7},{9,8},{10,9},{11,1... | collective-permute-start | bytes 737288 | tf_op jit(solution)/shard_map/middle/ppermute | solution.py:671
  61.1 0.0 collective-permute-start.6
  61.1 0.8 collective-permute-done.5.other_ref
  61.9 2.8 %all-to-all-done.2.do_ref = bf16[16,48,128]{2,1,0:T(8,128)(2,1)S(1)} async-done(((bf16[16,48,128]{2,1,0:T(8,128)(2,1)}), bf16[16,48,128]{2,1,0:T(8,128)(2,1)S(1)}, u32[]{:S(2)}, u32[]{:S(2)}) %all-to-all-start.2) | async-done | bytes 196640 | tf_op jit(solution)/shard_map/middle/all_to_all | solution.py:636
  64.6 3.1 %band_backward.1 = bf16[16,160,128]{2,1,0:T(8,128)(2,1)} custom-call(bf16[16,144,128]{2,1,0:T(8,128)(2,1)S(1)} %all-to-all-done.x_ref, bf16[16,48,128]{2,1,0:T(8,128)(2,1)S(1)} %copy-done, f32[3,2,512]{2,1,0:T(2,128)S(1)} %get-tuple-element.37.stat_ref, bf16[16,48,128]{2,1,0:T(8,128)(2,1)S(1)} %all-to-all-done.2.do_ref, f32[8,128]{1,0:T(8,128)S(1)} %add_add_fusion.mine_ref, ...), custom_call_target="tpu_custom_call" | custom-call | flops 25165824000 | bytes 2097152 | tf_op jit(solution)/shard_map/band_backward/pallas_call | solution.py:29
  67.8 4.5 %all-to-all-start.3 = ((bf16[16,160,128]{2,1,0:T(8,128)(2,1)}), bf16[16,160,128]{2,1,0:T(8,128)(2,1)S(1)}, u32[]{:S(2)}, u32[]{:S(2)}) async-start(bf16[16,160,128]{2,1,0:T(8,128)(2,1)} %band_backward.1), calls=%async_computation.3 | async-start | bytes 1310720 | tf_op jit(solution)/shard_map/band_backward/all_to_all | solution.py:636
  72.2 0.2 collective-permute-done.7.next_ref
  72.5 10.6 %window_gradient.1.base_hbm = f32[192,1024]{1,0:T(8,128)} custom-call(s32[8,128]{1,0:T(8,128)S(1)} %broadcast_in_dim.18.pos_ref, s32[8,128]{1,0:T(8,128)S(1)} %broadcast_in_dim.19.reach_ref, bf16[192,640]{1,0:T(8,128)(2,1)S(1)} %collective-permute-done.6.prev_ref, bf16[192,640]{1,0:T(8,128)(2,1)S(1)} %collective-permute-done.7.next_ref, ...), custom_call_target="tpu_custom_call" | custom-call | flops 53791948800 | bytes 8388608 | tf_op jit(solution)/shard_map/window_gradient/pallas_call | solution.py:29
  83.1 2.9 %all-to-all-done.3.x_ref = bf16[16,160,128]{2,1,0:T(8,128)(2,1)S(1)} async-done(((bf16[16,160,128]{2,1,0:T(8,128)(2,1)}), bf16[16,160,128]{2,1,0:T(8,128)(2,1)S(1)}, u32[]{:S(2)}, u32[]{:S(2)}) %all-to-all-start.3) | async-done | bytes 655392 | tf_op jit(solution)/shard_map/band_backward/all_to_all | solution.py:636
  86.0 4.1 %token_gradient.1 = (f32[192,1024]{1,0:T(8,128)}, f32[1,1]{1,0:T(1,128)}) custom-call(bf16[16,160,128]{2,1,0:T(8,128)(2,1)S(1)} %all-to-all-done.3.x_ref, f32[192,1024]{1,0:T(8,128)} %window_gradient.1.base_hbm, bf16[1024,1024]{1,0:T(8,128)(2,1)} %wq_hbm.9, bf16[1024,1024]{1,0:T(8,128)(2,1)} %wk_hbm.9, bf16[1024,1024]{1,0:T(8,128)(2,1)} %wv_hbm.9), custom_call_target="tpu_custom_call" | custom-call | flops 30198988800 | bytes 5242880 | tf_op jit(solution)/shard_map/token_gradient/pallas_call | solution.py:29
  (16 shorter events, 0.0 us)
Async XLA Ops:
  0.6 12.9 %copy-start.4 = (s32[4]{0:T(128)S(1)}, s32[4]{0:T(128)}, u32[]{:S(2)}) copy-start(s32[4]{0:T(128)} %param.15) | copy-start | bytes 52
  0.6 13.8 %collective-permute-start = (bf16[192,1024]{1,0:T(8,128)(2,1)}, bf16[192,1024]{1,0:T(8,128)(2,1)S(1)}, u32[]{:S(2)}, u32[]{:S(2)}) collective-permute-start(bf16[192,1024]{1,0:T(8,128)(2,1)} %bitcast.5), channel_id=1, source_target_pairs={{0,1},{1,2},{2,3},{3,4},{4,5},{5,6},{6,7},{7,0},{8,9},{9,10},{10,1... | collective-permute-start | bytes 1179656 | tf_op jit(solution)/shard_map/halo_tokens/ppermute | solution.py:654
  6.1 20.5 %all-to-all-start = ((bf16[16,144,128]{2,1,0:T(8,128)(2,1)}), bf16[16,144,128]{2,1,0:T(8,128)(2,1)S(1)}, u32[]{:S(2)}, u32[]{:S(2)}) async-start(bf16[16,144,128]{2,1,0:T(8,128)(2,1)} %band_projection.1), calls=%async_computation | async-start | bytes 1179648 | tf_op jit(solution)/shard_map/band_qkv_exchange/all_to_all | solution.py:636
  13.7 13.0 %copy-start.3 = (bf16[3,2,32,1024]{3,2,1,0:T(8,128)(2,1)S(1)}, bf16[3,2,32,1024]{3,2,1,0:T(8,128)(2,1)}, u32[]{:S(2)}) copy-start(bf16[3,2,32,1024]{3,2,1,0:T(8,128)(2,1)} %param.8) | copy-start | bytes 1179652
  26.6 10.8 %copy-start.2 = (s32[8]{0:T(128)S(1)}, s32[8]{0:T(128)}, u32[]{:S(2)}) copy-start(s32[8]{0:T(128)} %param.14) | copy-start | bytes 100
  26.6 10.8 %collective-permute-start.1 = (bf16[192,1024]{1,0:T(8,128)(2,1)S(1)}, bf16[192,1024]{1,0:T(8,128)(2,1)S(1)}, u32[]{:S(2)}, u32[]{:S(2)}) collective-permute-start(bf16[192,1024]{1,0:T(8,128)(2,1)S(1)} %bitcast.9), channel_id=1, source_target_pairs={{1,0},{2,1},{3,2},{4,3},{5,4},{6,5},{7,6},{0,7},{9,8},{10,9},{11,1... | collective-permute-start | bytes 1179656 | tf_op jit(solution)/shard_map/window_projection/ppermute | solution.py:660
  31.3 12.1 %all-to-all-start.1 = ((bf16[16,48,128]{2,1,0:T(8,128)(2,1)}), bf16[16,48,128]{2,1,0:T(8,128)(2,1)S(1)}, u32[]{:S(2)}, u32[]{:S(2)}) async-start(bf16[16,48,128]{2,1,0:T(8,128)(2,1)} %get-tuple-element.35.o_ref), calls=%async_computation.1 | async-start | bytes 393216 | tf_op jit(solution)/shard_map/band_forward/all_to_all | solution.py:636
  37.5 6.0 %copy-start.1 = (bf16[1024,1024]{1,0:T(8,128)(2,1)S(1)}, bf16[1024,1024]{1,0:T(8,128)(2,1)}, u32[]{:S(2)}) copy-start(bf16[1024,1024]{1,0:T(8,128)(2,1)} %wo_ref.1) | copy-start | bytes 6291460
  43.5 21.2 %copy-start = (bf16[16,48,128]{2,1,0:T(8,128)(2,1)S(1)}, bf16[16,48,128]{2,1,0:T(8,128)(2,1)}, u32[]{:S(2)}) copy-start(bf16[16,48,128]{2,1,0:T(8,128)(2,1)} %get-tuple-element.35.o_ref) | copy-start | bytes 589828
  47.9 8.1 %collective-permute-start.4 = (f32[8,128]{1,0:T(8,128)}, f32[8,128]{1,0:T(8,128)S(1)}, u32[]{:S(2)}, u32[]{:S(2)}) collective-permute-start(f32[8,128]{1,0:T(8,128)} %get-tuple-element.39), channel_id=1, source_target_pairs={{0,3},{1,2},{2,1},{3,0},{4,7},{5,6},{6,5},{7,4},{8,11},{9,10},{10,... | collective-permute-start | bytes 12296 | tf_op jit(solution)/shard_map/middle/ppermute | solution.py:674
  50.7 5.4 %collective-permute-start.3 = (f32[8,128]{1,0:T(8,128)}, f32[8,128]{1,0:T(8,128)S(1)}, u32[]{:S(2)}, u32[]{:S(2)}) collective-permute-start(f32[8,128]{1,0:T(8,128)} %get-tuple-element.39), channel_id=1, source_target_pairs={{0,2},{1,3},{2,0},{3,1},{4,6},{5,7},{6,4},{7,5},{8,10},{9,11},{10,... | collective-permute-start | bytes 12296 | tf_op jit(solution)/shard_map/middle/ppermute | solution.py:674
  50.9 5.1 %collective-permute-start.2 = (f32[8,128]{1,0:T(8,128)}, f32[8,128]{1,0:T(8,128)S(1)}, u32[]{:S(2)}, u32[]{:S(2)}) collective-permute-start(f32[8,128]{1,0:T(8,128)} %get-tuple-element.39), channel_id=1, source_target_pairs={{0,1},{1,0},{2,3},{3,2},{4,5},{5,4},{6,7},{7,6},{8,9},{9,8},{10,11... | collective-permute-start | bytes 12296 | tf_op jit(solution)/shard_map/middle/ppermute | solution.py:674
  51.5 13.1 %all-to-all-start.2 = ((bf16[16,48,128]{2,1,0:T(8,128)(2,1)}), bf16[16,48,128]{2,1,0:T(8,128)(2,1)S(1)}, u32[]{:S(2)}, u32[]{:S(2)}) async-start(bf16[16,48,128]{2,1,0:T(8,128)(2,1)} %get-tuple-element.38), calls=%async_computation.2 | async-start | bytes 393216 | tf_op jit(solution)/shard_map/middle/all_to_all | solution.py:636
  56.7 5.1 %collective-permute-start.5 = (f32[8,128]{1,0:T(8,128)S(1)}, f32[8,128]{1,0:T(8,128)S(1)}, u32[]{:S(2)}, u32[]{:S(2)}) collective-permute-start(f32[8,128]{1,0:T(8,128)S(1)} %add_add_fusion.mine_ref), channel_id=1, source_target_pairs={{0,4},{1,5},{2,6},{3,7},{4,0},{5,1},{6,2},{7,3},{8,12},{9,13},{10,... | collective-permute-start | bytes 12296 | tf_op jit(solution)/shard_map/band_backward/ppermute | solution.py:678
  58.9 13.6 %collective-permute-start.7 = (bf16[192,640]{1,0:T(8,128)(2,1)}, bf16[192,640]{1,0:T(8,128)(2,1)S(1)}, u32[]{:S(2)}, u32[]{:S(2)}) collective-permute-start(bf16[192,640]{1,0:T(8,128)(2,1)} %get-tuple-element.40.pay_hbm), channel_id=1, source_target_pairs={{1,0},{2,1},{3,2},{4,3},{5,4},{6,5},{7,6},{0,7},{9,8},{10,9},{11,1... | collective-permute-start | bytes 737288 | tf_op jit(solution)/shard_map/middle/ppermute | solution.py:671
  61.1 11.4 %collective-permute-start.6 = (bf16[192,640]{1,0:T(8,128)(2,1)}, bf16[192,640]{1,0:T(8,128)(2,1)S(1)}, u32[]{:S(2)}, u32[]{:S(2)}) collective-permute-start(bf16[192,640]{1,0:T(8,128)(2,1)} %get-tuple-element.40.pay_hbm), channel_id=1, source_target_pairs={{0,1},{1,2},{2,3},{3,4},{4,5},{5,6},{6,7},{7,0},{8,9},{9,10},{10,1... | collective-permute-start | bytes 737288 | tf_op jit(solution)/shard_map/middle/ppermute | solution.py:672
  67.8 18.2 %all-to-all-start.3 = ((bf16[16,160,128]{2,1,0:T(8,128)(2,1)}), bf16[16,160,128]{2,1,0:T(8,128)(2,1)S(1)}, u32[]{:S(2)}, u32[]{:S(2)}) async-start(bf16[16,160,128]{2,1,0:T(8,128)(2,1)} %band_backward.1), calls=%async_computation.3 | async-start | bytes 1310720 | tf_op jit(solution)/shard_map/band_backward/all_to_all | solution.py:636
